TPU v7x, 32 devices: a whole 2x2x4 slice. The times are simulated.
32 devices in a mesh: dp: 4 (over z), ctx: 8 (over y, x, core).
Axes of the slice: x: 2, y: 2, z: 4, core: 2. Of those that a mesh axis runs over, the one named last changes fastest.
Arguments:
- query_rows: bfloat16 [4, 1024, 2048], P('dp', 'ctx'), may hold values from -72 to 72
- key_rows: bfloat16 [4, 1024, 512], P('dp', 'ctx'), may hold values from -4 to 4
- value_rows: bfloat16 [4, 1024, 512], P('dp', 'ctx'), may hold values from -6 to 6
- grad_rows: bfloat16 [4, 1024, 2048], P('dp', 'ctx'), may hold values from -6 to 6
- bucket_rank: int32 [4, 1024], P('dp', 'ctx'), may hold values from 0 to 255, as said below
- sample_rows: int32 [4, 8], P('dp', 'ctx'), may hold values from 0 to 127, as said below
- sample_count: int32 [4, 8], P('dp', 'ctx'), may hold values from 1 to 3
- sink_logit: float32 [16], replicated, may hold values from 3 to 6
Outputs:
- query_grad: bfloat16 [4, 1024, 2048], P('dp', 'ctx')
- key_grad: bfloat16 [4, 1024, 512], P('dp', 'ctx')
- value_grad: bfloat16 [4, 1024, 512], P('dp', 'ctx')
- sink_grad: float32 [16], replicated
Inputs may be any that keep to these rules, and one draw needn't show every extreme that they name: `bucket_rank`: for every sequence and every m, the values over the 256 tokens held by ctx indices 2m and 2m+1 are a permutation of 0 to 255. `sample_rows`: slot c names a row of the 128 tokens held by ctx index c, counted from that block's first token; the slots of one block name distinct rows.
All inputs are finite; a program needn't handle non-finite values.
Results may differ from a plain program's by a relative error of at most 0.0075.
Values may be sent and summed in bfloat16 or wider, within the bound.
No kernel may reach another device: no remote copies, remote signals or barrier semaphores. Data moves between devices by JAX's collectives and lax.ppermute only.
A program may use at most 64 MiB of HBM per device.

v0:
```python
import jax
import jax.numpy as jnp
from jax import lax
from jax.sharding import PartitionSpec as P

HEADS = 16
KV_HEADS = 4
HDIM = 128
BUCKET = 128
SAMP_DEV = 1


def swapped(array, axis, apart):
    return lax.ppermute(array, axis, [(i, i ^ 1 << apart) for i in range(lax.axis_size(axis))])


def on_device(
    query_rows, key_rows, value_rows, grad_rows, bucket_rank, sample_rows, sample_count, sink_logit
):
    length = query_rows.shape[1]
    per_group = HEADS // KV_HEADS
    kv_width = KV_HEADS * HDIM
    score_scale = HDIM ** (-0.5)
    query_heads = query_rows[0].reshape(length, KV_HEADS, per_group, HDIM)
    grad_heads = grad_rows[0].reshape(length, KV_HEADS, per_group, HDIM)
    own_bucket = bucket_rank[0] // BUCKET
    own_mark = own_bucket.astype(jnp.bfloat16)
    far_keys, far_values, far_mark = swapped((key_rows[0], value_rows[0], own_mark), "ctx", 0)
    pair_keys = jnp.concatenate([key_rows[0], far_keys], 0).reshape(2 * length, KV_HEADS, HDIM)
    pair_values = jnp.concatenate([value_rows[0], far_values], 0).reshape(
        2 * length, KV_HEADS, HDIM
    )
    query_bucket = own_bucket.astype(jnp.float32)
    pair_bucket = jnp.concatenate([query_bucket, far_mark.astype(jnp.float32)], 0)
    picked = sample_rows[0]
    picked_keys = jnp.take(key_rows[0], picked, axis=0)
    picked_values = jnp.take(value_rows[0], picked, axis=0)
    picked_mark = jnp.take(own_mark, picked, axis=0)
    picked_count = sample_count[0].astype(jnp.bfloat16)
    panel_keys, panel_values, panel_mark, panel_count = (
        lax.all_gather(picked_keys, "ctx", axis=0, tiled=True),
        lax.all_gather(picked_values, "ctx", axis=0, tiled=True),
        lax.all_gather(picked_mark, "ctx", axis=0, tiled=True),
        lax.all_gather(picked_count, "ctx", axis=0, tiled=True),
    )
    samples = panel_keys.shape[0]
    sample_keys = panel_keys.reshape(samples, KV_HEADS, HDIM)
    sample_values = panel_values.reshape(samples, KV_HEADS, HDIM)
    owner_pair = jnp.arange(samples, dtype=jnp.int32) // SAMP_DEV // 2
    same_pair = owner_pair == lax.axis_index("ctx") // 2
    excluded = same_pair[None, :] & (
        query_bucket[:, None] == panel_mark.astype(jnp.float32)[None, :]
    )
    log_weight = jnp.log(panel_count.astype(jnp.float32))
    inside = query_bucket[:, None] == pair_bucket[None, :]
    bucket_score = (
        jnp.einsum("tkgd,jkd->tkgj", query_heads, pair_keys, preferred_element_type=jnp.float32)
        * score_scale
    )
    bucket_score = jnp.where(inside[:, None, None, :], bucket_score, -jnp.inf)
    sample_score = (
        jnp.einsum("tkgd,ckd->tkgc", query_heads, sample_keys, preferred_element_type=jnp.float32)
        * score_scale
        + log_weight
    )
    sample_score = jnp.where(excluded[:, None, None, :], -jnp.inf, sample_score)
    sink_row = sink_logit.reshape(KV_HEADS, per_group)
    row_max = jnp.maximum(
        jnp.maximum(jnp.max(bucket_score, -1), jnp.max(sample_score, -1)), sink_row
    )
    denominator = (
        jnp.exp(sink_row - row_max)
        + jnp.sum(jnp.exp(bucket_score - row_max[..., None]), -1)
        + jnp.sum(jnp.exp(sample_score - row_max[..., None]), -1)
    )
    log_total = row_max + jnp.log(denominator)
    bucket_prob = jnp.exp(bucket_score - log_total[..., None])
    sample_prob = jnp.exp(sample_score - log_total[..., None])
    sink_prob = jnp.exp(sink_row - log_total)
    bucket_half = bucket_prob.astype(jnp.bfloat16)
    sample_half = sample_prob.astype(jnp.bfloat16)
    attended = (
        jnp.einsum("tkgj,jkd->tkgd", bucket_half, pair_values, preferred_element_type=jnp.float32)
        + jnp.einsum(
            "tkgc,ckd->tkgd", sample_half, sample_values, preferred_element_type=jnp.float32
        )
    ).astype(jnp.bfloat16)
    delta = jnp.einsum("tkgd,tkgd->tkg", grad_heads, attended, preferred_element_type=jnp.float32)
    bucket_up = jnp.einsum(
        "tkgd,jkd->tkgj", grad_heads, pair_values, preferred_element_type=jnp.float32
    )
    sample_up = jnp.einsum(
        "tkgd,ckd->tkgc", grad_heads, sample_values, preferred_element_type=jnp.float32
    )
    bucket_ds = (bucket_prob * (bucket_up - delta[..., None])).astype(jnp.bfloat16)
    sample_ds = (sample_prob * (sample_up - delta[..., None])).astype(jnp.bfloat16)
    query_grad = score_scale * (
        jnp.einsum("tkgj,jkd->tkgd", bucket_ds, pair_keys, preferred_element_type=jnp.float32)
        + jnp.einsum("tkgc,ckd->tkgd", sample_ds, sample_keys, preferred_element_type=jnp.float32)
    )
    query_grad = query_grad.reshape(1, length, HEADS * HDIM).astype(jnp.bfloat16)
    key_pair_grad = score_scale * jnp.einsum(
        "tkgj,tkgd->jkd", bucket_ds, query_heads, preferred_element_type=jnp.float32
    )
    value_pair_grad = jnp.einsum(
        "tkgj,tkgd->jkd", bucket_half, grad_heads, preferred_element_type=jnp.float32
    )
    key_from_far, value_from_far = (
        swapped(key_pair_grad[length:].astype(jnp.bfloat16), "ctx", 0).astype(jnp.float32),
        swapped(value_pair_grad[length:].astype(jnp.bfloat16), "ctx", 0).astype(jnp.float32),
    )
    key_term = score_scale * jnp.einsum(
        "tkgc,tkgd->ckd", sample_ds, query_heads, preferred_element_type=jnp.float32
    )
    value_term = jnp.einsum(
        "tkgc,tkgd->ckd", sample_half, grad_heads, preferred_element_type=jnp.float32
    )
    own_slots = lax.psum_scatter(
        jnp.concatenate(
            [
                key_term.reshape(lax.axis_size("ctx") * SAMP_DEV, kv_width),
                value_term.reshape(lax.axis_size("ctx") * SAMP_DEV, kv_width),
            ],
            1,
        ),
        "ctx",
        scatter_dimension=0,
        tiled=True,
    )
    one_hot = (picked[:, None] == jnp.arange(length, dtype=jnp.int32)[None, :]).astype(jnp.float32)
    slot_rows = jnp.dot(
        one_hot.T, own_slots, preferred_element_type=jnp.float32, precision=lax.Precision.HIGHEST
    )
    key_grad = (
        key_pair_grad[:length].reshape(length, kv_width)
        + key_from_far.reshape(length, kv_width)
        + slot_rows[:, :kv_width]
    )
    value_grad = (
        value_pair_grad[:length].reshape(length, kv_width)
        + value_from_far.reshape(length, kv_width)
        + slot_rows[:, kv_width:]
    )
    sink_local = -jnp.sum(sink_prob * delta, 0).reshape(HEADS)
    sink_grad = lax.psum(sink_local, ("dp", "ctx"))
    return (
        query_grad,
        key_grad.reshape(1, length, kv_width).astype(jnp.bfloat16),
        value_grad.reshape(1, length, kv_width).astype(jnp.bfloat16),
        sink_grad,
    )


def solution(mesh):
    return jax.shard_map(
        on_device,
        mesh=mesh,
        in_specs=(
            P("dp", "ctx", None),
            P("dp", "ctx", None),
            P("dp", "ctx", None),
            P("dp", "ctx", None),
            P("dp", "ctx"),
            P("dp", "ctx"),
            P("dp", "ctx"),
            P(),
        ),
        out_specs=(P("dp", "ctx", None), P("dp", "ctx", None), P("dp", "ctx", None), P()),
        check_vma=False,
    )
```

profile of v0, /device:TPU:0, one launch (start us, length us, event | category | flops | bytes accessed | tf_op | source)
XLA Modules:
  0.0 134.4 jit_solution(5286458204152960814)
XLA Ops:
  0.7 0.7 fusion.47
  1.4 0.5 collective-permute-start.1
  1.8 1.0 copy.77
  2.9 0.1 collective-permute-start
  3.0 1.0 copy.84
  4.0 0.5 collective-permute-start.2
  5.2 0.5 compare_select_fusion
  5.7 1.2 dynamic-slice_select_fusion
  7.6 1.5 %select_reduce_fusion.1 = bf16[512]{0:T(512)(128)(2,1)S(1)} fusion(bf16[128,512]{0,1:T(8,128)(2,1)S(1)} %bitcast.150, s32[]{:T(128)} %bitcast.9, pred[]{:T(512)} %bitcast.11), kind=kLoop, calls=%fused_computation.51 | loop fusion | flops 512 | bytes 2053 | tf_op jit(solution)/shard_map/jit(_take)/select_n | solution.py:36
  9.1 1.3 fusion.48
  10.5 1.3 dynamic-update-slice.2
  11.8 0.8 dynamic-update-slice.3
  12.5 1.5 %select_reduce_fusion = bf16[512]{0:T(512)(128)(2,1)S(1)} fusion(bf16[128,512]{0,1:T(8,128)(2,1)S(1)} %bitcast.147, s32[]{:T(128)} %bitcast.9, pred[]{:T(512)} %bitcast.11), kind=kLoop, calls=%fused_computation.50 | loop fusion | flops 512 | bytes 2053 | tf_op jit(solution)/shard_map/jit(_take)/select_n | solution.py:37
  14.1 15.4 %all-reduce.3 = (bf16[8]{0:T(256)(128)(2,1)S(1)}, bf16[8]{0:T(256)(128)(2,1)S(1)}) all-reduce(bf16[8]{0:T(256)(128)(2,1)S(1)} %dynamic-update-slice.3, bf16[8]{0:T(256)(128)(2,1)S(1)} %dynamic-update-slice.2), channel_id=2, replica_groups=mesh['dp'=4,'ctx'=8] {'ctx'}, use_global_device_ids=true, to_apply=%add.1 | all-reduce | flops 16 | bytes 64
  29.4 7.9 %all-gather.1 = bf16[8,1,512]{2,1,0:T(2,128)(2,1)S(1)} all-gather(bf16[1,1,512]{2,1,0:T(2,128)(2,1)S(1)} %reshape.296), channel_id=1, replica_groups=mesh['dp'=4,'ctx'=8] {'ctx'}, dimensions={0}, use_global_device_ids=true | all-gather | bytes 9216 | tf_op jit(solution)/shard_map/all_gather | solution.py:41
  37.4 1.4 %reshape_squeeze.6 = bf16[128,4,4,128]{3,2,1,0:T(4,128)(2,1)S(1)} reshape(bf16[1,128,2048]{2,1,0:T(8,128)(2,1)} %param.10) | data formatting | bytes 1048576 | tf_op jit(solution)/shard_map/reshape;squeeze | solution.py:24
  38.8 0.8 copy.79
  39.5 0.7 max.28
  40.2 8.9 %all-gather.2 = bf16[8,1,512]{2,1,0:T(2,128)(2,1)S(1)} all-gather(bf16[1,1,512]{2,1,0:T(2,128)(2,1)S(1)} %reshape.298), channel_id=1, replica_groups=mesh['dp'=4,'ctx'=8] {'ctx'}, dimensions={0}, use_global_device_ids=true | all-gather | bytes 9216 | tf_op jit(solution)/shard_map/all_gather | solution.py:42
  49.1 0.5 fusion.42
  49.6 0.1 compare_and_fusion
  49.7 0.3 fusion.50
  50.0 0.1 copy.86
  50.1 0.4 reshape_squeeze.7
  50.5 0.0 copy-start
  50.5 0.5 copy.101
  51.0 0.1 broadcast_compare_fusion
  51.1 0.0 collective-permute-done
  51.1 0.2 copy-done
  51.3 0.8 copy.80
  52.1 1.4 %fusion.49 = (f32[128,4,4]{0,2,1:T(4,128)S(1)}, f32[128,4,4,256]{0,3,2,1:T(8,128)S(1)}) fusion(bf16[128,4,4,128]{3,2,1,0:T(4,128)(2,1)S(1)} %reshape_squeeze.6, bf16[128,4,128]{2,0,1:T(8,128)(2,1)} %copy.80, bf16[128,4,128]{2,0,1:T(8,128)(2,1)} %copy.79, pred[128,256]{0,1:T(8,128)(4,1)S(1)} %broadcast_compare_fusion), kind=kOutput, calls=%fused_computation.93 | convolution fusion | flops 136312832 | bytes 2924544 | tf_op jit(solution)/shard_map/tkgd,jkd->tkgj/dot_general | solution.py:57
  53.5 0.8 maximum_maximum_fusion
  54.3 0.3 exponential_reduce_fusion
  54.7 0.0 collective-permute-done.2
  54.7 1.0 copy.87
  55.7 0.1 log_add_fusion
  55.8 0.5 fusion.23
  56.3 1.4 %fusion.7 = f32[128,4,4,128]{0,3,2,1:T(8,128)} fusion(f32[4,128,128,4]{2,1,3,0:T(8,128)S(1)} %fusion.23, f32[128,4,4,8]{0,3,2,1:T(8,128)S(1)} %get-tuple-element.56, f32[128,4,4]{0,2,1:T(4,128)S(1)} %log_add_fusion, bf16[8,1,512]{2,1,0:T(2,128)(2,1)S(1)} %all-gather.2), kind=kOutput, calls=%fused_computation.15 | convolution fusion | flops 5013504 | bytes 2179072 | tf_op jit(solution)/shard_map/tkgc,ckd->tkgd/dot_general | solution.py:84
  57.7 2.6 %copy.113 = f32[128,4,4,128]{3,2,1,0:T(4,128)} copy(f32[128,4,4,128]{0,3,2,1:T(8,128)} %fusion.7) | data formatting | bytes 2097152
  60.3 2.8 %multiply_reduce_fusion = f32[128,4,4]{2,1,0:T(4,128)} fusion(f32[128,4,4,128]{3,2,1,0:T(4,128)} %copy.113, bf16[128,4,4,128]{3,2,1,0:T(4,128)(2,1)} %copy-done), kind=kLoop, calls=%fused_computation.30 | loop fusion | flops 784384 | bytes 1581056
  63.1 1.0 copy.114
  64.1 0.6 fusion.1
  64.7 0.2 fusion.15
  64.8 0.2 convolution_bitcast_fusion.3
  65.1 1.3 convolution_bitcast_fusion
  66.4 0.2 multiply_reduce_fusion.1
  66.6 0.5 fusion.9
  67.1 0.0 copy-start.1
  67.1 0.3 fusion.27
  67.5 0.4 collective-permute-start.3
  67.9 0.2 fusion.17
  68.1 23.4 %all-reduce.2 = f32[8,1024]{1,0:T(8,128)S(1)} all-reduce(f32[8,1024]{1,0:T(8,128)S(1)} %pad_maximum_fusion), channel_id=3, replica_groups=mesh['dp'=4,'ctx'=8] {'ctx'}, use_global_device_ids=true, to_apply=%region_4.6.clone | all-reduce | flops 8192 | bytes 65536
  91.5 0.1 neg.7
  91.6 0.0 collective-permute-start.4
  91.6 39.6 %psum.7 = f32[16]{0:T(128)} all-reduce(f32[16]{0:T(128)S(1)} %neg.7), channel_id=1, replica_groups=mesh['dp'=4,'ctx'=8] {'dp','ctx'}, use_global_device_ids=true, to_apply=%region_6.8 | all-reduce | flops 16 | bytes 128 | tf_op jit(solution)/shard_map/psum | solution.py:145
  131.2 0.3 fusion.5
  131.5 1.0 copy.103
  132.5 0.6 constant_dynamic-slice_fusion
  133.2 0.1 broadcast_multiply_fusion
  133.3 0.0 collective-permute-done.3
  133.3 0.1 copy.99
  133.5 0.0 collective-permute-done.4
  133.5 0.1 copy.102
  133.7 0.8 fusion.29
  (31 shorter events, 0.2 us)
Async XLA Ops:
  0.6 38.9 %copy-start.7 = (f32[16]{0:T(128)S(1)}, f32[16]{0:T(128)}, u32[]{:S(2)}) copy-start(f32[16]{0:T(128)} %param.17) | copy-start | bytes 196
  0.6 49.5 %copy-start.4 = (bf16[1,128,2048]{2,1,0:T(8,128)(2,1)S(1)}, bf16[1,128,2048]{2,1,0:T(8,128)(2,1)}, u32[]{:S(2)}) copy-start(bf16[1,128,2048]{2,1,0:T(8,128)(2,1)} %param.13) | copy-start | bytes 1572868
  1.4 49.6 %collective-permute-start.1 = (bf16[128]{0:T(256)(128)(2,1)S(1)}, bf16[128]{0:T(256)(128)(2,1)S(1)}, u32[]{:S(2)}, u32[]{:S(2)}) collective-permute-start(bf16[128]{0:T(256)(128)(2,1)S(1)} %get-tuple-element.45), channel_id=1, source_target_pairs={{0,1},{1,0},{2,3},{3,2},{4,5},{5,4},{6,7},{7,6},{8,9},{9,8},{10,11... | collective-permute-start | bytes 776 | tf_op jit(solution)/shard_map/ppermute | solution.py:14
  2.9 48.3 %collective-permute-start = (bf16[128,512]{0,1:T(8,128)(2,1)S(1)}, bf16[128,512]{0,1:T(8,128)(2,1)S(1)}, u32[]{:S(2)}, u32[]{:S(2)}) collective-permute-start(bf16[128,512]{0,1:T(8,128)(2,1)S(1)} %bitcast.149), channel_id=1, source_target_pairs={{0,1},{1,0},{2,3},{3,2},{4,5},{5,4},{6,7},{7,6},{8,9},{9,8},{10,11... | collective-permute-start | bytes 393224 | tf_op jit(solution)/shard_map/ppermute | solution.py:14
  4.0 50.7 %collective-permute-start.2 = (bf16[128,512]{0,1:T(8,128)(2,1)S(1)}, bf16[128,512]{0,1:T(8,128)(2,1)}, u32[]{:S(2)}, u32[]{:S(2)}) collective-permute-start(bf16[128,512]{0,1:T(8,128)(2,1)S(1)} %bitcast.146), channel_id=1, source_target_pairs={{0,1},{1,0},{2,3},{3,2},{4,5},{5,4},{6,7},{7,6},{8,9},{9,8},{10,11... | collective-permute-start | bytes 393224 | tf_op jit(solution)/shard_map/ppermute | solution.py:14
  50.5 0.8 copy-start
  53.5 2.2 %copy-start.5 = (f32[4,4]{1,0:T(4,128)S(1)}, f32[4,4]{1,0:T(4,128)}, u32[]{:S(2)}) copy-start(f32[4,4]{1,0:T(4,128)} %max.28) | copy-start | bytes 196
  65.1 2.0 %copy-start.2 = (bf16[128,4,128]{2,0,1:T(8,128)(2,1)S(1)}, bf16[128,4,128]{2,0,1:T(8,128)(2,1)}, u32[]{:S(2)}) copy-start(bf16[128,4,128]{2,0,1:T(8,128)(2,1)} %copy.79) | copy-start | bytes 393220
  65.1 2.0 %copy-start.3 = (bf16[128,4,128]{2,0,1:T(8,128)(2,1)S(1)}, bf16[128,4,128]{2,0,1:T(8,128)(2,1)}, u32[]{:S(2)}) copy-start(bf16[128,4,128]{2,0,1:T(8,128)(2,1)} %copy.80) | copy-start | bytes 393220
  67.1 24.4 %copy-start.1 = (f32[256,4,128]{0,2,1:T(8,128)S(1)}, f32[256,4,128]{0,2,1:T(8,128)}, u32[]{:S(2)}) copy-start(f32[256,4,128]{0,2,1:T(8,128)} %convolution_bitcast_fusion) | copy-start | bytes 1572868
  67.4 65.7 %copy-start.6 = (f32[128]{0:T(128)S(1)}, f32[128]{0:T(128)}, u32[]{:S(2)}) copy-start(f32[128]{0:T(128)} %fusion.42) | copy-start | bytes 1540
  67.5 65.8 %collective-permute-start.3 = (bf16[128,4,128]{0,2,1:T(8,128)(2,1)S(1)}, bf16[128,4,128]{0,2,1:T(8,128)(2,1)S(1)}, u32[]{:S(2)}, u32[]{:S(2)}) collective-permute-start(bf16[128,4,128]{0,2,1:T(8,128)(2,1)S(1)} %slice.59), channel_id=1, source_target_pairs={{0,1},{1,0},{2,3},{3,2},{4,5},{5,4},{6,7},{7,6},{8,9},{9,8},{10,11... | collective-permute-start | bytes 393224 | tf_op jit(solution)/shard_map/ppermute | solution.py:14
  91.6 41.9 %collective-permute-start.4 = (bf16[128,4,128]{0,2,1:T(8,128)(2,1)S(1)}, bf16[128,4,128]{0,2,1:T(8,128)(2,1)S(1)}, u32[]{:S(2)}, u32[]{:S(2)}) collective-permute-start(bf16[128,4,128]{0,2,1:T(8,128)(2,1)S(1)} %slice.58), channel_id=1, source_target_pairs={{0,1},{1,0},{2,3},{3,2},{4,5},{5,4},{6,7},{7,6},{8,9},{9,8},{10,11... | collective-permute-start | bytes 393224 | tf_op jit(solution)/shard_map/ppermute | solution.py:14
where the time goes:
time: 135 us; the launch traced here: 134 us
  blocking collectives  95.2 us (71%)
  local copies, waits for them, and re-layouts  16.9 us (13%)
  other arithmetic  11.4 us (8%)
  matrix products  7.17 us (5%)
  between operations  2.28 us (2%)
  starting transfers between devices  1.49 us (1%)
    psum x1, blocking collectives, on_device(): sink_grad = lax.psum(sink_local, ('dp', 'ctx'))  39.6 us
    unnamed x2, blocking collectives  38.8 us
    unnamed x28, local copies, waits for them, and re-layouts  9.9 us
    all_gather x1, blocking collectives, on_device(): lax.all_gather(picked_values, 'ctx', axis=0, tiled=True)  8.9 us
    all_gather x1, blocking collectives, on_device(): lax.all_gather(picked_keys, 'ctx', axis=0, tiled=True)  7.9 us
    unnamed x1, other arithmetic  2.77 us
  transfers between devices with their start and end apart: 5, of which 0 were waited for; matrix products, arithmetic and copies ran while one was open for 16% of the time, Pallas kernels for 0%

commit v1 on v0

v1 whole, which is shorter than its diff:
```python
import functools

import jax
import jax.numpy as jnp
from jax import lax
from jax.experimental import pallas as pl
from jax.experimental.pallas import tpu as pltpu
from jax.sharding import PartitionSpec as P

HEADS = 16
KV_HEADS = 4
HDIM = 128
BUCKET = 128
GROUP = HEADS // KV_HEADS
NEG = -1e30
PACK = 16
COUNT_ROW = 8
MARK_ROW = 9
TOKEN_MARK_ROW = 10

f32 = jnp.float32
bf16 = jnp.bfloat16
NT = (((1,), (1,)), ((), ()))
TN = (((0,), (0,)), ((), ()))
VMEM = pl.BlockSpec(memory_space=pltpu.VMEM)
SMEM = pl.BlockSpec(memory_space=pltpu.SMEM)


def moved(array, axis, apart):
    return lax.ppermute(array, axis, [(i, i ^ apart) for i in range(lax.axis_size(axis))])


def rounds(size, first):
    found, base = [], first
    while base < size:
        found.append([base] if base * 2 >= size else [base, 2 * base, 3 * base])
        base *= 2 if base * 2 >= size else 4
    return found


def iota(shape, dim):
    return lax.broadcasted_iota(jnp.int32, shape, dim)


def pack_kernel(row_ref, count_ref, keys_ref, values_ref, rank_ref, out_ref):
    length = keys_ref.shape[1]
    row = row_ref[0, 0]
    pick = (iota((PACK, length), 1) == row).astype(bf16)
    key = jnp.dot(pick, keys_ref[0], preferred_element_type=f32)
    value = jnp.dot(pick, values_ref[0], preferred_element_type=f32)
    marks = (rank_ref[...] >= BUCKET).astype(f32)
    lanes = iota((1, length), 1)
    mark = jnp.sum(jnp.where(lanes == row, marks, 0.0), axis=1, keepdims=True)
    rows = iota((PACK, HDIM), 0)
    tile = jnp.zeros((PACK, HDIM), f32)
    for j in range(KV_HEADS):
        tile = jnp.where(rows == j, key[:, j * HDIM : (j + 1) * HDIM], tile)
        tile = jnp.where(rows == KV_HEADS + j, value[:, j * HDIM : (j + 1) * HDIM], tile)
    tile = jnp.where(rows == COUNT_ROW, count_ref[0, 0].astype(f32), tile)
    tile = jnp.where(rows == MARK_ROW, mark, tile)
    tile = jnp.where(rows == TOKEN_MARK_ROW, marks, tile)
    out_ref[...] = tile.astype(bf16)


def main_kernel(
    slots, query_ref, grad_ref, keys_ref, values_ref, far_keys_ref, far_values_ref, packs_ref, sink_ref,
    dq_ref, own_ref, far_ref, keep_ref, send_ref, sinks_ref,
):
    length = query_ref.shape[1]
    padded = -(-slots // 16) * 16
    scale = HDIM**-0.5
    packs = packs_ref[...]

    def chosen(row):
        at = iota((padded, slots * PACK), 1)
        slot = iota((padded, slots * PACK), 0)
        return jnp.dot(
            (at == slot * PACK + row).astype(bf16), packs, preferred_element_type=f32
        )

    own_marks = packs[TOKEN_MARK_ROW : TOKEN_MARK_ROW + 1, :].astype(f32)
    far_marks = packs[PACK + TOKEN_MARK_ROW : PACK + TOKEN_MARK_ROW + 1, :].astype(f32)
    own_column = jnp.transpose(jnp.broadcast_to(own_marks, (length, length)))
    far_column = jnp.transpose(jnp.broadcast_to(far_marks, (length, length)))
    slot_at = iota((padded, length), 0)
    slot_bias = jnp.log(jnp.maximum(chosen(COUNT_ROW), 1.0))
    same = (slot_at < 2) & (chosen(MARK_ROW) == own_marks)
    slot_bias = jnp.where(same | (slot_at >= slots), NEG, slot_bias)
    bias = jnp.concatenate(
        [
            jnp.where(own_column == own_marks, 0.0, NEG),
            jnp.where(far_column == own_marks, 0.0, NEG),
            slot_bias,
        ],
        0,
    )
    bias = jnp.concatenate([bias] * GROUP, 1)
    sink_diag = iota((HEADS, HDIM), 0) == iota((HEADS, HDIM), 1)
    sinks = jnp.zeros((1, HDIM), f32)
    lane = iota((1, HDIM), 1)
    for j in range(KV_HEADS):
        cols = slice(j * HDIM, (j + 1) * HDIM)
        heads = [slice((j * GROUP + g) * HDIM, (j * GROUP + g + 1) * HDIM) for g in range(GROUP)]
        keys = jnp.concatenate(
            [keys_ref[0, :, cols], far_keys_ref[0, :, cols], chosen(j).astype(bf16)], 0
        )
        values = jnp.concatenate(
            [values_ref[0, :, cols], far_values_ref[0, :, cols], chosen(KV_HEADS + j).astype(bf16)], 0
        )
        query = jnp.concatenate([query_ref[0, :, at] for at in heads], 0)
        grad = jnp.concatenate([grad_ref[0, :, at] for at in heads], 0)
        sink = jnp.concatenate(
            [jnp.full((1, length), sink_ref[j * GROUP + g], f32) for g in range(GROUP)], 1
        )
        score = lax.dot_general(keys, query, NT, preferred_element_type=f32) * scale + bias
        top = jnp.maximum(jnp.max(score, axis=0, keepdims=True), sink)
        weight = jnp.exp(score - top)
        sink_weight = jnp.exp(sink - top)
        inverse = 1.0 / (jnp.sum(weight, axis=0, keepdims=True) + sink_weight)
        prob = weight * inverse
        up = lax.dot_general(values, grad, NT, preferred_element_type=f32)
        delta = jnp.sum(prob * up, axis=0, keepdims=True)
        ds = (prob * (up - delta)).astype(bf16)
        half = prob.astype(bf16)
        sink_row = sink_weight * inverse * delta
        for g in range(GROUP):
            total = jnp.sum(sink_row[:, g * length : (g + 1) * length], axis=1, keepdims=True)
            sinks = sinks - jnp.where(lane == j * GROUP + g, total, 0.0)
        dk = lax.dot_general(ds, query, (((1,), (0,)), ((), ())), preferred_element_type=f32) * scale
        dv = lax.dot_general(half, grad, (((1,), (0,)), ((), ())), preferred_element_type=f32)
        dq = lax.dot_general(keys, ds, TN, preferred_element_type=f32) * scale
        for g in range(GROUP):
            dq_ref[0, :, heads[g]] = jnp.transpose(dq[:, g * length : (g + 1) * length]).astype(bf16)
        wide = KV_HEADS * HDIM
        for base, part in ((0, dk), (wide, dv)):
            at = slice(base + j * HDIM, base + (j + 1) * HDIM)
            own_ref[:, at] = part[:length]
            far_ref[:, at] = part[length : 2 * length].astype(bf16)
        for row, part in ((j, dk), (KV_HEADS + j, dv)):
            for slot in range(slots):
                to_ref = send_ref if slot % 2 else keep_ref
                to_ref[slot // 2, row : row + 1, :] = part[2 * length + slot : 2 * length + slot + 1]
    sinks = jnp.where(iota((8, HDIM), 0) == 0, sinks, 0.0)
    sinks_ref[...] = sinks
    send_ref[slots // 2] = sinks
    keep_ref[slots // 2] = sinks


def last_kernel(row_ref, own_ref, recv_ref, *refs):
    slot_refs, (dk_ref, dv_ref) = refs[:-2], refs[-2:]
    length = own_ref.shape[0]
    slot = slot_refs[0][...]
    for more in slot_refs[1:]:
        slot = slot + more[...]
    mine = iota((length, HDIM), 0) == row_ref[0, 0]
    for out_ref, base in ((dk_ref, 0), (dv_ref, KV_HEADS)):
        for j in range(KV_HEADS):
            at = slice((base + j) * HDIM, (base + j + 1) * HDIM)
            total = own_ref[:, at] + recv_ref[:, at].astype(f32)
            total = total + jnp.where(mine, slot[base + j : base + j + 1, :], 0.0)
            out_ref[0, :, j * HDIM : (j + 1) * HDIM] = total.astype(bf16)


def on_device(
    query_rows, key_rows, value_rows, grad_rows, bucket_rank, sample_rows, sample_count, sink_logit
):
    length = query_rows.shape[1]
    wide = KV_HEADS * HDIM
    slots = lax.axis_size("ctx")
    far_keys = moved(key_rows, "ctx", 1)
    far_values = moved(value_rows, "ctx", 1)
    packs = pl.pallas_call(
        pack_kernel,
        out_shape=jax.ShapeDtypeStruct((PACK, HDIM), bf16),
        in_specs=[SMEM, SMEM, VMEM, VMEM, VMEM],
        out_specs=VMEM,
        name="pack_sample",
    )(sample_rows, sample_count, key_rows, value_rows, bucket_rank)
    packs = jnp.concatenate([packs, moved(packs, "ctx", 1)], 0)
    for offsets in rounds(slots, 2):
        packs = jnp.concatenate([packs] + [moved(packs, "ctx", d) for d in offsets], 0)
    half = slots // 2
    dq, own, far, keep, send, sinks = pl.pallas_call(
        functools.partial(main_kernel, slots),
        out_shape=[
            jax.ShapeDtypeStruct((1, length, HEADS * HDIM), bf16),
            jax.ShapeDtypeStruct((length, 2 * wide), f32),
            jax.ShapeDtypeStruct((length, 2 * wide), bf16),
            jax.ShapeDtypeStruct((half + 1, 8, HDIM), f32),
            jax.ShapeDtypeStruct((half + 1, 8, HDIM), f32),
            jax.ShapeDtypeStruct((8, HDIM), f32),
        ],
        in_specs=[VMEM] * 7 + [SMEM],
        out_specs=[VMEM] * 6,
        compiler_params=pltpu.CompilerParams(vmem_limit_bytes=24 * 1024 * 1024),
        name="attend",
    )(query_rows, grad_rows, key_rows, value_rows, far_keys, far_values, packs, sink_logit)
    terms = keep + moved(send, "ctx", 1)
    recv = moved(far, "ctx", 1)
    slots_left = half
    pieces = [terms[:half], terms[half]]
    for offsets in rounds(slots, 2):
        parts = len(offsets) + 1
        blocks, sinks = pieces
        blocks = blocks.reshape(blocks.shape[0] // parts, parts, 8, HDIM)
        arrived = [
            moved(jnp.concatenate([blocks[:, i + 1], sinks[None]], 0), "ctx", d)
            for i, d in enumerate(offsets)
        ]
        blocks = blocks[:, 0]
        if parts == 4:
            blocks = (blocks + arrived[0][:-1]) + (arrived[1][:-1] + arrived[2][:-1])
            sinks = (sinks + arrived[0][-1]) + (arrived[1][-1] + arrived[2][-1])
        else:
            blocks = blocks + arrived[0][:-1]
            sinks = sinks + arrived[0][-1]
        pieces = [blocks, sinks]
    slot, sinks = pieces
    dk, dv = pl.pallas_call(
        last_kernel,
        out_shape=[jax.ShapeDtypeStruct((1, length, wide), bf16)] * 2,
        in_specs=[SMEM] + [VMEM] * 3,
        out_specs=[VMEM] * 2,
        name="add_up",
    )(sample_rows, own, recv, slot[0])
    for offsets in rounds(lax.axis_size("dp"), 1):
        arrived = [moved(sinks, "dp", d) for d in offsets]
        if len(offsets) == 3:
            sinks = (sinks + arrived[0]) + (arrived[1] + arrived[2])
        else:
            sinks = sinks + arrived[0]
    return dq, dk, dv, sinks[0, :HEADS]


def solution(mesh):
    return jax.shard_map(
        on_device,
        mesh=mesh,
        in_specs=(
            P("dp", "ctx", None),
            P("dp", "ctx", None),
            P("dp", "ctx", None),
            P("dp", "ctx", None),
            P("dp", "ctx"),
            P("dp", "ctx"),
            P("dp", "ctx"),
            P(),
        ),
        out_specs=(P("dp", "ctx", None), P("dp", "ctx", None), P("dp", "ctx", None), P()),
        check_vma=False,
    )
```

time: 135 us -> 41.7 us (0.31)
  blocking collectives: 95.2 us -> 0 us
  starting transfers between devices: 1.49 us -> 13.4 us
  waiting for transfers between devices: 0.01 us -> 11.9 us
  local copies, waits for them, and re-layouts: 16.9 us -> 5.42 us
  other arithmetic: 11.4 us -> 0.61 us
  Pallas kernels: 0 us -> 7.99 us
  matrix products: 7.17 us -> 0 us
    psum x1 -> x0, blocking collectives: 39.6 us -> none  [on_device(): sink_grad = lax.psum(sink_local, ('dp', 'ctx'))]
    unnamed x2 -> x0, blocking collectives: 38.8 us -> none
    all_gather x2 -> x0, blocking collectives: 16.8 us -> none  [the longest x1 8.9 us: on_device(): lax.all_gather(picked_values, 'ctx', axis=0, tiled=True)]
    ppermute x5 -> x14, waiting for transfers between devices: 0.01 us -> 11.9 us  [moved(): lax.ppermute(array, axis, [(i, i ^ apart) for i in range(lax.axis_size(ax...]
    ppermute x5 -> x14, starting transfers between devices: 1.49 us -> 13.4 us  [moved(): lax.ppermute(array, axis, [(i, i ^ apart) for i in range(lax.axis_size(ax...]
    pallas_call x0 -> x3, Pallas kernels: none -> 7.99 us  [the longest x1 4.36 us: on_device(): pl.pallas_call(functools.partial(main_kernel, slots), out_shape=[jax.Shap...]
    dot_general x12 -> x0, matrix products: 7.17 us -> none  [the longest x1 1.42 us: on_device(): jnp.einsum('tkgd,jkd->tkgj', query_heads, pair_keys, preferred_element_ty...]
    unnamed x28 -> x20, local copies, waits for them, and re-layouts: 9.9 us -> 4.89 us
  transfers between devices with their start and end apart: 5 -> 14, of which waited for: 0 -> 8; matrix products, arithmetic and copies ran while one was open for 16% -> 3% of each run, Pallas kernels for 0% -> 4%
where the time goes in v1:
time: 41.7 us; the launch traced here: 41.4 us
  starting transfers between devices  13.4 us (32%)
  waiting for transfers between devices  11.9 us (29%)
  Pallas kernels  7.99 us (19%)
  local copies, waits for them, and re-layouts  5.42 us (13%)
  between operations  2.03 us (5%)
  other arithmetic  0.61 us (1%)
    ppermute x14, starting transfers between devices, moved(): lax.ppermute(array, axis, [(i, i ^ apart) for i in range(lax.axis_size(ax...  13.4 us
    ppermute x14, waiting for transfers between devices, moved(): lax.ppermute(array, axis, [(i, i ^ apart) for i in range(lax.axis_size(ax...  11.9 us
    unnamed x20, local copies, waits for them, and re-layouts  4.89 us
    pallas_call x1, Pallas kernels, on_device(): pl.pallas_call(functools.partial(main_kernel, slots), out_shape=[jax.Shap...  4.36 us
    pallas_call x1, Pallas kernels, on_device(): pl.pallas_call(last_kernel, out_shape=[jax.ShapeDtypeStruct((1, length, w...  1.87 us
    pallas_call x1, Pallas kernels, on_device(): pl.pallas_call(pack_kernel, out_shape=jax.ShapeDtypeStruct((PACK, HDIM),...  1.76 us
  transfers between devices with their start and end apart: 14, of which 8 were waited for; matrix products, arithmetic and copies ran while one was open for 3% of the time, Pallas kernels for 4%

profile of v1, /device:TPU:0, one launch (start us, length us, event | category | flops | bytes accessed | tf_op | source)
XLA Modules:
  0.0 41.4 jit_solution(14478285294741032486)
XLA Ops:
  0.6 0.5 %collective-permute-start = (bf16[1,128,512]{2,1,0:T(8,128)(2,1)}, bf16[1,128,512]{2,1,0:T(8,128)(2,1)S(1)}, u32[]{:S(2)}, u32[]{:S(2)}) collective-permute-start(bf16[1,128,512]{2,1,0:T(8,128)(2,1)} %keys_ref.3), channel_id=1, source_target_pairs={{0,1},{1,0},{2,3},{3,2},{4,5},{5,4},{6,7},{7,6},{8,9},{9,8},{10,11... | collective-permute-start | bytes 393224 | tf_op jit(solution)/shard_map/ppermute | solution.py:30
  1.2 0.1 collective-permute-start.1
  2.5 0.0 copy-start
  2.5 0.0 copy-start.1
  2.5 1.8 %pack_sample.1 = bf16[16,128]{1,0:T(8,128)(2,1)} custom-call(s32[1,1]{1,0:T(1,128)S(6)} %copy.16.row_ref, s32[1,1]{1,0:T(1,128)S(6)} %copy.17.count_ref, bf16[1,128,512]{2,1,0:T(8,128)(2,1)} %keys_ref.3, bf16[1,128,512]{2,1,0:T(8,128)(2,1)} %values_ref.3, s32[1,128]{1,0:T(1,128)} %rank_ref.1), custom_call_target="tpu_custom_call" | custom-call | tf_op jit(solution)/shard_map/pack_sample/pallas_call | solution.py:172
  4.3 0.0 copy-start.7
  4.3 0.4 %collective-permute-start.2 = (bf16[16,128]{1,0:T(8,128)(2,1)}, bf16[16,128]{1,0:T(8,128)(2,1)S(1)}, u32[]{:S(2)}, u32[]{:S(2)}) collective-permute-start(bf16[16,128]{1,0:T(8,128)(2,1)} %pack_sample.1), channel_id=1, source_target_pairs={{0,1},{1,0},{2,3},{3,2},{4,5},{5,4},{6,7},{7,6},{8,9},{9,8},{10,11... | collective-permute-start | bytes 12296 | tf_op jit(solution)/shard_map/ppermute | solution.py:30
  4.7 0.7 %constant_dynamic-update-slice_fusion.4 = bf16[128,128]{1,0:T(8,128)(2,1)S(1)} fusion(bf16[16,128]{1,0:T(8,128)(2,1)} %pack_sample.1), kind=kLoop, calls=%fused_computation.5 | loop fusion | bytes 8192
  5.4 0.3 collective-permute-done.2
  5.8 0.0 copy-done.7
  5.8 3.8 %collective-permute-start.5 = (bf16[32,128]{1,0:T(8,128)(2,1)S(1)}, bf16[32,128]{1,0:T(8,128)(2,1)S(1)}, u32[]{:S(2)}, u32[]{:S(2)}) collective-permute-start(bf16[32,128]{1,0:T(8,128)(2,1)S(1)} %pad_maximum_fusion.3), channel_id=1, source_target_pairs={{0,6},{1,7},{2,4},{3,5},{4,2},{5,3},{6,0},{7,1},{8,14},{9,15},{10,... | collective-permute-start | bytes 24584 | tf_op jit(solution)/shard_map/ppermute | solution.py:30
  9.6 0.5 %collective-permute-start.4 = (bf16[32,128]{1,0:T(8,128)(2,1)S(1)}, bf16[32,128]{1,0:T(8,128)(2,1)S(1)}, u32[]{:S(2)}, u32[]{:S(2)}) collective-permute-start(bf16[32,128]{1,0:T(8,128)(2,1)S(1)} %pad_maximum_fusion.3), channel_id=1, source_target_pairs={{0,4},{1,5},{2,6},{3,7},{4,0},{5,1},{6,2},{7,3},{8,12},{9,13},{10,... | collective-permute-start | bytes 24584 | tf_op jit(solution)/shard_map/ppermute | solution.py:30
  10.1 0.1 collective-permute-start.3
  10.2 3.5 %collective-permute-done.3 = bf16[32,128]{1,0:T(8,128)(2,1)S(1)} collective-permute-done((bf16[32,128]{1,0:T(8,128)(2,1)S(1)}, bf16[32,128]{1,0:T(8,128)(2,1)S(1)}, u32[]{:S(2)}, u32[]{:S(2)}) %collective-permute-start.3) | collective-permute-done | bytes 8224 | tf_op jit(solution)/shard_map/ppermute | solution.py:30
  13.7 0.0 collective-permute-done.4
  13.7 0.0 copy-start.5
  13.7 0.0 collective-permute-done.5
  13.8 0.0 collective-permute-done.far_keys_ref
  13.8 0.0 collective-permute-done.1.far_values_ref
  13.8 0.0 copy-done
  13.8 0.0 copy-done.1
  13.8 0.6 %copy-done.5 = f32[16]{0:T(128)S(1)} copy-done((f32[16]{0:T(128)S(1)}, f32[16]{0:T(128)}, u32[]{:S(2)}) %copy-start.5) | copy-done | bytes 88
  14.4 0.0 copy-start.2
  14.4 1.0 %copy-done.2 = bf16[1,128,2048]{2,1,0:T(8,128)(2,1)S(1)} copy-done((bf16[1,128,2048]{2,1,0:T(8,128)(2,1)S(1)}, bf16[1,128,2048]{2,1,0:T(8,128)(2,1)}, u32[]{:S(2)}) %copy-start.2) | copy-done | bytes 524312
  15.4 0.0 copy-start.3
  15.4 1.0 %copy-done.3 = bf16[1,128,2048]{2,1,0:T(8,128)(2,1)S(1)} copy-done((bf16[1,128,2048]{2,1,0:T(8,128)(2,1)S(1)}, bf16[1,128,2048]{2,1,0:T(8,128)(2,1)}, u32[]{:S(2)}) %copy-start.3) | copy-done | bytes 524312
  16.5 4.4 %attend.1 = (bf16[1,128,2048]{2,1,0:T(8,128)(2,1)}, f32[128,1024]{1,0:T(8,128)S(1)}, bf16[128,1024]{1,0:T(8,128)(2,1)S(1)}, f32[5,8,128]{2,1,0:T(8,128)S(1)}, f3...) custom-call(bf16[1,128,2048]{2,1,0:T(8,128)(2,1)S(1)} %copy-done.2, bf16[1,128,2048]{2,1,0:T(8,128)(2,1)S(1)} %copy-done.3, ...), custom_call_target="tpu_custom_call" | custom-call | tf_op jit(solution)/shard_map/attend/pallas_call | solution.py:183
  20.8 0.0 copy-start.4
  20.8 0.8 %copy-done.4 = f32[128,1024]{1,0:T(8,128)} copy-done((f32[128,1024]{1,0:T(8,128)}, f32[128,1024]{1,0:T(8,128)S(1)}, u32[]{:S(2)}) %copy-start.4) | copy-done | bytes 524312
  21.6 0.0 collective-permute-start.7
  21.6 1.2 %collective-permute-done.7 = f32[5,8,128]{2,1,0:T(8,128)S(1)} collective-permute-done((f32[5,8,128]{2,1,0:T(8,128)S(1)}, f32[5,8,128]{2,1,0:T(8,128)S(1)}, u32[]{:S(2)}, u32[]{:S(2)}) %collective-permute-start.7) | collective-permute-done | bytes 20512 | tf_op jit(solution)/shard_map/ppermute | solution.py:30
  22.9 0.2 collective-permute-start.8
  23.1 2.8 %collective-permute-start.10 = (f32[2,8,128]{2,1,0:T(8,128)S(1)}, f32[2,8,128]{2,1,0:T(8,128)S(1)}, u32[]{:S(2)}, u32[]{:S(2)}) collective-permute-start(f32[2,8,128]{2,1,0:T(8,128)S(1)} %get-tuple-element.24), channel_id=1, source_target_pairs={{0,6},{1,7},{2,4},{3,5},{4,2},{5,3},{6,0},{7,1},{8,14},{9,15},{10,... | collective-permute-start | bytes 24584 | tf_op jit(solution)/shard_map/ppermute | solution.py:30
  25.9 0.5 %collective-permute-start.9 = (f32[2,8,128]{2,1,0:T(8,128)S(1)}, f32[2,8,128]{2,1,0:T(8,128)S(1)}, u32[]{:S(2)}, u32[]{:S(2)}) collective-permute-start(f32[2,8,128]{2,1,0:T(8,128)S(1)} %get-tuple-element.25), channel_id=1, source_target_pairs={{0,4},{1,5},{2,6},{3,7},{4,0},{5,1},{6,2},{7,3},{8,12},{9,13},{10,... | collective-permute-start | bytes 24584 | tf_op jit(solution)/shard_map/ppermute | solution.py:30
  26.4 0.2 collective-permute-done.8
  26.6 1.0 %collective-permute-done.10 = f32[2,8,128]{2,1,0:T(8,128)S(1)} collective-permute-done((f32[2,8,128]{2,1,0:T(8,128)S(1)}, f32[2,8,128]{2,1,0:T(8,128)S(1)}, u32[]{:S(2)}, u32[]{:S(2)}) %collective-permute-start.10) | collective-permute-done | bytes 8224 | tf_op jit(solution)/shard_map/ppermute | solution.py:30
  27.6 1.9 %collective-permute-done.9 = f32[2,8,128]{2,1,0:T(8,128)S(1)} collective-permute-done((f32[2,8,128]{2,1,0:T(8,128)S(1)}, f32[2,8,128]{2,1,0:T(8,128)S(1)}, u32[]{:S(2)}, u32[]{:S(2)}) %collective-permute-start.9) | collective-permute-done | bytes 8224 | tf_op jit(solution)/shard_map/ppermute | solution.py:30
  29.6 0.6 %fusion.1 = (f32[8,128]{1,0:T(8,128)S(1)}, f32[8,128]{1,0:T(8,128)}) fusion(f32[2,8,128]{2,1,0:T(8,128)S(1)} %collective-permute-done.10, f32[2,8,128]{2,1,0:T(8,128)S(1)} %collective-permute-done.9, f32[2,8,128]{2,1,0:T(8,128)S(1)} %collective-permute-done.8, f32[5,8,128]{2,1,0:T(8,128)S(1)} %add.35, f32[1,4,8,128]{3,2,1,0:T(8,128)S(1)} %slice_bitcast_fusion), kind=kLoop, calls=%fused_computation.12 | loop fusion | flops 6144 | bytes 40960 | tf_op jit(solution)/shard_map/add | solution.py:213
  30.2 3.6 %collective-permute-start.13 = (f32[8,128]{1,0:T(8,128)S(1)}, f32[8,128]{1,0:T(8,128)S(1)}, u32[]{:S(2)}, u32[]{:S(2)}) collective-permute-start(f32[8,128]{1,0:T(8,128)S(1)} %get-tuple-element.18), channel_id=1, source_target_pairs={{0,24},{8,16},{16,8},{24,0},{1,25},{9,17},{17,9},{25,1},{2,26},{10... | collective-permute-start | bytes 12296 | tf_op jit(solution)/shard_map/ppermute | solution.py:30
  33.8 0.0 collective-permute-start.12
  33.8 0.8 %collective-permute-start.11 = (f32[8,128]{1,0:T(8,128)S(1)}, f32[8,128]{1,0:T(8,128)S(1)}, u32[]{:S(2)}, u32[]{:S(2)}) collective-permute-start(f32[8,128]{1,0:T(8,128)S(1)} %get-tuple-element.18), channel_id=1, source_target_pairs={{0,8},{8,0},{16,24},{24,16},{1,9},{9,1},{17,25},{25,17},{2,10},{10... | collective-permute-start | bytes 12296 | tf_op jit(solution)/shard_map/ppermute | solution.py:30
  34.6 0.0 collective-permute-start.6
  34.6 1.0 %collective-permute-done.13 = f32[8,128]{1,0:T(8,128)S(1)} collective-permute-done((f32[8,128]{1,0:T(8,128)S(1)}, f32[8,128]{1,0:T(8,128)S(1)}, u32[]{:S(2)}, u32[]{:S(2)}) %collective-permute-start.13) | collective-permute-done | bytes 4128 | tf_op jit(solution)/shard_map/ppermute | solution.py:30
  35.6 2.7 %collective-permute-done.12 = f32[8,128]{1,0:T(8,128)S(1)} collective-permute-done((f32[8,128]{1,0:T(8,128)S(1)}, f32[8,128]{1,0:T(8,128)S(1)}, u32[]{:S(2)}, u32[]{:S(2)}) %collective-permute-start.12) | collective-permute-done | bytes 4128 | tf_op jit(solution)/shard_map/ppermute | solution.py:30
  38.3 0.0 collective-permute-done.11
  38.3 0.5 %slice_bitcast_fusion.5 = f32[16]{0:T(128)} fusion(f32[8,128]{1,0:T(8,128)S(1)} %add_add_fusion), kind=kLoop, calls=%fused_computation.23 | loop fusion | bytes 128 | tf_op jit(solution)/shard_map/squeeze | solution.py:232
  38.8 0.0 collective-permute-done.6.recv_ref
  38.8 0.0 copy-start.6
  38.8 0.7 %copy-done.6 = bf16[128,1024]{1,0:T(8,128)(2,1)} copy-done((bf16[128,1024]{1,0:T(8,128)(2,1)}, bf16[128,1024]{1,0:T(8,128)(2,1)S(1)}, u32[]{:S(2)}) %copy-start.6) | copy-done | bytes 262168
  39.5 1.9 %add_up.1 = (bf16[1,128,512]{2,1,0:T(8,128)(2,1)}, bf16[1,128,512]{2,1,0:T(8,128)(2,1)}) custom-call(s32[1,1]{1,0:T(1,128)S(6)} %copy.16.row_ref, f32[128,1024]{1,0:T(8,128)} %copy-done.4, bf16[128,1024]{1,0:T(8,128)(2,1)} %copy-done.6, f32[8,128]{1,0:T(8,128)} %get-tuple-element.19.refs_0_), custom_call_target="tpu_custom_call" | custom-call | tf_op jit(solution)/shard_map/add_up/pallas_call | solution.py:219
  (11 shorter events, 0.1 us)
Async XLA Ops:
  0.6 13.1 %collective-permute-start = (bf16[1,128,512]{2,1,0:T(8,128)(2,1)}, bf16[1,128,512]{2,1,0:T(8,128)(2,1)S(1)}, u32[]{:S(2)}, u32[]{:S(2)}) collective-permute-start(bf16[1,128,512]{2,1,0:T(8,128)(2,1)} %keys_ref.3), channel_id=1, source_target_pairs={{0,1},{1,0},{2,3},{3,2},{4,5},{5,4},{6,7},{7,6},{8,9},{9,8},{10,11... | collective-permute-start | bytes 393224 | tf_op jit(solution)/shard_map/ppermute | solution.py:30
  1.2 12.6 %collective-permute-start.1 = (bf16[1,128,512]{2,1,0:T(8,128)(2,1)}, bf16[1,128,512]{2,1,0:T(8,128)(2,1)S(1)}, u32[]{:S(2)}, u32[]{:S(2)}) collective-permute-start(bf16[1,128,512]{2,1,0:T(8,128)(2,1)} %values_ref.3), channel_id=1, source_target_pairs={{0,1},{1,0},{2,3},{3,2},{4,5},{5,4},{6,7},{7,6},{8,9},{9,8},{10,11... | collective-permute-start | bytes 393224 | tf_op jit(solution)/shard_map/ppermute | solution.py:30
  2.5 11.3 %copy-start = (bf16[1,128,512]{2,1,0:T(8,128)(2,1)S(1)}, bf16[1,128,512]{2,1,0:T(8,128)(2,1)}, u32[]{:S(2)}) copy-start(bf16[1,128,512]{2,1,0:T(8,128)(2,1)} %keys_ref.3) | copy-start | bytes 393220
  2.5 11.3 %copy-start.1 = (bf16[1,128,512]{2,1,0:T(8,128)(2,1)S(1)}, bf16[1,128,512]{2,1,0:T(8,128)(2,1)}, u32[]{:S(2)}) copy-start(bf16[1,128,512]{2,1,0:T(8,128)(2,1)} %values_ref.3) | copy-start | bytes 393220
  4.3 1.5 %copy-start.7 = (bf16[16,128]{1,0:T(8,128)(2,1)S(1)}, bf16[16,128]{1,0:T(8,128)(2,1)}, u32[]{:S(2)}) copy-start(bf16[16,128]{1,0:T(8,128)(2,1)} %pack_sample.1) | copy-start | bytes 12292
  4.3 1.5 %collective-permute-start.2 = (bf16[16,128]{1,0:T(8,128)(2,1)}, bf16[16,128]{1,0:T(8,128)(2,1)S(1)}, u32[]{:S(2)}, u32[]{:S(2)}) collective-permute-start(bf16[16,128]{1,0:T(8,128)(2,1)} %pack_sample.1), channel_id=1, source_target_pairs={{0,1},{1,0},{2,3},{3,2},{4,5},{5,4},{6,7},{7,6},{8,9},{9,8},{10,11... | collective-permute-start | bytes 12296 | tf_op jit(solution)/shard_map/ppermute | solution.py:30
  5.8 8.0 %collective-permute-start.5 = (bf16[32,128]{1,0:T(8,128)(2,1)S(1)}, bf16[32,128]{1,0:T(8,128)(2,1)S(1)}, u32[]{:S(2)}, u32[]{:S(2)}) collective-permute-start(bf16[32,128]{1,0:T(8,128)(2,1)S(1)} %pad_maximum_fusion.3), channel_id=1, source_target_pairs={{0,6},{1,7},{2,4},{3,5},{4,2},{5,3},{6,0},{7,1},{8,14},{9,15},{10,... | collective-permute-start | bytes 24584 | tf_op jit(solution)/shard_map/ppermute | solution.py:30
  9.6 4.2 %collective-permute-start.4 = (bf16[32,128]{1,0:T(8,128)(2,1)S(1)}, bf16[32,128]{1,0:T(8,128)(2,1)S(1)}, u32[]{:S(2)}, u32[]{:S(2)}) collective-permute-start(bf16[32,128]{1,0:T(8,128)(2,1)S(1)} %pad_maximum_fusion.3), channel_id=1, source_target_pairs={{0,4},{1,5},{2,6},{3,7},{4,0},{5,1},{6,2},{7,3},{8,12},{9,13},{10,... | collective-permute-start | bytes 24584 | tf_op jit(solution)/shard_map/ppermute | solution.py:30
  10.1 3.7 %collective-permute-start.3 = (bf16[32,128]{1,0:T(8,128)(2,1)S(1)}, bf16[32,128]{1,0:T(8,128)(2,1)S(1)}, u32[]{:S(2)}, u32[]{:S(2)}) collective-permute-start(bf16[32,128]{1,0:T(8,128)(2,1)S(1)} %pad_maximum_fusion.3), channel_id=1, source_target_pairs={{0,2},{1,3},{2,0},{3,1},{4,6},{5,7},{6,4},{7,5},{8,10},{9,11},{10,... | collective-permute-start | bytes 24584 | tf_op jit(solution)/shard_map/ppermute | solution.py:30
  13.7 0.7 %copy-start.5 = (f32[16]{0:T(128)S(1)}, f32[16]{0:T(128)}, u32[]{:S(2)}) copy-start(f32[16]{0:T(128)} %sink_ref.1) | copy-start | bytes 196
  14.4 1.0 %copy-start.2 = (bf16[1,128,2048]{2,1,0:T(8,128)(2,1)S(1)}, bf16[1,128,2048]{2,1,0:T(8,128)(2,1)}, u32[]{:S(2)}) copy-start(bf16[1,128,2048]{2,1,0:T(8,128)(2,1)} %query_ref.1) | copy-start | bytes 1572868
  15.4 1.0 %copy-start.3 = (bf16[1,128,2048]{2,1,0:T(8,128)(2,1)S(1)}, bf16[1,128,2048]{2,1,0:T(8,128)(2,1)}, u32[]{:S(2)}) copy-start(bf16[1,128,2048]{2,1,0:T(8,128)(2,1)} %grad_ref.1) | copy-start | bytes 1572868
  20.8 0.8 %copy-start.4 = (f32[128,1024]{1,0:T(8,128)}, f32[128,1024]{1,0:T(8,128)S(1)}, u32[]{:S(2)}) copy-start(f32[128,1024]{1,0:T(8,128)S(1)} %get-tuple-element.12.own_ref) | copy-start | bytes 1572868
  21.6 1.2 %collective-permute-start.7 = (f32[5,8,128]{2,1,0:T(8,128)S(1)}, f32[5,8,128]{2,1,0:T(8,128)S(1)}, u32[]{:S(2)}, u32[]{:S(2)}) collective-permute-start(f32[5,8,128]{2,1,0:T(8,128)S(1)} %get-tuple-element.15), channel_id=1, source_target_pairs={{0,1},{1,0},{2,3},{3,2},{4,5},{5,4},{6,7},{7,6},{8,9},{9,8},{10,11... | collective-permute-start | bytes 61448 | tf_op jit(solution)/shard_map/ppermute | solution.py:30
  22.9 3.7 %collective-permute-start.8 = (f32[2,8,128]{2,1,0:T(8,128)S(1)}, f32[2,8,128]{2,1,0:T(8,128)S(1)}, u32[]{:S(2)}, u32[]{:S(2)}) collective-permute-start(f32[2,8,128]{2,1,0:T(8,128)S(1)} %get-tuple-element.23), channel_id=1, source_target_pairs={{0,2},{1,3},{2,0},{3,1},{4,6},{5,7},{6,4},{7,5},{8,10},{9,11},{10,... | collective-permute-start | bytes 24584 | tf_op jit(solution)/shard_map/ppermute | solution.py:30
  23.1 4.6 %collective-permute-start.10 = (f32[2,8,128]{2,1,0:T(8,128)S(1)}, f32[2,8,128]{2,1,0:T(8,128)S(1)}, u32[]{:S(2)}, u32[]{:S(2)}) collective-permute-start(f32[2,8,128]{2,1,0:T(8,128)S(1)} %get-tuple-element.24), channel_id=1, source_target_pairs={{0,6},{1,7},{2,4},{3,5},{4,2},{5,3},{6,0},{7,1},{8,14},{9,15},{10,... | collective-permute-start | bytes 24584 | tf_op jit(solution)/shard_map/ppermute | solution.py:30
  25.9 3.7 %collective-permute-start.9 = (f32[2,8,128]{2,1,0:T(8,128)S(1)}, f32[2,8,128]{2,1,0:T(8,128)S(1)}, u32[]{:S(2)}, u32[]{:S(2)}) collective-permute-start(f32[2,8,128]{2,1,0:T(8,128)S(1)} %get-tuple-element.25), channel_id=1, source_target_pairs={{0,4},{1,5},{2,6},{3,7},{4,0},{5,1},{6,2},{7,3},{8,12},{9,13},{10,... | collective-permute-start | bytes 24584 | tf_op jit(solution)/shard_map/ppermute | solution.py:30
  30.2 5.4 %collective-permute-start.13 = (f32[8,128]{1,0:T(8,128)S(1)}, f32[8,128]{1,0:T(8,128)S(1)}, u32[]{:S(2)}, u32[]{:S(2)}) collective-permute-start(f32[8,128]{1,0:T(8,128)S(1)} %get-tuple-element.18), channel_id=1, source_target_pairs={{0,24},{8,16},{16,8},{24,0},{1,25},{9,17},{17,9},{25,1},{2,26},{10... | collective-permute-start | bytes 12296 | tf_op jit(solution)/shard_map/ppermute | solution.py:30
  33.8 4.5 %collective-permute-start.12 = (f32[8,128]{1,0:T(8,128)S(1)}, f32[8,128]{1,0:T(8,128)S(1)}, u32[]{:S(2)}, u32[]{:S(2)}) collective-permute-start(f32[8,128]{1,0:T(8,128)S(1)} %get-tuple-element.18), channel_id=1, source_target_pairs={{0,16},{8,24},{16,0},{24,8},{1,17},{9,25},{17,1},{25,9},{2,18},{10... | collective-permute-start | bytes 12296 | tf_op jit(solution)/shard_map/ppermute | solution.py:30
  33.8 4.5 %collective-permute-start.11 = (f32[8,128]{1,0:T(8,128)S(1)}, f32[8,128]{1,0:T(8,128)S(1)}, u32[]{:S(2)}, u32[]{:S(2)}) collective-permute-start(f32[8,128]{1,0:T(8,128)S(1)} %get-tuple-element.18), channel_id=1, source_target_pairs={{0,8},{8,0},{16,24},{24,16},{1,9},{9,1},{17,25},{25,17},{2,10},{10... | collective-permute-start | bytes 12296 | tf_op jit(solution)/shard_map/ppermute | solution.py:30
  34.6 4.3 %collective-permute-start.6 = (bf16[128,1024]{1,0:T(8,128)(2,1)S(1)}, bf16[128,1024]{1,0:T(8,128)(2,1)S(1)}, u32[]{:S(2)}, u32[]{:S(2)}) collective-permute-start(bf16[128,1024]{1,0:T(8,128)(2,1)S(1)} %get-tuple-element.13), channel_id=1, source_target_pairs={{0,1},{1,0},{2,3},{3,2},{4,5},{5,4},{6,7},{7,6},{8,9},{9,8},{10,11... | collective-permute-start | bytes 786440 | tf_op jit(solution)/shard_map/ppermute | solution.py:30
  38.8 0.7 %copy-start.6 = (bf16[128,1024]{1,0:T(8,128)(2,1)}, bf16[128,1024]{1,0:T(8,128)(2,1)S(1)}, u32[]{:S(2)}) copy-start(bf16[128,1024]{1,0:T(8,128)(2,1)S(1)} %collective-permute-done.6.recv_ref) | copy-start | bytes 786436

commit v2 on v1

--- a/solution.py
+++ b/solution.py
@@ -17,13 +17,14 @@
 COUNT_ROW = 8
 MARK_ROW = 9
 TOKEN_MARK_ROW = 10
+SINK_ROW = 8
 
 f32 = jnp.float32
 bf16 = jnp.bfloat16
 NT = (((1,), (1,)), ((), ()))
 TN = (((0,), (0,)), ((), ()))
 VMEM = pl.BlockSpec(memory_space=pltpu.VMEM)
-SMEM = pl.BlockSpec(memory_space=pltpu.SMEM)
+SMALL = pltpu.CompilerParams(vmem_limit_bytes=6 * 1024 * 1024)
 
 
 def moved(array, axis, apart):
@@ -44,7 +45,7 @@
 
 def pack_kernel(row_ref, count_ref, keys_ref, values_ref, rank_ref, out_ref):
     length = keys_ref.shape[1]
-    row = row_ref[0, 0]
+    row = row_ref[...]
     pick = (iota((PACK, length), 1) == row).astype(bf16)
     key = jnp.dot(pick, keys_ref[0], preferred_element_type=f32)
     value = jnp.dot(pick, values_ref[0], preferred_element_type=f32)
@@ -56,7 +57,7 @@
     for j in range(KV_HEADS):
         tile = jnp.where(rows == j, key[:, j * HDIM : (j + 1) * HDIM], tile)
         tile = jnp.where(rows == KV_HEADS + j, value[:, j * HDIM : (j + 1) * HDIM], tile)
-    tile = jnp.where(rows == COUNT_ROW, count_ref[0, 0].astype(f32), tile)
+    tile = jnp.where(rows == COUNT_ROW, count_ref[...].astype(f32), tile)
     tile = jnp.where(rows == MARK_ROW, mark, tile)
     tile = jnp.where(rows == TOKEN_MARK_ROW, marks, tile)
     out_ref[...] = tile.astype(bf16)
@@ -64,7 +65,7 @@
 
 def main_kernel(
     slots, query_ref, grad_ref, keys_ref, values_ref, far_keys_ref, far_values_ref, packs_ref, sink_ref,
-    dq_ref, own_ref, far_ref, keep_ref, send_ref, sinks_ref,
+    dq_ref, own_ref, far_ref, out_ref,
 ):
     length = query_ref.shape[1]
     padded = -(-slots // 16) * 16
@@ -95,9 +96,9 @@
         0,
     )
     bias = jnp.concatenate([bias] * GROUP, 1)
-    sink_diag = iota((HEADS, HDIM), 0) == iota((HEADS, HDIM), 1)
     sinks = jnp.zeros((1, HDIM), f32)
     lane = iota((1, HDIM), 1)
+    terms = []
     for j in range(KV_HEADS):
         cols = slice(j * HDIM, (j + 1) * HDIM)
         heads = [slice((j * GROUP + g) * HDIM, (j * GROUP + g + 1) * HDIM) for g in range(GROUP)]
@@ -110,7 +111,7 @@
         query = jnp.concatenate([query_ref[0, :, at] for at in heads], 0)
         grad = jnp.concatenate([grad_ref[0, :, at] for at in heads], 0)
         sink = jnp.concatenate(
-            [jnp.full((1, length), sink_ref[j * GROUP + g], f32) for g in range(GROUP)], 1
+            [jnp.broadcast_to(sink_ref[:, j * GROUP + g : j * GROUP + g + 1], (1, length)) for g in range(GROUP)], 1
         )
         score = lax.dot_general(keys, query, NT, preferred_element_type=f32) * scale + bias
         top = jnp.maximum(jnp.max(score, axis=0, keepdims=True), sink)
@@ -136,23 +137,32 @@
             at = slice(base + j * HDIM, base + (j + 1) * HDIM)
             own_ref[:, at] = part[:length]
             far_ref[:, at] = part[length : 2 * length].astype(bf16)
-        for row, part in ((j, dk), (KV_HEADS + j, dv)):
-            for slot in range(slots):
-                to_ref = send_ref if slot % 2 else keep_ref
-                to_ref[slot // 2, row : row + 1, :] = part[2 * length + slot : 2 * length + slot + 1]
-    sinks = jnp.where(iota((8, HDIM), 0) == 0, sinks, 0.0)
-    sinks_ref[...] = sinks
-    send_ref[slots // 2] = sinks
-    keep_ref[slots // 2] = sinks
-
-
-def last_kernel(row_ref, own_ref, recv_ref, *refs):
-    slot_refs, (dk_ref, dv_ref) = refs[:-2], refs[-2:]
+        terms.append((dk[2 * length :], dv[2 * length :]))
+    high = sinks.astype(bf16).astype(f32)
+    middle = (sinks - high).astype(bf16).astype(f32)
+    low = sinks - high - middle
+    rows = iota((PACK, HDIM), 0)
+    tile = jnp.zeros((PACK, HDIM), f32)
+    for i, part in enumerate((high, middle, low)):
+        tile = jnp.where(rows == SINK_ROW + i, part, tile)
+    out_ref[...] = jnp.broadcast_to(tile.astype(bf16)[None], out_ref.shape)
+    first = lax.axis_index("dp") * slots
+    for slot in range(slots):
+        mine = tile
+        for j in range(KV_HEADS):
+            for row, part in zip((j, KV_HEADS + j), terms[j]):
+                mine = jnp.where(rows == row, part[slot : slot + 1], mine)
+        out_ref[first + (lax.axis_index("ctx") ^ slot)] = mine.astype(bf16)
+
+
+def last_kernel(slots, row_ref, own_ref, recv_ref, terms_ref, dk_ref, dv_ref, sink_ref):
     length = own_ref.shape[0]
-    slot = slot_refs[0][...]
-    for more in slot_refs[1:]:
-        slot = slot + more[...]
-    mine = iota((length, HDIM), 0) == row_ref[0, 0]
+    parts = jnp.sum(terms_ref[...].astype(f32), axis=0)
+    sink = parts[SINK_ROW : SINK_ROW + 1] + parts[SINK_ROW + 1 : SINK_ROW + 2]
+    sink_ref[...] = (sink + parts[SINK_ROW + 2 : SINK_ROW + 3])[:, :HEADS]
+    first = lax.axis_index("dp") * slots
+    slot = jnp.sum(terms_ref[pl.ds(first, slots)].astype(f32), axis=0)
+    mine = iota((length, HDIM), 0) == row_ref[...]
     for out_ref, base in ((dk_ref, 0), (dv_ref, KV_HEADS)):
         for j in range(KV_HEADS):
             at = slice((base + j) * HDIM, (base + j + 1) * HDIM)
@@ -172,64 +182,40 @@
     packs = pl.pallas_call(
         pack_kernel,
         out_shape=jax.ShapeDtypeStruct((PACK, HDIM), bf16),
-        in_specs=[SMEM, SMEM, VMEM, VMEM, VMEM],
+        in_specs=[VMEM] * 5,
         out_specs=VMEM,
+        compiler_params=SMALL,
         name="pack_sample",
     )(sample_rows, sample_count, key_rows, value_rows, bucket_rank)
     packs = jnp.concatenate([packs, moved(packs, "ctx", 1)], 0)
     for offsets in rounds(slots, 2):
         packs = jnp.concatenate([packs] + [moved(packs, "ctx", d) for d in offsets], 0)
-    half = slots // 2
-    dq, own, far, keep, send, sinks = pl.pallas_call(
+    devices = slots * lax.axis_size("dp")
+    dq, own, far, terms = pl.pallas_call(
         functools.partial(main_kernel, slots),
         out_shape=[
             jax.ShapeDtypeStruct((1, length, HEADS * HDIM), bf16),
             jax.ShapeDtypeStruct((length, 2 * wide), f32),
             jax.ShapeDtypeStruct((length, 2 * wide), bf16),
-            jax.ShapeDtypeStruct((half + 1, 8, HDIM), f32),
-            jax.ShapeDtypeStruct((half + 1, 8, HDIM), f32),
-            jax.ShapeDtypeStruct((8, HDIM), f32),
+            jax.ShapeDtypeStruct((devices, PACK, HDIM), bf16),
         ],
-        in_specs=[VMEM] * 7 + [SMEM],
-        out_specs=[VMEM] * 6,
+        in_specs=[VMEM] * 8,
+        out_specs=[VMEM] * 4,
         compiler_params=pltpu.CompilerParams(vmem_limit_bytes=24 * 1024 * 1024),
         name="attend",
-    )(query_rows, grad_rows, key_rows, value_rows, far_keys, far_values, packs, sink_logit)
-    terms = keep + moved(send, "ctx", 1)
+    )(query_rows, grad_rows, key_rows, value_rows, far_keys, far_values, packs, sink_logit[None])
     recv = moved(far, "ctx", 1)
-    slots_left = half
-    pieces = [terms[:half], terms[half]]
-    for offsets in rounds(slots, 2):
-        parts = len(offsets) + 1
-        blocks, sinks = pieces
-        blocks = blocks.reshape(blocks.shape[0] // parts, parts, 8, HDIM)
-        arrived = [
-            moved(jnp.concatenate([blocks[:, i + 1], sinks[None]], 0), "ctx", d)
-            for i, d in enumerate(offsets)
-        ]
-        blocks = blocks[:, 0]
-        if parts == 4:
-            blocks = (blocks + arrived[0][:-1]) + (arrived[1][:-1] + arrived[2][:-1])
-            sinks = (sinks + arrived[0][-1]) + (arrived[1][-1] + arrived[2][-1])
-        else:
-            blocks = blocks + arrived[0][:-1]
-            sinks = sinks + arrived[0][-1]
-        pieces = [blocks, sinks]
-    slot, sinks = pieces
-    dk, dv = pl.pallas_call(
-        last_kernel,
-        out_shape=[jax.ShapeDtypeStruct((1, length, wide), bf16)] * 2,
-        in_specs=[SMEM] + [VMEM] * 3,
-        out_specs=[VMEM] * 2,
+    terms = lax.all_to_all(terms, ("dp", "ctx"), 0, 0, tiled=True)
+    dk, dv, sink_grad = pl.pallas_call(
+        functools.partial(last_kernel, slots),
+        out_shape=[jax.ShapeDtypeStruct((1, length, wide), bf16)] * 2
+        + [jax.ShapeDtypeStruct((1, HEADS), f32)],
+        in_specs=[VMEM] * 4,
+        out_specs=[VMEM] * 3,
+        compiler_params=SMALL,
         name="add_up",
-    )(sample_rows, own, recv, slot[0])
-    for offsets in rounds(lax.axis_size("dp"), 1):
-        arrived = [moved(sinks, "dp", d) for d in offsets]
-        if len(offsets) == 3:
-            sinks = (sinks + arrived[0]) + (arrived[1] + arrived[2])
-        else:
-            sinks = sinks + arrived[0]
-    return dq, dk, dv, sinks[0, :HEADS]
+    )(sample_rows, own, recv, terms)
+    return dq, dk, dv, sink_grad[0]
 
 
 def solution(mesh):

time: 41.7 us -> 34.6 us (0.83)
  blocking collectives: 0 us -> 13.1 us
  starting transfers between devices: 13.4 us -> 5.41 us
  waiting for transfers between devices: 11.9 us -> 4.42 us
  Pallas kernels: 7.99 us -> 4.89 us
  local copies, waits for them, and re-layouts: 5.42 us -> 4.54 us
  other arithmetic: 0.61 us -> 0.01 us
    all_to_all x0 -> x1, blocking collectives: none -> 13.1 us  [on_device(): terms = lax.all_to_all(terms, ('dp', 'ctx'), 0, 0, tiled=True)]
    ppermute x14 -> x7, starting transfers between devices: 13.4 us -> 5.41 us  [moved(): lax.ppermute(array, axis, [(i, i ^ apart) for i in range(lax.axis_size(ax...]
    ppermute x14 -> x7, waiting for transfers between devices: 11.9 us -> 4.42 us  [moved(): lax.ppermute(array, axis, [(i, i ^ apart) for i in range(lax.axis_size(ax...]
    pallas_call x1, Pallas kernels: 1.76 us -> 0.2 us  [on_device(): pl.pallas_call(pack_kernel, out_shape=jax.ShapeDtypeStruct((PACK, HDIM),...]
    pallas_call x1, Pallas kernels: 1.87 us -> 0.82 us  [on_device(): pl.pallas_call(functools.partial(last_kernel, slots), out_shape=[jax.Shap...]
    add x3 -> x0, other arithmetic: 0.61 us -> none  [the longest x1 0.6 us: on_device(): sinks = sinks + arrived[0][-1] + (arrived[1][-1] + arrived[2][-1])]
    squeeze x2 -> x0, local copies, waits for them, and re-layouts: 0.52 us -> none  [the longest x1 0.51 us: on_device(): return (dq, dk, dv, sinks[0, :HEADS])]
    pallas_call x1, Pallas kernels: 4.36 us -> 3.86 us  [on_device(): pl.pallas_call(functools.partial(main_kernel, slots), out_shape=[jax.Shap...]
  transfers between devices with their start and end apart: 14 -> 7, of which waited for: 8 -> 2; matrix products, arithmetic and copies ran while one was open for 3% -> 0% of each run, Pallas kernels for 4% -> 1%
where the time goes in v2:
time: 34.6 us; the launch traced here: 34.3 us
  blocking collectives  13.1 us (38%)
  starting transfers between devices  5.41 us (16%)
  Pallas kernels  4.89 us (14%)
  local copies, waits for them, and re-layouts  4.54 us (13%)
  waiting for transfers between devices  4.42 us (13%)
  between operations  2.03 us (6%)
    all_to_all x1, blocking collectives, on_device(): terms = lax.all_to_all(terms, ('dp', 'ctx'), 0, 0, tiled=True)  13.1 us
    ppermute x7, starting transfers between devices, moved(): lax.ppermute(array, axis, [(i, i ^ apart) for i in range(lax.axis_size(ax...  5.41 us
    unnamed x20, local copies, waits for them, and re-layouts  4.53 us
    ppermute x7, waiting for transfers between devices, moved(): lax.ppermute(array, axis, [(i, i ^ apart) for i in range(lax.axis_size(ax...  4.42 us
    pallas_call x1, Pallas kernels, on_device(): pl.pallas_call(functools.partial(main_kernel, slots), out_shape=[jax.Shap...  3.86 us
    pallas_call x1, Pallas kernels, on_device(): pl.pallas_call(functools.partial(last_kernel, slots), out_shape=[jax.Shap...  0.82 us
  transfers between devices with their start and end apart: 7, of which 2 were waited for; matrix products, arithmetic and copies ran while one was open for 0% of the time, Pallas kernels for 1%

profile of v2, /device:TPU:0, one launch (start us, length us, event | category | flops | bytes accessed | tf_op | source)
XLA Modules:
  0.0 34.3 jit_solution(12785778021928914571)
XLA Ops:
  0.6 0.5 %collective-permute-start = (bf16[1,128,512]{2,1,0:T(8,128)(2,1)}, bf16[1,128,512]{2,1,0:T(8,128)(2,1)S(1)}, u32[]{:S(2)}, u32[]{:S(2)}) collective-permute-start(bf16[1,128,512]{2,1,0:T(8,128)(2,1)} %keys_ref.3), channel_id=1, source_target_pairs={{0,1},{1,0},{2,3},{3,2},{4,5},{5,4},{6,7},{7,6},{8,9},{9,8},{10,11... | collective-permute-start | bytes 393224 | tf_op jit(solution)/shard_map/ppermute | solution.py:31
  1.2 0.1 collective-permute-start.1
  1.9 0.0 copy-start.6
  2.5 0.0 copy-done.6
  2.6 0.0 copy-start
  2.6 0.9 %copy-done = bf16[1,128,512]{2,1,0:T(8,128)(2,1)S(1)} copy-done((bf16[1,128,512]{2,1,0:T(8,128)(2,1)S(1)}, bf16[1,128,512]{2,1,0:T(8,128)(2,1)}, u32[]{:S(2)}) %copy-start) | copy-done | bytes 131096
  3.5 0.0 copy-start.2
  3.5 0.9 %copy-done.2 = bf16[1,128,512]{2,1,0:T(8,128)(2,1)S(1)} copy-done((bf16[1,128,512]{2,1,0:T(8,128)(2,1)S(1)}, bf16[1,128,512]{2,1,0:T(8,128)(2,1)}, u32[]{:S(2)}) %copy-start.2) | copy-done | bytes 131096
  4.4 0.0 copy-start.1
  4.4 0.0 copy-start.3
  4.4 0.2 pack_sample.1
  4.6 0.5 %collective-permute-start.2 = (bf16[16,128]{1,0:T(8,128)(2,1)S(1)}, bf16[16,128]{1,0:T(8,128)(2,1)S(1)}, u32[]{:S(2)}, u32[]{:S(2)}) collective-permute-start(bf16[16,128]{1,0:T(8,128)(2,1)S(1)} %pack_sample.1), channel_id=1, source_target_pairs={{0,1},{1,0},{2,3},{3,2},{4,5},{5,4},{6,7},{7,6},{8,9},{9,8},{10,11... | collective-permute-start | bytes 12296 | tf_op jit(solution)/shard_map/ppermute | solution.py:31
  5.0 0.8 %collective-permute-done.2 = bf16[16,128]{1,0:T(8,128)(2,1)S(1)} collective-permute-done((bf16[16,128]{1,0:T(8,128)(2,1)S(1)}, bf16[16,128]{1,0:T(8,128)(2,1)S(1)}, u32[]{:S(2)}, u32[]{:S(2)}) %collective-permute-start.2) | collective-permute-done | bytes 4128 | tf_op jit(solution)/shard_map/ppermute | solution.py:31
  5.9 3.8 %collective-permute-start.5 = (bf16[32,128]{1,0:T(8,128)(2,1)S(1)}, bf16[32,128]{1,0:T(8,128)(2,1)S(1)}, u32[]{:S(2)}, u32[]{:S(2)}) collective-permute-start(bf16[32,128]{1,0:T(8,128)(2,1)S(1)} %pad_maximum_fusion), channel_id=1, source_target_pairs={{0,6},{1,7},{2,4},{3,5},{4,2},{5,3},{6,0},{7,1},{8,14},{9,15},{10,... | collective-permute-start | bytes 24584 | tf_op jit(solution)/shard_map/ppermute | solution.py:31
  9.7 0.5 %collective-permute-start.4 = (bf16[32,128]{1,0:T(8,128)(2,1)S(1)}, bf16[32,128]{1,0:T(8,128)(2,1)S(1)}, u32[]{:S(2)}, u32[]{:S(2)}) collective-permute-start(bf16[32,128]{1,0:T(8,128)(2,1)S(1)} %pad_maximum_fusion), channel_id=1, source_target_pairs={{0,4},{1,5},{2,6},{3,7},{4,0},{5,1},{6,2},{7,3},{8,12},{9,13},{10,... | collective-permute-start | bytes 24584 | tf_op jit(solution)/shard_map/ppermute | solution.py:31
  10.2 0.1 collective-permute-start.3
  10.2 3.6 %collective-permute-done.3 = bf16[32,128]{1,0:T(8,128)(2,1)S(1)} collective-permute-done((bf16[32,128]{1,0:T(8,128)(2,1)S(1)}, bf16[32,128]{1,0:T(8,128)(2,1)S(1)}, u32[]{:S(2)}, u32[]{:S(2)}) %collective-permute-start.3) | collective-permute-done | bytes 8224 | tf_op jit(solution)/shard_map/ppermute | solution.py:31
  13.8 0.0 collective-permute-done.4
  13.8 0.0 collective-permute-done.5
  13.8 0.0 copy-start.7
  13.9 0.0 collective-permute-done.far_keys_ref
  13.9 0.0 collective-permute-done.1.far_values_ref
  13.9 0.0 copy-done.1
  13.9 0.0 copy-done.3
  13.9 0.6 %copy-done.7 = f32[16]{0:T(128)S(1)} copy-done((f32[16]{0:T(128)S(1)}, f32[16]{0:T(128)}, u32[]{:S(2)}) %copy-start.7) | copy-done | bytes 88
  14.5 0.0 copy-start.4
  14.5 1.0 %copy-done.4 = bf16[1,128,2048]{2,1,0:T(8,128)(2,1)S(1)} copy-done((bf16[1,128,2048]{2,1,0:T(8,128)(2,1)S(1)}, bf16[1,128,2048]{2,1,0:T(8,128)(2,1)}, u32[]{:S(2)}) %copy-start.4) | copy-done | bytes 524312
  15.5 0.0 copy-start.5
  15.5 1.0 %copy-done.5 = bf16[1,128,2048]{2,1,0:T(8,128)(2,1)S(1)} copy-done((bf16[1,128,2048]{2,1,0:T(8,128)(2,1)S(1)}, bf16[1,128,2048]{2,1,0:T(8,128)(2,1)}, u32[]{:S(2)}) %copy-start.5) | copy-done | bytes 524312
  16.6 3.9 %attend.1 = (bf16[1,128,2048]{2,1,0:T(8,128)(2,1)}, f32[128,1024]{1,0:T(8,128)S(1)}, bf16[128,1024]{1,0:T(8,128)(2,1)S(1)}, bf16[32,16,128]{2,1,0:T(8,128)(2,1)S(1)}) custom-call(bf16[1,128,2048]{2,1,0:T(8,128)(2,1)S(1)} %copy-done.4, bf16[1,128,2048]{2,1,0:T(8,128)(2,1)S(1)} %copy-done.5, bf16[1,128,512]{2,1,0:T(8,128)(2,1)S(1)} %copy-done.1, ...), custom_call_target="tpu_custom_call" | custom-call | tf_op jit(solution)/shard_map/attend/pallas_call | solution.py:194
  20.5 0.0 collective-permute-start.6
  20.5 13.1 %all_to_all.5.terms_ref = bf16[32,16,128]{2,1,0:T(8,128)(2,1)S(1)} all-to-all(bf16[32,16,128]{2,1,0:T(8,128)(2,1)S(1)} %get-tuple-element.14), channel_id=1, replica_groups=mesh['dp'=4,'ctx'=8] {'dp','ctx'}, dimensions={0} | all-to-all | bytes 262144 | tf_op jit(solution)/shard_map/all_to_all | solution.py:208
  33.5 0.0 collective-permute-done.6.recv_ref
  33.5 0.8 %add_up.1 = (bf16[1,128,512]{2,1,0:T(8,128)(2,1)}, bf16[1,128,512]{2,1,0:T(8,128)(2,1)}, f32[1,16]{1,0:T(1,128)}) custom-call(s32[1,1]{1,0:T(1,128)S(6)} %copy.16.row_ref, f32[128,1024]{1,0:T(8,128)S(1)} %get-tuple-element.12.own_ref, bf16[128,1024]{1,0:T(8,128)(2,1)S(1)} %collective-permute-done.6.recv_ref, bf16[32,16,128]{2,1,0:T(8,128)(2,1)S(1)} %all_to_all.5.terms_ref), custom_call_target="tpu_custom_call" | custom-call | tf_op jit(solution)/shard_map/add_up/pallas_call | solution.py:209
  (6 shorter events, 0.0 us)
Async XLA Ops:
  0.6 13.2 %collective-permute-start = (bf16[1,128,512]{2,1,0:T(8,128)(2,1)}, bf16[1,128,512]{2,1,0:T(8,128)(2,1)S(1)}, u32[]{:S(2)}, u32[]{:S(2)}) collective-permute-start(bf16[1,128,512]{2,1,0:T(8,128)(2,1)} %keys_ref.3), channel_id=1, source_target_pairs={{0,1},{1,0},{2,3},{3,2},{4,5},{5,4},{6,7},{7,6},{8,9},{9,8},{10,11... | collective-permute-start | bytes 393224 | tf_op jit(solution)/shard_map/ppermute | solution.py:31
  1.2 12.7 %collective-permute-start.1 = (bf16[1,128,512]{2,1,0:T(8,128)(2,1)}, bf16[1,128,512]{2,1,0:T(8,128)(2,1)S(1)}, u32[]{:S(2)}, u32[]{:S(2)}) collective-permute-start(bf16[1,128,512]{2,1,0:T(8,128)(2,1)} %values_ref.3), channel_id=1, source_target_pairs={{0,1},{1,0},{2,3},{3,2},{4,5},{5,4},{6,7},{7,6},{8,9},{9,8},{10,11... | collective-permute-start | bytes 393224 | tf_op jit(solution)/shard_map/ppermute | solution.py:31
  1.9 0.7 %copy-start.6 = (s32[1,128]{1,0:T(1,128)S(1)}, s32[1,128]{1,0:T(1,128)}, u32[]{:S(2)}) copy-start(s32[1,128]{1,0:T(1,128)} %rank_ref.1) | copy-start | bytes 1540
  2.6 0.9 %copy-start = (bf16[1,128,512]{2,1,0:T(8,128)(2,1)S(1)}, bf16[1,128,512]{2,1,0:T(8,128)(2,1)}, u32[]{:S(2)}) copy-start(bf16[1,128,512]{2,1,0:T(8,128)(2,1)} %keys_ref.3) | copy-start | bytes 393220
  3.5 0.9 %copy-start.2 = (bf16[1,128,512]{2,1,0:T(8,128)(2,1)S(1)}, bf16[1,128,512]{2,1,0:T(8,128)(2,1)}, u32[]{:S(2)}) copy-start(bf16[1,128,512]{2,1,0:T(8,128)(2,1)} %values_ref.3) | copy-start | bytes 393220
  4.4 9.5 %copy-start.1 = (bf16[1,128,512]{2,1,0:T(8,128)(2,1)S(1)}, bf16[1,128,512]{2,1,0:T(8,128)(2,1)}, u32[]{:S(2)}) copy-start(bf16[1,128,512]{2,1,0:T(8,128)(2,1)} %keys_ref.3) | copy-start | bytes 393220
  4.4 9.5 %copy-start.3 = (bf16[1,128,512]{2,1,0:T(8,128)(2,1)S(1)}, bf16[1,128,512]{2,1,0:T(8,128)(2,1)}, u32[]{:S(2)}) copy-start(bf16[1,128,512]{2,1,0:T(8,128)(2,1)} %values_ref.3) | copy-start | bytes 393220
  4.6 1.3 %collective-permute-start.2 = (bf16[16,128]{1,0:T(8,128)(2,1)S(1)}, bf16[16,128]{1,0:T(8,128)(2,1)S(1)}, u32[]{:S(2)}, u32[]{:S(2)}) collective-permute-start(bf16[16,128]{1,0:T(8,128)(2,1)S(1)} %pack_sample.1), channel_id=1, source_target_pairs={{0,1},{1,0},{2,3},{3,2},{4,5},{5,4},{6,7},{7,6},{8,9},{9,8},{10,11... | collective-permute-start | bytes 12296 | tf_op jit(solution)/shard_map/ppermute | solution.py:31
  5.9 8.0 %collective-permute-start.5 = (bf16[32,128]{1,0:T(8,128)(2,1)S(1)}, bf16[32,128]{1,0:T(8,128)(2,1)S(1)}, u32[]{:S(2)}, u32[]{:S(2)}) collective-permute-start(bf16[32,128]{1,0:T(8,128)(2,1)S(1)} %pad_maximum_fusion), channel_id=1, source_target_pairs={{0,6},{1,7},{2,4},{3,5},{4,2},{5,3},{6,0},{7,1},{8,14},{9,15},{10,... | collective-permute-start | bytes 24584 | tf_op jit(solution)/shard_map/ppermute | solution.py:31
  9.7 4.2 %collective-permute-start.4 = (bf16[32,128]{1,0:T(8,128)(2,1)S(1)}, bf16[32,128]{1,0:T(8,128)(2,1)S(1)}, u32[]{:S(2)}, u32[]{:S(2)}) collective-permute-start(bf16[32,128]{1,0:T(8,128)(2,1)S(1)} %pad_maximum_fusion), channel_id=1, source_target_pairs={{0,4},{1,5},{2,6},{3,7},{4,0},{5,1},{6,2},{7,3},{8,12},{9,13},{10,... | collective-permute-start | bytes 24584 | tf_op jit(solution)/shard_map/ppermute | solution.py:31
  10.2 3.7 %collective-permute-start.3 = (bf16[32,128]{1,0:T(8,128)(2,1)S(1)}, bf16[32,128]{1,0:T(8,128)(2,1)S(1)}, u32[]{:S(2)}, u32[]{:S(2)}) collective-permute-start(bf16[32,128]{1,0:T(8,128)(2,1)S(1)} %pad_maximum_fusion), channel_id=1, source_target_pairs={{0,2},{1,3},{2,0},{3,1},{4,6},{5,7},{6,4},{7,5},{8,10},{9,11},{10,... | collective-permute-start | bytes 24584 | tf_op jit(solution)/shard_map/ppermute | solution.py:31
  13.8 0.7 %copy-start.7 = (f32[16]{0:T(128)S(1)}, f32[16]{0:T(128)}, u32[]{:S(2)}) copy-start(f32[16]{0:T(128)} %param.15) | copy-start | bytes 196
  14.5 1.0 %copy-start.4 = (bf16[1,128,2048]{2,1,0:T(8,128)(2,1)S(1)}, bf16[1,128,2048]{2,1,0:T(8,128)(2,1)}, u32[]{:S(2)}) copy-start(bf16[1,128,2048]{2,1,0:T(8,128)(2,1)} %query_ref.1) | copy-start | bytes 1572868
  15.5 1.0 %copy-start.5 = (bf16[1,128,2048]{2,1,0:T(8,128)(2,1)S(1)}, bf16[1,128,2048]{2,1,0:T(8,128)(2,1)}, u32[]{:S(2)}) copy-start(bf16[1,128,2048]{2,1,0:T(8,128)(2,1)} %grad_ref.1) | copy-start | bytes 1572868
  20.5 13.1 %collective-permute-start.6 = (bf16[128,1024]{1,0:T(8,128)(2,1)S(1)}, bf16[128,1024]{1,0:T(8,128)(2,1)S(1)}, u32[]{:S(2)}, u32[]{:S(2)}) collective-permute-start(bf16[128,1024]{1,0:T(8,128)(2,1)S(1)} %get-tuple-element.13), channel_id=1, source_target_pairs={{0,1},{1,0},{2,3},{3,2},{4,5},{5,4},{6,7},{7,6},{8,9},{9,8},{10,11... | collective-permute-start | bytes 786440 | tf_op jit(solution)/shard_map/ppermute | solution.py:31

commit v3 on v2

v3 whole, which is shorter than its diff:
```python
import functools

import jax
import jax.numpy as jnp
from jax import lax
from jax.experimental import pallas as pl
from jax.experimental.pallas import tpu as pltpu
from jax.sharding import PartitionSpec as P

HEADS = 16
KV_HEADS = 4
HDIM = 128
BUCKET = 128
GROUP = HEADS // KV_HEADS
NEG = -1e30
PACK = 16
COUNT_ROW = 8
MARK_ROW = 9
TOKEN_MARK_ROW = 10
SINK_ROW = 8

f32 = jnp.float32
bf16 = jnp.bfloat16
NN = (((1,), (0,)), ((), ()))
NT = (((1,), (1,)), ((), ()))
TN = (((0,), (0,)), ((), ()))
VMEM = pl.BlockSpec(memory_space=pltpu.VMEM)
SMEM = pl.BlockSpec(memory_space=pltpu.SMEM)
HBM = pl.BlockSpec(memory_space=pltpu.HBM)
LARGE = pltpu.CompilerParams(vmem_limit_bytes=24 * 1024 * 1024)
SMALL = pltpu.CompilerParams(vmem_limit_bytes=6 * 1024 * 1024)


def in_hbm(*arrays):
    return [pltpu.with_memory_space_constraint(array, pltpu.HBM) for array in arrays]


def moved(array, axis, apart):
    return lax.ppermute(array, axis, [(i, i ^ apart) for i in range(lax.axis_size(axis))])


def rounds(size):
    found, base = [], 2
    while base < size:
        found.append([base + 1] if base * 2 >= size else [base + 1, 2 * base + 1, 3 * base + 1])
        base *= 2 if base * 2 >= size else 4
    return found


def slot_order(size):
    order = [0, 1]
    for offsets in rounds(size):
        order = order + [d ^ near for d in offsets for near in order]
    return order


def iota(shape, dim):
    return lax.broadcasted_iota(jnp.int32, shape, dim)


def pack_kernel(
    row_ref, count_ref, rank_hbm, sink_hbm, keys_hbm, values_hbm, query_hbm, grad_hbm,
    kv_ref, qg_ref, out_ref, meta_ref, rank_ref, sink_ref, sems,
):
    wide = keys_hbm.shape[2]
    rows = query_hbm.shape[2]
    copies = [
        pltpu.make_async_copy(from_ref, to_ref, sems.at[i])
        for i, (from_ref, to_ref) in enumerate(
            [
                (keys_hbm.at[0], kv_ref.at[:, :wide]),
                (values_hbm.at[0], kv_ref.at[:, wide:]),
                (rank_hbm, rank_ref),
                (sink_hbm, sink_ref),
                (query_hbm.at[0], qg_ref.at[:, :rows]),
                (grad_hbm.at[0], qg_ref.at[:, rows:]),
            ]
        )
    ]
    for copy in copies:
        copy.start()
    for copy in copies[:4]:
        copy.wait()
    length = kv_ref.shape[0]
    row = row_ref[0, 0]
    pick = (iota((PACK, length), 1) == row).astype(bf16)
    picked = jnp.dot(pick, kv_ref[...], preferred_element_type=f32)
    marks = (rank_ref[...] >= BUCKET).astype(f32)
    mark = jnp.sum(jnp.where(iota((1, length), 1) == row, marks, 0.0), axis=1, keepdims=True)
    at = iota((PACK, HDIM), 0)
    tile = jnp.zeros((PACK, HDIM), f32)
    for j in range(2 * KV_HEADS):
        tile = jnp.where(at == j, picked[:, j * HDIM : (j + 1) * HDIM], tile)
    tile = jnp.where(at == COUNT_ROW, count_ref[0, 0].astype(f32), tile)
    tile = jnp.where(at == MARK_ROW, mark, tile)
    tile = jnp.where(at == TOKEN_MARK_ROW, marks, tile)
    out_ref[...] = tile.astype(bf16)
    at = iota((8, length), 0)
    meta = jnp.where(at == 0, row.astype(f32), 0.0)
    for h in range(HEADS):
        meta = jnp.where((at == 1) & (iota((8, length), 1) == h), sink_ref[:, h : h + 1], meta)
    meta_ref[...] = meta
    for copy in copies[4:]:
        copy.wait()


def columns(j):
    return slice(j * HDIM, (j + 1) * HDIM)


def stacked(qg_ref, base, j):
    heads = [base + j * GROUP + g for g in range(GROUP)]
    return jnp.concatenate([qg_ref[:, columns(h)] for h in heads], 0)


def score_kernel(qg_ref, kv_ref, own_tile_ref, tile_ref, weight_ref, up_ref, stats_ref):
    length = kv_ref.shape[0]
    scale = HDIM**-0.5
    own_marks = own_tile_ref[...].astype(f32)[TOKEN_MARK_ROW : TOKEN_MARK_ROW + 1]
    marks = tile_ref[...].astype(f32)[TOKEN_MARK_ROW : TOKEN_MARK_ROW + 1]
    column = jnp.transpose(jnp.broadcast_to(marks, (length, length)))
    bias = jnp.where(column == own_marks, 0.0, NEG)
    bias = jnp.concatenate([bias] * GROUP, 1)
    for j in range(KV_HEADS):
        at = slice(j * GROUP * HDIM, (j + 1) * GROUP * HDIM)
        score = lax.dot_general(kv_ref[:, columns(j)], stacked(qg_ref, 0, j), NT, preferred_element_type=f32)
        score = score * scale + bias
        top = jnp.max(score, axis=0, keepdims=True)
        weight = jnp.exp(score - top)
        weight_ref[:, at] = weight
        stats_ref[0:1, at] = top
        stats_ref[1:2, at] = jnp.sum(weight, axis=0, keepdims=True)
        up_ref[:, at] = lax.dot_general(
            kv_ref[:, columns(KV_HEADS + j)], stacked(qg_ref, HEADS, j), NT, preferred_element_type=f32
        )


def main_kernel(
    slots, qg_ref, own_weight_ref, own_up_ref, own_stats_ref, far_weight_ref, far_up_ref, far_stats_ref,
    kv_ref, far_ref, packs_ref, meta_ref, dq_hbm, own_grad_ref, far_grad_ref, out_ref, dq_ref, sems,
):
    length = kv_ref.shape[0]
    rows = HEADS * HDIM
    group = GROUP * HDIM
    padded = -(-slots // 16) * 16
    order = slot_order(slots)
    scale = HDIM**-0.5
    packs = packs_ref[...]
    at = iota((padded, slots * PACK), 1)
    slot = iota((padded, slots * PACK), 0)
    pick = jnp.concatenate([(at == slot * PACK + row).astype(bf16) for row in range(MARK_ROW + 1)], 0)
    picked = jnp.dot(pick, packs, preferred_element_type=f32)
    chosen = [picked[i * padded : (i + 1) * padded] for i in range(MARK_ROW + 1)]
    slot_keys = [part.astype(bf16) for part in chosen[:KV_HEADS]]
    slot_values = [part.astype(bf16) for part in chosen[KV_HEADS : 2 * KV_HEADS]]
    own_marks = packs[:PACK].astype(f32)[TOKEN_MARK_ROW : TOKEN_MARK_ROW + 1]
    slot_at = iota((padded, length), 0)
    bias = jnp.log(jnp.maximum(chosen[COUNT_ROW], 1.0))
    same = (slot_at < 2) & (chosen[MARK_ROW] == own_marks)
    bias = jnp.where(same | (slot_at >= slots), NEG, bias)
    sink = jnp.concatenate(
        [jnp.broadcast_to(meta_ref[1:2, h : h + 1], (1, length)) for h in range(HEADS)], 1
    )
    query = [stacked(qg_ref, 0, j) for j in range(KV_HEADS)]
    grad = [stacked(qg_ref, HEADS, j) for j in range(KV_HEADS)]
    score = jnp.concatenate(
        [lax.dot_general(slot_keys[j], query[j], NT, preferred_element_type=f32) for j in range(KV_HEADS)], 1
    )
    slot_up = jnp.concatenate(
        [lax.dot_general(slot_values[j], grad[j], NT, preferred_element_type=f32) for j in range(KV_HEADS)], 1
    )
    score = score * scale + jnp.concatenate([bias] * HEADS, 1)
    own_top, far_top = own_stats_ref[0:1], far_stats_ref[0:1]
    top = jnp.maximum(jnp.maximum(own_top, far_top), jnp.maximum(jnp.max(score, axis=0, keepdims=True), sink))
    slot_weight = jnp.exp(score - top)
    sink_weight = jnp.exp(sink - top)
    own_scale, far_scale = jnp.exp(own_top - top), jnp.exp(far_top - top)
    total = own_scale * own_stats_ref[1:2] + far_scale * far_stats_ref[1:2]
    total = total + (jnp.sum(slot_weight, axis=0, keepdims=True) + sink_weight)
    inverse = 1.0 / total
    own_scale, far_scale = own_scale * inverse, far_scale * inverse
    slot_prob = slot_weight * inverse
    sink_prob = sink_weight * inverse
    slot_delta = jnp.sum(slot_prob * slot_up, axis=0, keepdims=True)
    sinks = jnp.zeros((1, HDIM), f32)
    lane = iota((1, HDIM), 1)
    sent = []
    halves = []
    signals = []
    for j in range(KV_HEADS):
        at = slice(j * group, (j + 1) * group)
        own_prob = own_weight_ref[:, at] * own_scale[:, at]
        far_prob = far_weight_ref[:, at] * far_scale[:, at]
        own_up, far_up = own_up_ref[:, at], far_up_ref[:, at]
        delta = jnp.sum(own_prob * own_up + far_prob * far_up, axis=0, keepdims=True) + slot_delta[:, at]
        ds = jnp.concatenate(
            [
                (own_prob * (own_up - delta)).astype(bf16),
                (far_prob * (far_up - delta)).astype(bf16),
                (slot_prob[:, at] * (slot_up[:, at] - delta)).astype(bf16),
            ],
            0,
        )
        half = jnp.concatenate(
            [own_prob.astype(bf16), far_prob.astype(bf16), slot_prob[:, at].astype(bf16)], 0
        )
        sink_row = sink_prob[:, at] * delta
        for g in range(GROUP):
            part = jnp.sum(sink_row[:, g * length : (g + 1) * length], axis=1, keepdims=True)
            sinks = sinks - jnp.where(lane == j * GROUP + g, part, 0.0)
        keys = jnp.concatenate([kv_ref[:, columns(j)], far_ref[:, columns(j)], slot_keys[j]], 0)
        dq = (lax.dot_general(keys, ds, TN, preferred_element_type=f32) * scale).astype(bf16)
        for g in range(GROUP):
            dq_ref[:, columns(j * GROUP + g)] = jnp.transpose(dq[:, g * length : (g + 1) * length])
        copy = pltpu.make_async_copy(
            dq_ref.at[:, pl.ds(j * group, group)], dq_hbm.at[0, :, pl.ds(j * group, group)], sems.at[j]
        )
        copy.start()
        sent.append(copy)
        halves.append(half)
        signals.append(ds)
    high = sinks.astype(bf16).astype(f32)
    middle = (sinks - high).astype(bf16).astype(f32)
    low = sinks - high - middle
    at = iota((PACK, HDIM), 0)
    tile = jnp.zeros((PACK, HDIM), f32)
    for i, part in enumerate((high, middle, low)):
        tile = jnp.where(at == SINK_ROW + i, part, tile)
    out_ref[...] = jnp.broadcast_to(tile.astype(bf16)[None], out_ref.shape)
    tiles = [tile] * slots
    for j in range(KV_HEADS):
        dk = lax.dot_general(signals[j], query[j], NN, preferred_element_type=f32) * scale
        dv = lax.dot_general(halves[j], grad[j], NN, preferred_element_type=f32)
        for to, part in ((j, dk), (KV_HEADS + j, dv)):
            own_grad_ref[:, columns(to)] = part[:length]
            far_grad_ref[:, columns(to)] = part[length : 2 * length].astype(bf16)
            for slot in range(slots):
                row = part[2 * length + slot : 2 * length + slot + 1]
                tiles[slot] = jnp.where(at == to, row, tiles[slot])
    first = lax.axis_index("dp") * slots
    for slot in range(slots):
        out_ref[first + (lax.axis_index("ctx") ^ order[slot])] = tiles[slot].astype(bf16)
    for copy in sent:
        copy.wait()


def last_kernel(slots, meta_ref, own_ref, recv_ref, terms_ref, dk_ref, dv_ref, sink_ref):
    length = own_ref.shape[0]
    parts = jnp.sum(terms_ref[...].astype(f32), axis=0)
    sink = parts[SINK_ROW : SINK_ROW + 1] + parts[SINK_ROW + 1 : SINK_ROW + 2]
    sink_ref[...] = (sink + parts[SINK_ROW + 2 : SINK_ROW + 3])[:, :HEADS]
    first = lax.axis_index("dp") * slots
    slot = jnp.sum(terms_ref[pl.ds(first, slots)].astype(f32), axis=0)
    mine = iota((length, HDIM), 0).astype(f32) == meta_ref[0:1]
    for out_ref, base in ((dk_ref, 0), (dv_ref, KV_HEADS)):
        for j in range(KV_HEADS):
            at = slice((base + j) * HDIM, (base + j + 1) * HDIM)
            total = own_ref[:, at] + recv_ref[:, at].astype(f32)
            total = total + jnp.where(mine, slot[base + j : base + j + 1, :], 0.0)
            out_ref[0, :, j * HDIM : (j + 1) * HDIM] = total.astype(bf16)


def on_device(
    query_rows, key_rows, value_rows, grad_rows, bucket_rank, sample_rows, sample_count, sink_logit
):
    length = query_rows.shape[1]
    wide = KV_HEADS * HDIM
    slots = lax.axis_size("ctx")
    rows = HEADS * HDIM
    kv, qg, tile, meta = pl.pallas_call(
        pack_kernel,
        out_shape=[
            jax.ShapeDtypeStruct((length, 2 * wide), bf16),
            jax.ShapeDtypeStruct((length, 2 * rows), bf16),
            jax.ShapeDtypeStruct((PACK, HDIM), bf16),
            jax.ShapeDtypeStruct((8, length), f32),
        ],
        in_specs=[SMEM] * 2 + [HBM] * 6,
        out_specs=[VMEM] * 4,
        scratch_shapes=[
            pltpu.VMEM((1, length), jnp.int32),
            pltpu.VMEM((1, HEADS), f32),
            pltpu.SemaphoreType.DMA((6,)),
        ],
        compiler_params=SMALL,
        name="pack_sample",
    )(
        sample_rows,
        sample_count,
        *in_hbm(bucket_rank, sink_logit[None], key_rows, value_rows, query_rows, grad_rows),
    )

    def scores(keys_values, keys_tile):
        return pl.pallas_call(
            score_kernel,
            out_shape=[
                jax.ShapeDtypeStruct((length, rows), f32),
                jax.ShapeDtypeStruct((length, rows), f32),
                jax.ShapeDtypeStruct((8, rows), f32),
            ],
            in_specs=[VMEM] * 4,
            out_specs=[VMEM] * 3,
            compiler_params=LARGE,
            cost_estimate=pl.CostEstimate(
                flops=4 * length * length * rows, transcendentals=length * rows, bytes_accessed=10 * length * rows
            ),
            name="scores",
        )(qg, keys_values, tile, keys_tile)

    far_tile = moved(tile, "ctx", 1)
    far_kv = moved(kv, "ctx", 1)
    own_weight, own_up, own_stats = scores(kv, tile)
    far_weight, far_up, far_stats = scores(far_kv, far_tile)
    packs = jnp.concatenate([tile, far_tile], 0)
    for offsets in rounds(slots):
        packs = jnp.concatenate([packs] + [moved(packs, "ctx", d) for d in offsets], 0)
    devices = slots * lax.axis_size("dp")
    dq, own, far, terms = pl.pallas_call(
        functools.partial(main_kernel, slots),
        out_shape=[
            jax.ShapeDtypeStruct((1, length, rows), bf16),
            jax.ShapeDtypeStruct((length, 2 * wide), f32),
            jax.ShapeDtypeStruct((length, 2 * wide), bf16),
            jax.ShapeDtypeStruct((devices, PACK, HDIM), bf16),
        ],
        in_specs=[VMEM] * 11,
        out_specs=[HBM] + [VMEM] * 3,
        scratch_shapes=[pltpu.VMEM((length, rows), bf16), pltpu.SemaphoreType.DMA((KV_HEADS,))],
        compiler_params=LARGE,
        name="gradients",
    )(qg, own_weight, own_up, own_stats, far_weight, far_up, far_stats, kv, far_kv, packs, meta)
    recv = moved(far, "ctx", 1)
    terms = lax.all_to_all(terms, ("dp", "ctx"), 0, 0, tiled=True)
    dk, dv, sink_grad = pl.pallas_call(
        functools.partial(last_kernel, slots),
        out_shape=[jax.ShapeDtypeStruct((1, length, wide), bf16)] * 2
        + [jax.ShapeDtypeStruct((1, HEADS), f32)],
        in_specs=[VMEM] * 4,
        out_specs=[VMEM] * 3,
        compiler_params=SMALL,
        name="add_up",
    )(meta, own, recv, terms)
    return dq, dk, dv, sink_grad[0]


def solution(mesh):
    return jax.shard_map(
        on_device,
        mesh=mesh,
        in_specs=(
            P("dp", "ctx", None),
            P("dp", "ctx", None),
            P("dp", "ctx", None),
            P("dp", "ctx", None),
            P("dp", "ctx"),
            P("dp", "ctx"),
            P("dp", "ctx"),
            P(),
        ),
        out_specs=(P("dp", "ctx", None), P("dp", "ctx", None), P("dp", "ctx", None), P()),
        check_vma=False,
    )
```

time: 34.6 us -> 29.9 us (0.86)
  local copies, waits for them, and re-layouts: 4.54 us -> 0.03 us
  Pallas kernels: 4.89 us -> 6.03 us
  waiting for transfers between devices: 4.42 us -> 3.78 us
  starting transfers between devices: 5.41 us -> 4.99 us
    unnamed x20 -> x3, local copies, waits for them, and re-layouts: 4.53 us -> 0.02 us
    pallas_call x1 -> x3, Pallas kernels: 0.2 us -> 2.58 us  [the longest x1 1.42 us: on_device(): pl.pallas_call(pack_kernel, out_shape=[jax.ShapeDtypeStruct((length, 2 *...]
    pallas_call x1, Pallas kernels: 3.86 us -> 2.68 us  [on_device(): pl.pallas_call(functools.partial(main_kernel, slots), out_shape=[jax.Shap...]
    ppermute x7 -> x6, waiting for transfers between devices: 4.42 us -> 3.78 us  [moved(): lax.ppermute(array, axis, [(i, i ^ apart) for i in range(lax.axis_size(ax...]
    ppermute x7 -> x6, starting transfers between devices: 5.41 us -> 4.99 us  [moved(): lax.ppermute(array, axis, [(i, i ^ apart) for i in range(lax.axis_size(ax...]
  transfers between devices with their start and end apart: 7 -> 6, of which waited for: 2 -> 2; matrix products, arithmetic and copies ran while one was open for 0% -> 0% of each run, Pallas kernels for 1% -> 2%
where the time goes in v3:
time: 29.9 us; the launch traced here: 29.7 us
  blocking collectives  12.9 us (43%)
  Pallas kernels  6.03 us (20%)
  starting transfers between devices  4.99 us (17%)
  waiting for transfers between devices  3.78 us (13%)
  between operations  1.96 us (7%)
    all_to_all x1, blocking collectives, on_device(): terms = lax.all_to_all(terms, ('dp', 'ctx'), 0, 0, tiled=True)  12.9 us
    ppermute x6, starting transfers between devices, moved(): lax.ppermute(array, axis, [(i, i ^ apart) for i in range(lax.axis_size(ax...  4.99 us
    ppermute x6, waiting for transfers between devices, moved(): lax.ppermute(array, axis, [(i, i ^ apart) for i in range(lax.axis_size(ax...  3.78 us
    pallas_call x1, Pallas kernels, on_device(): pl.pallas_call(functools.partial(main_kernel, slots), out_shape=[jax.Shap...  2.68 us
    pallas_call x1, Pallas kernels, on_device(): pl.pallas_call(pack_kernel, out_shape=[jax.ShapeDtypeStruct((length, 2 *...  1.42 us
    pallas_call x2, Pallas kernels, scores(): pl.pallas_call(score_kernel, out_shape=[jax.ShapeDtypeStruct((length, row...  1.16 us
    pallas_call x1, Pallas kernels, on_device(): pl.pallas_call(functools.partial(last_kernel, slots), out_shape=[jax.Shap...  0.77 us
  transfers between devices with their start and end apart: 6, of which 2 were waited for; matrix products, arithmetic and copies ran while one was open for 0% of the time, Pallas kernels for 2%

profile of v3, /device:TPU:0, one launch (start us, length us, event | category | flops | bytes accessed | tf_op | source)
XLA Modules:
  0.0 29.7 jit_solution(3339491982057184269)
XLA Ops:
  1.9 1.4 %pack_sample.1 = (bf16[128,1024]{1,0:T(8,128)(2,1)S(1)}, bf16[128,4096]{1,0:T(8,128)(2,1)S(1)}, bf16[16,128]{1,0:T(8,128)(2,1)S(1)}, f32[8,128]{1,0:T(8,128)S(1)}) custom-call(s32[1,1]{1,0:T(1,128)S(6)} %copy.17.row_ref, s32[1,1]{1,0:T(1,128)S(6)} %copy.18.count_ref, s32[1,128]{1,0:T(1,128)} %rank_hbm.1, f32[1,16]{1,0:T(1,128)} %bitcast.2, ...), custom_call_target="tpu_custom_call" | custom-call | tf_op jit(solution)/shard_map/pack_sample/pallas_call | solution.py:270
  3.4 0.5 %collective-permute-start.1 = (bf16[16,128]{1,0:T(8,128)(2,1)S(1)}, bf16[16,128]{1,0:T(8,128)(2,1)S(1)}, u32[]{:S(2)}, u32[]{:S(2)}) collective-permute-start(bf16[16,128]{1,0:T(8,128)(2,1)S(1)} %get-tuple-element.23.own_tile_ref.tile_ref), channel_id=1, source_target_pairs={{0,1},{1,0},{2,3},{3,2},{4,5},{5,4},{6,7},{7,6},{8,9},{9,8},{10,11... | collective-permute-start | bytes 12296 | tf_op jit(solution)/shard_map/ppermute | solution.py:39
  3.9 0.1 collective-permute-start
  4.0 0.7 %collective-permute-done.1.tile_ref = bf16[16,128]{1,0:T(8,128)(2,1)S(1)} collective-permute-done((bf16[16,128]{1,0:T(8,128)(2,1)S(1)}, bf16[16,128]{1,0:T(8,128)(2,1)S(1)}, u32[]{:S(2)}, u32[]{:S(2)}) %collective-permute-start.1) | collective-permute-done | bytes 4128 | tf_op jit(solution)/shard_map/ppermute | solution.py:39
  4.7 2.6 %collective-permute-start.2 = (bf16[32,128]{1,0:T(8,128)(2,1)S(1)}, bf16[32,128]{1,0:T(8,128)(2,1)S(1)}, u32[]{:S(2)}, u32[]{:S(2)}) collective-permute-start(bf16[32,128]{1,0:T(8,128)(2,1)S(1)} %get-tuple-element.38), channel_id=1, source_target_pairs={{0,3},{1,2},{2,1},{3,0},{4,7},{5,6},{6,5},{7,4},{8,11},{9,10},{10,... | collective-permute-start | bytes 24584 | tf_op jit(solution)/shard_map/ppermute | solution.py:39
  7.3 0.6 %scores.2 = (f32[128,2048]{1,0:T(8,128)S(1)}, f32[128,2048]{1,0:T(8,128)S(1)}, f32[8,2048]{1,0:T(8,128)S(1)}) custom-call(bf16[128,4096]{1,0:T(8,128)(2,1)S(1)} %get-tuple-element.21.qg_ref, bf16[128,1024]{1,0:T(8,128)(2,1)S(1)} %get-tuple-element.22.kv_ref, bf16[16,128]{1,0:T(8,128)(2,1)S(1)} %get-tuple-element.23.own_tile_ref.tile_ref, ...), custom_call_target="tpu_custom_call" | custom-call | flops 134217728 | bytes 2621440 | tf_op jit(solution)/shard_map/scores/pallas_call | solution.py:294
  7.9 1.5 %collective-permute-start.4 = (bf16[32,128]{1,0:T(8,128)(2,1)S(1)}, bf16[32,128]{1,0:T(8,128)(2,1)S(1)}, u32[]{:S(2)}, u32[]{:S(2)}) collective-permute-start(bf16[32,128]{1,0:T(8,128)(2,1)S(1)} %get-tuple-element.38), channel_id=1, source_target_pairs={{0,7},{1,6},{2,5},{3,4},{4,3},{5,2},{6,1},{7,0},{8,15},{9,14},{10,... | collective-permute-start | bytes 24584 | tf_op jit(solution)/shard_map/ppermute | solution.py:39
  9.4 0.1 collective-permute-start.3
  9.5 0.0 collective-permute-done.2
  9.5 3.0 %collective-permute-done.3 = bf16[32,128]{1,0:T(8,128)(2,1)S(1)} collective-permute-done((bf16[32,128]{1,0:T(8,128)(2,1)S(1)}, bf16[32,128]{1,0:T(8,128)(2,1)S(1)}, u32[]{:S(2)}, u32[]{:S(2)}) %collective-permute-start.3) | collective-permute-done | bytes 8224 | tf_op jit(solution)/shard_map/ppermute | solution.py:39
  12.5 0.0 collective-permute-done.4
  12.6 0.0 collective-permute-done.kv_ref.far_ref
  12.6 0.6 %scores.3 = (f32[128,2048]{1,0:T(8,128)S(1)}, f32[128,2048]{1,0:T(8,128)S(1)}, f32[8,2048]{1,0:T(8,128)S(1)}) custom-call(bf16[128,4096]{1,0:T(8,128)(2,1)S(1)} %get-tuple-element.21.qg_ref, bf16[128,1024]{1,0:T(8,128)(2,1)S(1)} %collective-permute-done.kv_ref.far_ref, bf16[16,128]{1,0:T(8,128)(2,1)S(1)} %get-tuple-element.23.own_tile_ref.tile_ref, ...), custom_call_target="tpu_custom_call" | custom-call | flops 134217728 | bytes 2621440 | tf_op jit(solution)/shard_map/scores/pallas_call | solution.py:294
  13.1 2.7 %gradients.1 = (bf16[1,128,2048]{2,1,0:T(8,128)(2,1)}, f32[128,1024]{1,0:T(8,128)S(1)}, bf16[128,1024]{1,0:T(8,128)(2,1)S(1)}, bf16[32,16,128]{2,1,0:T(8,128)(2,1)S(1)}) custom-call(bf16[128,4096]{1,0:T(8,128)(2,1)S(1)} %get-tuple-element.21.qg_ref, f32[128,2048]{1,0:T(8,128)S(1)} %get-tuple-element.24.own_weight_ref, ...), custom_call_target="tpu_custom_call" | custom-call | tf_op jit(solution)/shard_map/gradients/pallas_call | solution.py:318
  15.8 0.2 collective-permute-start.5
  16.0 12.9 %all_to_all.5.terms_ref = bf16[32,16,128]{2,1,0:T(8,128)(2,1)S(1)} all-to-all(bf16[32,16,128]{2,1,0:T(8,128)(2,1)S(1)} %get-tuple-element.34), channel_id=1, replica_groups=mesh['dp'=4,'ctx'=8] {'dp','ctx'}, dimensions={0} | all-to-all | bytes 262144 | tf_op jit(solution)/shard_map/all_to_all | solution.py:333
  28.9 0.0 collective-permute-done.5.recv_ref
  28.9 0.8 %add_up.1 = (bf16[1,128,512]{2,1,0:T(8,128)(2,1)}, bf16[1,128,512]{2,1,0:T(8,128)(2,1)}, f32[1,16]{1,0:T(1,128)}) custom-call(f32[8,128]{1,0:T(8,128)S(1)} %get-tuple-element.30.meta_ref, f32[128,1024]{1,0:T(8,128)S(1)} %get-tuple-element.32.own_ref, bf16[128,1024]{1,0:T(8,128)(2,1)S(1)} %collective-permute-done.5.recv_ref, ...), custom_call_target="tpu_custom_call" | custom-call | tf_op jit(solution)/shard_map/add_up/pallas_call | solution.py:334
  (5 shorter events, 0.0 us)
Async XLA Ops:
  3.4 1.3 %collective-permute-start.1 = (bf16[16,128]{1,0:T(8,128)(2,1)S(1)}, bf16[16,128]{1,0:T(8,128)(2,1)S(1)}, u32[]{:S(2)}, u32[]{:S(2)}) collective-permute-start(bf16[16,128]{1,0:T(8,128)(2,1)S(1)} %get-tuple-element.23.own_tile_ref.tile_ref), channel_id=1, source_target_pairs={{0,1},{1,0},{2,3},{3,2},{4,5},{5,4},{6,7},{7,6},{8,9},{9,8},{10,11... | collective-permute-start | bytes 12296 | tf_op jit(solution)/shard_map/ppermute | solution.py:39
  3.9 8.7 %collective-permute-start = (bf16[128,1024]{1,0:T(8,128)(2,1)S(1)}, bf16[128,1024]{1,0:T(8,128)(2,1)S(1)}, u32[]{:S(2)}, u32[]{:S(2)}) collective-permute-start(bf16[128,1024]{1,0:T(8,128)(2,1)S(1)} %get-tuple-element.22.kv_ref), channel_id=1, source_target_pairs={{0,1},{1,0},{2,3},{3,2},{4,5},{5,4},{6,7},{7,6},{8,9},{9,8},{10,11... | collective-permute-start | bytes 786440 | tf_op jit(solution)/shard_map/ppermute | solution.py:39
  4.7 4.8 %collective-permute-start.2 = (bf16[32,128]{1,0:T(8,128)(2,1)S(1)}, bf16[32,128]{1,0:T(8,128)(2,1)S(1)}, u32[]{:S(2)}, u32[]{:S(2)}) collective-permute-start(bf16[32,128]{1,0:T(8,128)(2,1)S(1)} %get-tuple-element.38), channel_id=1, source_target_pairs={{0,3},{1,2},{2,1},{3,0},{4,7},{5,6},{6,5},{7,4},{8,11},{9,10},{10,... | collective-permute-start | bytes 24584 | tf_op jit(solution)/shard_map/ppermute | solution.py:39
  7.9 4.7 %collective-permute-start.4 = (bf16[32,128]{1,0:T(8,128)(2,1)S(1)}, bf16[32,128]{1,0:T(8,128)(2,1)S(1)}, u32[]{:S(2)}, u32[]{:S(2)}) collective-permute-start(bf16[32,128]{1,0:T(8,128)(2,1)S(1)} %get-tuple-element.38), channel_id=1, source_target_pairs={{0,7},{1,6},{2,5},{3,4},{4,3},{5,2},{6,1},{7,0},{8,15},{9,14},{10,... | collective-permute-start | bytes 24584 | tf_op jit(solution)/shard_map/ppermute | solution.py:39
  9.4 3.1 %collective-permute-start.3 = (bf16[32,128]{1,0:T(8,128)(2,1)S(1)}, bf16[32,128]{1,0:T(8,128)(2,1)S(1)}, u32[]{:S(2)}, u32[]{:S(2)}) collective-permute-start(bf16[32,128]{1,0:T(8,128)(2,1)S(1)} %get-tuple-element.38), channel_id=1, source_target_pairs={{0,5},{1,4},{2,7},{3,6},{4,1},{5,0},{6,3},{7,2},{8,13},{9,12},{10,... | collective-permute-start | bytes 24584 | tf_op jit(solution)/shard_map/ppermute | solution.py:39
  15.8 13.1 %collective-permute-start.5 = (bf16[128,1024]{1,0:T(8,128)(2,1)S(1)}, bf16[128,1024]{1,0:T(8,128)(2,1)S(1)}, u32[]{:S(2)}, u32[]{:S(2)}) collective-permute-start(bf16[128,1024]{1,0:T(8,128)(2,1)S(1)} %get-tuple-element.33), channel_id=1, source_target_pairs={{0,1},{1,0},{2,3},{3,2},{4,5},{5,4},{6,7},{7,6},{8,9},{9,8},{10,11... | collective-permute-start | bytes 786440 | tf_op jit(solution)/shard_map/ppermute | solution.py:39

commit v4 on v3

v4 whole, which is shorter than its diff:
```python
import functools

import jax
import jax.numpy as jnp
from jax import lax
from jax.experimental import pallas as pl
from jax.experimental.pallas import tpu as pltpu
from jax.sharding import PartitionSpec as P

HEADS = 16
KV_HEADS = 4
HDIM = 128
BUCKET = 128
GROUP = HEADS // KV_HEADS
NEG = -1e30
PACK = 16
COUNT_ROW = 8
MARK_ROW = 9
TOKEN_MARK_ROW = 10

f32 = jnp.float32
bf16 = jnp.bfloat16
NN = (((1,), (0,)), ((), ()))
NT = (((1,), (1,)), ((), ()))
TN = (((0,), (0,)), ((), ()))
VMEM = pl.BlockSpec(memory_space=pltpu.VMEM)
SMEM = pl.BlockSpec(memory_space=pltpu.SMEM)
HBM = pl.BlockSpec(memory_space=pltpu.HBM)
LARGE = pltpu.CompilerParams(vmem_limit_bytes=24 * 1024 * 1024)
SMALL = pltpu.CompilerParams(vmem_limit_bytes=6 * 1024 * 1024)


def in_hbm(*arrays):
    return [pltpu.with_memory_space_constraint(array, pltpu.HBM) for array in arrays]


def moved(array, axis, apart):
    return lax.ppermute(array, axis, [(i, i ^ apart) for i in range(lax.axis_size(axis))])


def rounds(size):
    found, base = [], 2
    while base < size:
        found.append([base + 1] if base * 2 >= size else [base + 1, 2 * base + 1, 3 * base + 1])
        base *= 2 if base * 2 >= size else 4
    return found


def slot_order(size):
    order = [0, 1]
    for offsets in rounds(size):
        order = order + [d ^ near for d in offsets for near in order]
    return order


def iota(shape, dim):
    return lax.broadcasted_iota(jnp.int32, shape, dim)


def pack_kernel(
    row_ref, count_ref, rank_hbm, sink_hbm, keys_hbm, values_hbm,
    kv_ref, out_ref, meta_ref, rank_ref, sink_ref, sems,
):
    wide = keys_hbm.shape[2]
    copies = [
        pltpu.make_async_copy(from_ref, to_ref, sems.at[i])
        for i, (from_ref, to_ref) in enumerate(
            [
                (keys_hbm.at[0], kv_ref.at[:, :wide]),
                (values_hbm.at[0], kv_ref.at[:, wide:]),
                (rank_hbm, rank_ref),
                (sink_hbm, sink_ref),
            ]
        )
    ]
    for copy in copies:
        copy.start()
    for copy in copies:
        copy.wait()
    length = kv_ref.shape[0]
    row = row_ref[0, 0]
    pick = (iota((PACK, length), 1) == row).astype(bf16)
    picked = jnp.dot(pick, kv_ref[...], preferred_element_type=f32)
    marks = (rank_ref[...] >= BUCKET).astype(f32)
    mark = jnp.sum(jnp.where(iota((1, length), 1) == row, marks, 0.0), axis=1, keepdims=True)
    at = iota((PACK, HDIM), 0)
    tile = jnp.zeros((PACK, HDIM), f32)
    for j in range(2 * KV_HEADS):
        tile = jnp.where(at == j, picked[:, j * HDIM : (j + 1) * HDIM], tile)
    tile = jnp.where(at == COUNT_ROW, count_ref[0, 0].astype(f32), tile)
    tile = jnp.where(at == MARK_ROW, mark, tile)
    tile = jnp.where(at == TOKEN_MARK_ROW, marks, tile)
    out_ref[...] = tile.astype(bf16)
    at = iota((8, length), 0)
    meta = jnp.where(at == 0, row.astype(f32), 0.0)
    for h in range(HEADS):
        meta = jnp.where((at == 1) & (iota((8, length), 1) == h), sink_ref[:, h : h + 1], meta)
    meta_ref[...] = meta


def columns(j):
    return slice(j * HDIM, (j + 1) * HDIM)


def stacked(ref, j):
    return jnp.concatenate([ref[0, :, columns(j * GROUP + g)] for g in range(GROUP)], 0)


def score_kernel(
    query_ref, grad_ref, kv_ref, far_ref, packs_ref, meta_ref, weight_ref, up_ref, stats_ref, same_ref
):
    same_ref[...] = packs_ref[...]
    length = kv_ref.shape[0]
    scale = HDIM**-0.5
    marks = packs_ref[...].astype(f32)
    own_marks = marks[TOKEN_MARK_ROW : TOKEN_MARK_ROW + 1]
    far_marks = marks[PACK + TOKEN_MARK_ROW : PACK + TOKEN_MARK_ROW + 1]
    own_column = jnp.transpose(jnp.broadcast_to(own_marks, (length, length)))
    far_column = jnp.transpose(jnp.broadcast_to(far_marks, (length, length)))
    bias = jnp.concatenate(
        [jnp.where(own_column == own_marks, 0.0, NEG), jnp.where(far_column == own_marks, 0.0, NEG)], 0
    )
    bias = jnp.concatenate([bias] * GROUP, 1)
    for j in range(KV_HEADS):
        at = slice(j * GROUP * HDIM, (j + 1) * GROUP * HDIM)
        keys = jnp.concatenate([kv_ref[:, columns(j)], far_ref[:, columns(j)]], 0)
        values = jnp.concatenate([kv_ref[:, columns(KV_HEADS + j)], far_ref[:, columns(KV_HEADS + j)]], 0)
        score = lax.dot_general(keys, stacked(query_ref, j), NT, preferred_element_type=f32) * scale + bias
        heads = range(j * GROUP, (j + 1) * GROUP)
        sink = jnp.concatenate([jnp.broadcast_to(meta_ref[1:2, h : h + 1], (1, length)) for h in heads], 1)
        top = jnp.maximum(jnp.max(score, axis=0, keepdims=True), sink)
        weight = jnp.exp(score - top)
        sink_weight = jnp.exp(sink - top)
        weight_ref[:, at] = weight
        up = lax.dot_general(values, stacked(grad_ref, j), NT, preferred_element_type=f32)
        up_ref[:, at] = up
        stats_ref[0:1, at] = top
        stats_ref[1:2, at] = jnp.sum(weight, axis=0, keepdims=True) + sink_weight
        stats_ref[2:3, at] = jnp.sum(weight * up, axis=0, keepdims=True)
        stats_ref[3:4, at] = sink_weight


def main_kernel(
    slots, query_ref, grad_ref, weight_ref, up_ref, stats_ref,
    kv_ref, far_ref, packs_ref, dq_hbm, own_grad_ref, far_grad_ref, out_ref, dq_ref, sinks_ref, sems,
):
    length = kv_ref.shape[0]
    rows = HEADS * HDIM
    group = GROUP * HDIM
    padded = -(-slots // 16) * 16
    order = slot_order(slots)
    scale = HDIM**-0.5
    packs = packs_ref[...]
    at = iota((padded, slots * PACK), 1)
    slot = iota((padded, slots * PACK), 0)
    pick = jnp.concatenate([(at == slot * PACK + row).astype(bf16) for row in range(MARK_ROW + 1)], 0)
    picked = jnp.dot(pick, packs, preferred_element_type=f32)
    chosen = [picked[i * padded : (i + 1) * padded] for i in range(MARK_ROW + 1)]
    slot_keys = [part.astype(bf16) for part in chosen[:KV_HEADS]]
    slot_values = [part.astype(bf16) for part in chosen[KV_HEADS : 2 * KV_HEADS]]
    own_marks = packs[:PACK].astype(f32)[TOKEN_MARK_ROW : TOKEN_MARK_ROW + 1]
    slot_at = iota((padded, length), 0)
    bias = jnp.log(jnp.maximum(chosen[COUNT_ROW], 1.0))
    same = (slot_at < 2) & (chosen[MARK_ROW] == own_marks)
    bias = jnp.where(same | (slot_at >= slots), NEG, bias)
    query = [stacked(query_ref, j) for j in range(KV_HEADS)]
    grad = [stacked(grad_ref, j) for j in range(KV_HEADS)]
    score = jnp.concatenate(
        [lax.dot_general(slot_keys[j], query[j], NT, preferred_element_type=f32) for j in range(KV_HEADS)], 1
    )
    slot_up = jnp.concatenate(
        [lax.dot_general(slot_values[j], grad[j], NT, preferred_element_type=f32) for j in range(KV_HEADS)], 1
    )
    score = score * scale + jnp.concatenate([bias] * HEADS, 1)
    pair_top = stats_ref[0:1]
    top = jnp.maximum(pair_top, jnp.max(score, axis=0, keepdims=True))
    slot_weight = jnp.exp(score - top)
    pair_scale = jnp.exp(pair_top - top)
    inverse = 1.0 / (pair_scale * stats_ref[1:2] + jnp.sum(slot_weight, axis=0, keepdims=True))
    pair_scale = pair_scale * inverse
    slot_prob = slot_weight * inverse
    delta = pair_scale * stats_ref[2:3] + jnp.sum(slot_prob * slot_up, axis=0, keepdims=True)
    slot_ds = (slot_prob * (slot_up - delta)).astype(bf16)
    slot_half = slot_prob.astype(bf16)
    sink_rows = pair_scale * stats_ref[3:4] * delta
    for h in range(HEADS):
        sinks_ref[h : h + 1] = sink_rows[:, h * length : (h + 1) * length]
    sent = []
    halves = []
    signals = []
    for j in range(KV_HEADS):
        at = slice(j * group, (j + 1) * group)
        prob = weight_ref[:, at] * pair_scale[:, at]
        ds = jnp.concatenate([(prob * (up_ref[:, at] - delta[:, at])).astype(bf16), slot_ds[:, at]], 0)
        half = jnp.concatenate([prob.astype(bf16), slot_half[:, at]], 0)
        keys = jnp.concatenate([kv_ref[:, columns(j)], far_ref[:, columns(j)], slot_keys[j]], 0)
        dq = (lax.dot_general(ds, keys, TN, preferred_element_type=f32) * scale).astype(bf16)
        for g in range(GROUP):
            dq_ref[:, columns(j * GROUP + g)] = dq[g * length : (g + 1) * length]
        copy = pltpu.make_async_copy(
            dq_ref.at[:, pl.ds(j * group, group)], dq_hbm.at[0, :, pl.ds(j * group, group)], sems.at[j]
        )
        copy.start()
        sent.append(copy)
        halves.append(half)
        signals.append(ds)
    sinks = jnp.sum(sinks_ref[...], axis=1, keepdims=True)
    sinks = jnp.where(iota((HEADS, HDIM), 0) == iota((HEADS, HDIM), 1), -sinks, 0.0)
    sinks = jnp.sum(sinks, axis=0, keepdims=True)
    high = sinks.astype(bf16).astype(f32)
    ends = (high, sinks - high)
    wide = KV_HEADS * HDIM
    key_rows, value_rows = [], []
    for j in range(KV_HEADS):
        dk = lax.dot_general(signals[j], query[j], NN, preferred_element_type=f32) * scale
        dv = lax.dot_general(halves[j], grad[j], NN, preferred_element_type=f32)
        for to, part, kept in ((j, dk, key_rows), (KV_HEADS + j, dv, value_rows)):
            own_grad_ref[:, columns(to)] = part[:length]
            far_grad_ref[:, columns(to)] = part[length : 2 * length].astype(bf16)
            kept.append(part[2 * length :])

    def piece(first, second):
        shape = out_ref.shape[1:]
        upper = jnp.broadcast_to(jnp.concatenate([first, ends[0]], 1), shape)
        lower = jnp.broadcast_to(jnp.concatenate([second, ends[1]], 1), shape)
        return jnp.where(iota(shape, 0) == 0, upper, lower).astype(bf16)

    nothing = jnp.zeros((1, wide), f32)
    out_ref[...] = jnp.broadcast_to(piece(nothing, nothing)[None], out_ref.shape)
    key_rows = jnp.concatenate(key_rows, 1)
    value_rows = jnp.concatenate(value_rows, 1)
    first = lax.axis_index("dp") * slots
    for slot in range(slots):
        out_ref[first + (lax.axis_index("ctx") ^ order[slot])] = piece(
            key_rows[slot : slot + 1], value_rows[slot : slot + 1]
        )
    for copy in sent:
        copy.wait()


def last_kernel(slots, meta_ref, own_ref, recv_ref, terms_ref, dk_ref, dv_ref, sink_ref):
    length = own_ref.shape[0]
    wide = KV_HEADS * HDIM
    ends = jnp.sum(terms_ref[:, :, wide:].astype(f32), axis=0)
    sink_ref[...] = (ends[0:1] + ends[1:2])[:, :HEADS]
    first = lax.axis_index("dp") * slots
    slot = jnp.sum(terms_ref[pl.ds(first, slots), :, :wide].astype(f32), axis=0)
    mine = iota((length, HDIM), 0).astype(f32) == meta_ref[0:1]
    for i, out_ref in enumerate((dk_ref, dv_ref)):
        for j in range(KV_HEADS):
            at = columns(i * KV_HEADS + j)
            total = own_ref[:, at] + recv_ref[:, at].astype(f32)
            total = total + jnp.where(mine, slot[i : i + 1, columns(j)], 0.0)
            out_ref[0, :, columns(j)] = total.astype(bf16)


def on_device(
    query_rows, key_rows, value_rows, grad_rows, bucket_rank, sample_rows, sample_count, sink_logit
):
    length = query_rows.shape[1]
    wide = KV_HEADS * HDIM
    slots = lax.axis_size("ctx")
    rows = HEADS * HDIM
    kv, tile, meta = pl.pallas_call(
        pack_kernel,
        out_shape=[
            jax.ShapeDtypeStruct((length, 2 * wide), bf16),
            jax.ShapeDtypeStruct((PACK, HDIM), bf16),
            jax.ShapeDtypeStruct((8, length), f32),
        ],
        in_specs=[SMEM] * 2 + [HBM] * 4,
        out_specs=[VMEM] * 3,
        scratch_shapes=[
            pltpu.VMEM((1, length), jnp.int32),
            pltpu.VMEM((1, HEADS), f32),
            pltpu.SemaphoreType.DMA((4,)),
        ],
        compiler_params=SMALL,
        cost_estimate=pl.CostEstimate(flops=10**10, transcendentals=0, bytes_accessed=10**7),
        name="pack_sample",
    )(
        sample_rows,
        sample_count,
        *in_hbm(bucket_rank, sink_logit[None], key_rows, value_rows),
    )

    far_tile = moved(tile, "ctx", 1)
    far_kv = moved(kv, "ctx", 1)
    packs = jnp.concatenate([tile, far_tile], 0)
    weight, up, stats, same = pl.pallas_call(
        score_kernel,
        out_shape=[
            jax.ShapeDtypeStruct((2 * length, rows), f32),
            jax.ShapeDtypeStruct((2 * length, rows), f32),
            jax.ShapeDtypeStruct((8, rows), f32),
            jax.ShapeDtypeStruct(packs.shape, bf16),
        ],
        in_specs=[VMEM] * 6,
        out_specs=[VMEM] * 4,
        compiler_params=LARGE,
        cost_estimate=pl.CostEstimate(
            flops=8 * length * length * rows, transcendentals=2 * length * rows, bytes_accessed=20 * length * rows
        ),
        name="pair_scores",
    )(query_rows, grad_rows, kv, far_kv, packs, meta)
    for offsets in rounds(slots):
        arrived = [moved(packs, "ctx", d) for d in offsets]
        packs = jnp.concatenate([same] + arrived, 0)
        same = packs
    devices = slots * lax.axis_size("dp")
    dq, own, far, terms = pl.pallas_call(
        functools.partial(main_kernel, slots),
        out_shape=[
            jax.ShapeDtypeStruct((1, length, rows), bf16),
            jax.ShapeDtypeStruct((length, 2 * wide), f32),
            jax.ShapeDtypeStruct((length, 2 * wide), bf16),
            jax.ShapeDtypeStruct((devices, 2, wide + HDIM), bf16),
        ],
        in_specs=[VMEM] * 8,
        out_specs=[HBM] + [VMEM] * 3,
        scratch_shapes=[
            pltpu.VMEM((length, rows), bf16),
            pltpu.VMEM((HEADS, length), f32),
            pltpu.SemaphoreType.DMA((KV_HEADS,)),
        ],
        compiler_params=LARGE,
        name="gradients",
    )(query_rows, grad_rows, weight, up, stats, kv, far_kv, packs)
    recv = moved(far, "ctx", 1)
    terms = lax.all_to_all(terms, ("dp", "ctx"), 0, 0, tiled=True)
    dk, dv, sink_grad = pl.pallas_call(
        functools.partial(last_kernel, slots),
        out_shape=[jax.ShapeDtypeStruct((1, length, wide), bf16)] * 2
        + [jax.ShapeDtypeStruct((1, HEADS), f32)],
        in_specs=[VMEM] * 4,
        out_specs=[VMEM] * 3,
        compiler_params=SMALL,
        name="add_up",
    )(meta, own, recv, terms)
    return dq, dk, dv, sink_grad[0]


def solution(mesh):
    return jax.shard_map(
        on_device,
        mesh=mesh,
        in_specs=(
            P("dp", "ctx", None),
            P("dp", "ctx", None),
            P("dp", "ctx", None),
            P("dp", "ctx", None),
            P("dp", "ctx"),
            P("dp", "ctx"),
            P("dp", "ctx"),
            P(),
        ),
        out_specs=(P("dp", "ctx", None), P("dp", "ctx", None), P("dp", "ctx", None), P()),
        check_vma=False,
    )
```

time: 29.9 us -> 27.5 us (0.920)
  waiting for transfers between devices: 3.78 us -> 2.81 us
  Pallas kernels: 6.03 us -> 5.25 us
  blocking collectives: 12.9 us -> 12.3 us
    ppermute x6, waiting for transfers between devices: 3.78 us -> 2.81 us  [moved(): lax.ppermute(array, axis, [(i, i ^ apart) for i in range(lax.axis_size(ax...]
    pallas_call x1, Pallas kernels: 2.68 us -> 1.93 us  [on_device(): pl.pallas_call(functools.partial(main_kernel, slots), out_shape=[jax.Shap...]
    all_to_all x1, blocking collectives: 12.9 us -> 12.3 us  [on_device(): terms = lax.all_to_all(terms, ('dp', 'ctx'), 0, 0, tiled=True)]
    pallas_call x2 -> x1, Pallas kernels: 1.16 us -> 1.27 us  [on_device(): pl.pallas_call(score_kernel, out_shape=[jax.ShapeDtypeStruct((2 * length,...]
  transfers between devices with their start and end apart: 6 -> 6, of which waited for: 2 -> 3; matrix products, arithmetic and copies ran while one was open for 0% -> 0% of each run, Pallas kernels for 2% -> 5%
where the time goes in v4:
time: 27.5 us; the launch traced here: 27.3 us
  blocking collectives  12.3 us (45%)
  Pallas kernels  5.25 us (19%)
  starting transfers between devices  4.92 us (18%)
  waiting for transfers between devices  2.81 us (10%)
  between operations  1.98 us (7%)
    all_to_all x1, blocking collectives, on_device(): terms = lax.all_to_all(terms, ('dp', 'ctx'), 0, 0, tiled=True)  12.3 us
    ppermute x6, starting transfers between devices, moved(): lax.ppermute(array, axis, [(i, i ^ apart) for i in range(lax.axis_size(ax...  4.92 us
    ppermute x6, waiting for transfers between devices, moved(): lax.ppermute(array, axis, [(i, i ^ apart) for i in range(lax.axis_size(ax...  2.81 us
    pallas_call x1, Pallas kernels, on_device(): pl.pallas_call(functools.partial(main_kernel, slots), out_shape=[jax.Shap...  1.93 us
    pallas_call x1, Pallas kernels, on_device(): pl.pallas_call(score_kernel, out_shape=[jax.ShapeDtypeStruct((2 * length,...  1.27 us
    pallas_call x1, Pallas kernels, on_device(): pl.pallas_call(pack_kernel, out_shape=[jax.ShapeDtypeStruct((length, 2 *...  1.25 us
    pallas_call x1, Pallas kernels, on_device(): pl.pallas_call(functools.partial(last_kernel, slots), out_shape=[jax.Shap...  0.8 us
  transfers between devices with their start and end apart: 6, of which 3 were waited for; matrix products, arithmetic and copies ran while one was open for 0% of the time, Pallas kernels for 5%

profile of v4, /device:TPU:0, one launch (start us, length us, event | category | flops | bytes accessed | tf_op | source)
XLA Modules:
  0.0 27.3 jit_solution(7918711599332344250)
XLA Ops:
  1.9 0.0 copy-start
  1.9 0.0 copy-start.1
  1.9 1.2 %pack_sample.1 = (bf16[128,1024]{1,0:T(8,128)(2,1)S(1)}, bf16[16,128]{1,0:T(8,128)(2,1)S(1)}, f32[8,128]{1,0:T(8,128)S(1)}) custom-call(s32[1,1]{1,0:T(1,128)S(6)} %copy.13.row_ref, s32[1,1]{1,0:T(1,128)S(6)} %copy.14.count_ref, s32[1,128]{1,0:T(1,128)} %rank_hbm.1, f32[1,16]{1,0:T(1,128)} %bitcast.2, bf16[1,128,512]{2,1,0:T(8,128)(2,1)} %keys_hbm.1, ...), custom_call_target="tpu_custom_call" | custom-call | flops 10000000000 | bytes 10000000 | tf_op jit(solution)/shard_map/pack_sample/pallas_call | solution.py:264
  3.2 0.5 %collective-permute-start = (bf16[128,1024]{1,0:T(8,128)(2,1)S(1)}, bf16[128,1024]{1,0:T(8,128)(2,1)S(1)}, u32[]{:S(2)}, u32[]{:S(2)}) collective-permute-start(bf16[128,1024]{1,0:T(8,128)(2,1)S(1)} %get-tuple-element.18.kv_ref), channel_id=1, source_target_pairs={{0,1},{1,0},{2,3},{3,2},{4,5},{5,4},{6,7},{7,6},{8,9},{9,8},{10,11... | collective-permute-start | bytes 786440 | tf_op jit(solution)/shard_map/ppermute | solution.py:38
  3.7 0.1 collective-permute-start.1
  3.8 1.1 %collective-permute-done.1 = bf16[16,128]{1,0:T(8,128)(2,1)S(1)} collective-permute-done((bf16[16,128]{1,0:T(8,128)(2,1)S(1)}, bf16[16,128]{1,0:T(8,128)(2,1)S(1)}, u32[]{:S(2)}, u32[]{:S(2)}) %collective-permute-start.1) | collective-permute-done | bytes 4128 | tf_op jit(solution)/shard_map/ppermute | solution.py:38
  4.9 3.6 %collective-permute-start.4 = (bf16[32,128]{1,0:T(8,128)(2,1)S(1)}, bf16[32,128]{1,0:T(8,128)(2,1)S(1)}, u32[]{:S(2)}, u32[]{:S(2)}) collective-permute-start(bf16[32,128]{1,0:T(8,128)(2,1)S(1)} %constant_dynamic-update-slice_fusion.packs_ref), channel_id=1, source_target_pairs={{0,7},{1,6},{2,5},{3,4},{4,3},{5,2},{6,1},{7,0},{8,15},{9,14},{10,... | collective-permute-start | bytes 24584 | tf_op jit(solution)/shard_map/ppermute | solution.py:38
  8.5 0.5 %collective-permute-start.3 = (bf16[32,128]{1,0:T(8,128)(2,1)S(1)}, bf16[32,128]{1,0:T(8,128)(2,1)S(1)}, u32[]{:S(2)}, u32[]{:S(2)}) collective-permute-start(bf16[32,128]{1,0:T(8,128)(2,1)S(1)} %constant_dynamic-update-slice_fusion.packs_ref), channel_id=1, source_target_pairs={{0,5},{1,4},{2,7},{3,6},{4,1},{5,0},{6,3},{7,2},{8,13},{9,12},{10,... | collective-permute-start | bytes 24584 | tf_op jit(solution)/shard_map/ppermute | solution.py:38
  8.9 0.1 collective-permute-start.2
  9.0 0.0 collective-permute-done.far_ref
  9.0 0.0 copy-done
  9.0 0.0 copy-done.1
  9.0 1.3 %pair_scores.1 = (f32[256,2048]{1,0:T(8,128)S(1)}, f32[256,2048]{1,0:T(8,128)S(1)}, f32[8,2048]{1,0:T(8,128)S(1)}, bf16[32,128]{1,0:T(8,128)(2,1)S(1)}) custom-call(bf16[1,128,2048]{2,1,0:T(8,128)(2,1)S(1)} %copy-done, bf16[1,128,2048]{2,1,0:T(8,128)(2,1)S(1)} %copy-done.1, bf16[128,1024]{1,0:T(8,128)(2,1)S(1)} %get-tuple-element.18.kv_ref, ...), custom_call_target="tpu_custom_call" | custom-call | flops 268435456 | bytes 5242880 | tf_op jit(solution)/shard_map/pair_scores/pallas_call | solution.py:290
  10.3 0.0 collective-permute-done.4
  10.3 1.2 %collective-permute-done.3 = bf16[32,128]{1,0:T(8,128)(2,1)S(1)} collective-permute-done((bf16[32,128]{1,0:T(8,128)(2,1)S(1)}, bf16[32,128]{1,0:T(8,128)(2,1)S(1)}, u32[]{:S(2)}, u32[]{:S(2)}) %collective-permute-start.3) | collective-permute-done | bytes 8224 | tf_op jit(solution)/shard_map/ppermute | solution.py:38
  11.5 0.5 %collective-permute-done.2 = bf16[32,128]{1,0:T(8,128)(2,1)S(1)} collective-permute-done((bf16[32,128]{1,0:T(8,128)(2,1)S(1)}, bf16[32,128]{1,0:T(8,128)(2,1)S(1)}, u32[]{:S(2)}, u32[]{:S(2)}) %collective-permute-start.2) | collective-permute-done | bytes 8224 | tf_op jit(solution)/shard_map/ppermute | solution.py:38
  12.0 1.9 %gradients.1 = (bf16[1,128,2048]{2,1,0:T(8,128)(2,1)}, f32[128,1024]{1,0:T(8,128)S(1)}, bf16[128,1024]{1,0:T(8,128)(2,1)S(1)}, bf16[32,2,640]{2,1,0:T(2,128)(2,1)S(1)}) custom-call(bf16[1,128,2048]{2,1,0:T(8,128)(2,1)S(1)} %copy-done, bf16[1,128,2048]{2,1,0:T(8,128)(2,1)S(1)} %copy-done.1, f32[256,2048]{1,0:T(8,128)S(1)} %get-tuple-element.21.weight_ref, ...), custom_call_target="tpu_custom_call" | custom-call | tf_op jit(solution)/shard_map/gradients/pallas_call | solution.py:311
  14.0 0.2 collective-permute-start.5
  14.2 12.3 %all_to_all.5.terms_ref = bf16[32,2,640]{2,1,0:T(2,128)(2,1)S(1)} all-to-all(bf16[32,2,640]{2,1,0:T(2,128)(2,1)S(1)} %get-tuple-element.28), channel_id=1, replica_groups=mesh['dp'=4,'ctx'=8] {'dp','ctx'}, dimensions={0} | all-to-all | bytes 163840 | tf_op jit(solution)/shard_map/all_to_all | solution.py:330
  26.5 0.0 collective-permute-done.5.recv_ref
  26.5 0.8 %add_up.1 = (bf16[1,128,512]{2,1,0:T(8,128)(2,1)}, bf16[1,128,512]{2,1,0:T(8,128)(2,1)}, f32[1,16]{1,0:T(1,128)}) custom-call(f32[8,128]{1,0:T(8,128)S(1)} %get-tuple-element.20.meta_ref, f32[128,1024]{1,0:T(8,128)S(1)} %get-tuple-element.26.own_ref, bf16[128,1024]{1,0:T(8,128)(2,1)S(1)} %collective-permute-done.5.recv_ref, ...), custom_call_target="tpu_custom_call" | custom-call | tf_op jit(solution)/shard_map/add_up/pallas_call | solution.py:331
  (3 shorter events, 0.0 us)
Async XLA Ops:
  1.9 7.1 %copy-start = (bf16[1,128,2048]{2,1,0:T(8,128)(2,1)S(1)}, bf16[1,128,2048]{2,1,0:T(8,128)(2,1)}, u32[]{:S(2)}) copy-start(bf16[1,128,2048]{2,1,0:T(8,128)(2,1)} %query_ref.3) | copy-start | bytes 1572868
  1.9 7.1 %copy-start.1 = (bf16[1,128,2048]{2,1,0:T(8,128)(2,1)S(1)}, bf16[1,128,2048]{2,1,0:T(8,128)(2,1)}, u32[]{:S(2)}) copy-start(bf16[1,128,2048]{2,1,0:T(8,128)(2,1)} %grad_ref.3) | copy-start | bytes 1572868
  3.2 5.8 %collective-permute-start = (bf16[128,1024]{1,0:T(8,128)(2,1)S(1)}, bf16[128,1024]{1,0:T(8,128)(2,1)S(1)}, u32[]{:S(2)}, u32[]{:S(2)}) collective-permute-start(bf16[128,1024]{1,0:T(8,128)(2,1)S(1)} %get-tuple-element.18.kv_ref), channel_id=1, source_target_pairs={{0,1},{1,0},{2,3},{3,2},{4,5},{5,4},{6,7},{7,6},{8,9},{9,8},{10,11... | collective-permute-start | bytes 786440 | tf_op jit(solution)/shard_map/ppermute | solution.py:38
  3.7 1.2 %collective-permute-start.1 = (bf16[16,128]{1,0:T(8,128)(2,1)S(1)}, bf16[16,128]{1,0:T(8,128)(2,1)S(1)}, u32[]{:S(2)}, u32[]{:S(2)}) collective-permute-start(bf16[16,128]{1,0:T(8,128)(2,1)S(1)} %get-tuple-element.19), channel_id=1, source_target_pairs={{0,1},{1,0},{2,3},{3,2},{4,5},{5,4},{6,7},{7,6},{8,9},{9,8},{10,11... | collective-permute-start | bytes 12296 | tf_op jit(solution)/shard_map/ppermute | solution.py:38
  4.9 5.4 %collective-permute-start.4 = (bf16[32,128]{1,0:T(8,128)(2,1)S(1)}, bf16[32,128]{1,0:T(8,128)(2,1)S(1)}, u32[]{:S(2)}, u32[]{:S(2)}) collective-permute-start(bf16[32,128]{1,0:T(8,128)(2,1)S(1)} %constant_dynamic-update-slice_fusion.packs_ref), channel_id=1, source_target_pairs={{0,7},{1,6},{2,5},{3,4},{4,3},{5,2},{6,1},{7,0},{8,15},{9,14},{10,... | collective-permute-start | bytes 24584 | tf_op jit(solution)/shard_map/ppermute | solution.py:38
  8.5 3.1 %collective-permute-start.3 = (bf16[32,128]{1,0:T(8,128)(2,1)S(1)}, bf16[32,128]{1,0:T(8,128)(2,1)S(1)}, u32[]{:S(2)}, u32[]{:S(2)}) collective-permute-start(bf16[32,128]{1,0:T(8,128)(2,1)S(1)} %constant_dynamic-update-slice_fusion.packs_ref), channel_id=1, source_target_pairs={{0,5},{1,4},{2,7},{3,6},{4,1},{5,0},{6,3},{7,2},{8,13},{9,12},{10,... | collective-permute-start | bytes 24584 | tf_op jit(solution)/shard_map/ppermute | solution.py:38
  8.9 3.1 %collective-permute-start.2 = (bf16[32,128]{1,0:T(8,128)(2,1)S(1)}, bf16[32,128]{1,0:T(8,128)(2,1)S(1)}, u32[]{:S(2)}, u32[]{:S(2)}) collective-permute-start(bf16[32,128]{1,0:T(8,128)(2,1)S(1)} %constant_dynamic-update-slice_fusion.packs_ref), channel_id=1, source_target_pairs={{0,3},{1,2},{2,1},{3,0},{4,7},{5,6},{6,5},{7,4},{8,11},{9,10},{10,... | collective-permute-start | bytes 24584 | tf_op jit(solution)/shard_map/ppermute | solution.py:38
  14.0 12.6 %collective-permute-start.5 = (bf16[128,1024]{1,0:T(8,128)(2,1)S(1)}, bf16[128,1024]{1,0:T(8,128)(2,1)S(1)}, u32[]{:S(2)}, u32[]{:S(2)}) collective-permute-start(bf16[128,1024]{1,0:T(8,128)(2,1)S(1)} %get-tuple-element.27), channel_id=1, source_target_pairs={{0,1},{1,0},{2,3},{3,2},{4,5},{5,4},{6,7},{7,6},{8,9},{9,8},{10,11... | collective-permute-start | bytes 786440 | tf_op jit(solution)/shard_map/ppermute | solution.py:38

commit v5 on v4

--- a/solution.py
+++ b/solution.py
@@ -27,6 +27,7 @@
 SMEM = pl.BlockSpec(memory_space=pltpu.SMEM)
 HBM = pl.BlockSpec(memory_space=pltpu.HBM)
 LARGE = pltpu.CompilerParams(vmem_limit_bytes=24 * 1024 * 1024)
+LOADS = pl.CostEstimate(flops=10**10, transcendentals=0, bytes_accessed=10**7)
 SMALL = pltpu.CompilerParams(vmem_limit_bytes=6 * 1024 * 1024)
 
 
@@ -57,32 +58,22 @@
     return lax.broadcasted_iota(jnp.int32, shape, dim)
 
 
+def token_kernel(out_ref):
+    out_ref[...] = iota(out_ref.shape, 1)
+
+
 def pack_kernel(
-    row_ref, count_ref, rank_hbm, sink_hbm, keys_hbm, values_hbm,
-    kv_ref, out_ref, meta_ref, rank_ref, sink_ref, sems,
+    row_ref, count_ref, token_ref, rank_ref, sink_ref, keys_ref, values_ref, kv_ref, out_ref, meta_ref
 ):
-    wide = keys_hbm.shape[2]
-    copies = [
-        pltpu.make_async_copy(from_ref, to_ref, sems.at[i])
-        for i, (from_ref, to_ref) in enumerate(
-            [
-                (keys_hbm.at[0], kv_ref.at[:, :wide]),
-                (values_hbm.at[0], kv_ref.at[:, wide:]),
-                (rank_hbm, rank_ref),
-                (sink_hbm, sink_ref),
-            ]
-        )
-    ]
-    for copy in copies:
-        copy.start()
-    for copy in copies:
-        copy.wait()
+    wide = keys_ref.shape[2]
+    kv_ref[:, :wide] = keys_ref[0]
+    kv_ref[:, wide:] = values_ref[0]
     length = kv_ref.shape[0]
     row = row_ref[0, 0]
-    pick = (iota((PACK, length), 1) == row).astype(bf16)
+    pick = (token_ref[...] == row).astype(bf16)
     picked = jnp.dot(pick, kv_ref[...], preferred_element_type=f32)
     marks = (rank_ref[...] >= BUCKET).astype(f32)
-    mark = jnp.sum(jnp.where(iota((1, length), 1) == row, marks, 0.0), axis=1, keepdims=True)
+    mark = jnp.sum(jnp.where(token_ref[:1] == row, marks, 0.0), axis=1, keepdims=True)
     at = iota((PACK, HDIM), 0)
     tile = jnp.zeros((PACK, HDIM), f32)
     for j in range(2 * KV_HEADS):
@@ -93,8 +84,8 @@
     out_ref[...] = tile.astype(bf16)
     at = iota((8, length), 0)
     meta = jnp.where(at == 0, row.astype(f32), 0.0)
-    for h in range(HEADS):
-        meta = jnp.where((at == 1) & (iota((8, length), 1) == h), sink_ref[:, h : h + 1], meta)
+    sinks = jnp.concatenate([sink_ref[...], jnp.zeros((1, length - HEADS), f32)], 1)
+    meta = jnp.where(at == 1, sinks, meta)
     meta_ref[...] = meta
 
 
@@ -261,6 +252,15 @@
     wide = KV_HEADS * HDIM
     slots = lax.axis_size("ctx")
     rows = HEADS * HDIM
+    token = pl.pallas_call(
+        token_kernel,
+        out_shape=jax.ShapeDtypeStruct((PACK, length), jnp.int32),
+        out_specs=VMEM,
+        compiler_params=SMALL,
+        cost_estimate=LOADS,
+        name="token_lanes",
+    )()
+    sample_rows, sample_count, token = lax.optimization_barrier((sample_rows, sample_count, token))
     kv, tile, meta = pl.pallas_call(
         pack_kernel,
         out_shape=[
@@ -268,21 +268,12 @@
             jax.ShapeDtypeStruct((PACK, HDIM), bf16),
             jax.ShapeDtypeStruct((8, length), f32),
         ],
-        in_specs=[SMEM] * 2 + [HBM] * 4,
+        in_specs=[SMEM] * 2 + [VMEM] * 5,
         out_specs=[VMEM] * 3,
-        scratch_shapes=[
-            pltpu.VMEM((1, length), jnp.int32),
-            pltpu.VMEM((1, HEADS), f32),
-            pltpu.SemaphoreType.DMA((4,)),
-        ],
         compiler_params=SMALL,
-        cost_estimate=pl.CostEstimate(flops=10**10, transcendentals=0, bytes_accessed=10**7),
+        cost_estimate=LOADS,
         name="pack_sample",
-    )(
-        sample_rows,
-        sample_count,
-        *in_hbm(bucket_rank, sink_logit[None], key_rows, value_rows),
-    )
+    )(sample_rows, sample_count, token, bucket_rank, sink_logit[None], key_rows, value_rows)
 
     far_tile = moved(tile, "ctx", 1)
     far_kv = moved(kv, "ctx", 1)

time: 27.5 us -> 26.5 us (0.964)
  Pallas kernels: 5.25 us -> 4.16 us
    pallas_call x1, Pallas kernels: 1.25 us -> 0.15 us  [on_device(): pl.pallas_call(pack_kernel, out_shape=[jax.ShapeDtypeStruct((length, 2 *...]
where the time goes in v5:
time: 26.5 us; the launch traced here: 26.3 us
  blocking collectives  12.3 us (46%)
  starting transfers between devices  4.83 us (18%)
  Pallas kernels  4.16 us (16%)
  waiting for transfers between devices  2.83 us (11%)
  between operations  2.09 us (8%)
    all_to_all x1, blocking collectives, on_device(): terms = lax.all_to_all(terms, ('dp', 'ctx'), 0, 0, tiled=True)  12.3 us
    ppermute x6, starting transfers between devices, moved(): lax.ppermute(array, axis, [(i, i ^ apart) for i in range(lax.axis_size(ax...  4.83 us
    ppermute x6, waiting for transfers between devices, moved(): lax.ppermute(array, axis, [(i, i ^ apart) for i in range(lax.axis_size(ax...  2.83 us
    pallas_call x1, Pallas kernels, on_device(): pl.pallas_call(functools.partial(main_kernel, slots), out_shape=[jax.Shap...  1.93 us
    pallas_call x1, Pallas kernels, on_device(): pl.pallas_call(score_kernel, out_shape=[jax.ShapeDtypeStruct((2 * length,...  1.27 us
    pallas_call x1, Pallas kernels, on_device(): pl.pallas_call(functools.partial(last_kernel, slots), out_shape=[jax.Shap...  0.8 us
  transfers between devices with their start and end apart: 6, of which 3 were waited for; matrix products, arithmetic and copies ran while one was open for 0% of the time, Pallas kernels for 5%

profile of v5, /device:TPU:0, one launch (start us, length us, event | category | flops | bytes accessed | tf_op | source)
XLA Modules:
  0.0 26.3 jit_solution(17065203873360166048)
XLA Ops:
  0.6 0.0 copy-start.5
  0.6 0.0 copy-start.4
  0.7 0.0 copy-start.3
  0.7 0.0 copy-start.2
  2.0 0.0 copy-done.5
  2.0 0.0 copy-done.4
  2.0 0.0 copy-done.3
  2.1 0.0 copy-done.2
  2.1 0.0 copy-start
  2.1 0.0 copy-start.1
  2.1 0.2 pack_sample.1
  2.2 0.5 %collective-permute-start = (bf16[128,1024]{1,0:T(8,128)(2,1)S(1)}, bf16[128,1024]{1,0:T(8,128)(2,1)S(1)}, u32[]{:S(2)}, u32[]{:S(2)}) collective-permute-start(bf16[128,1024]{1,0:T(8,128)(2,1)S(1)} %get-tuple-element.24.kv_ref), channel_id=1, source_target_pairs={{0,1},{1,0},{2,3},{3,2},{4,5},{5,4},{6,7},{7,6},{8,9},{9,8},{10,11... | collective-permute-start | bytes 786440 | tf_op jit(solution)/shard_map/ppermute | solution.py:39
  2.7 0.1 collective-permute-start.1
  2.8 1.1 %collective-permute-done.1 = bf16[16,128]{1,0:T(8,128)(2,1)S(1)} collective-permute-done((bf16[16,128]{1,0:T(8,128)(2,1)S(1)}, bf16[16,128]{1,0:T(8,128)(2,1)S(1)}, u32[]{:S(2)}, u32[]{:S(2)}) %collective-permute-start.1) | collective-permute-done | bytes 4128 | tf_op jit(solution)/shard_map/ppermute | solution.py:39
  3.9 3.6 %collective-permute-start.4 = (bf16[32,128]{1,0:T(8,128)(2,1)S(1)}, bf16[32,128]{1,0:T(8,128)(2,1)S(1)}, u32[]{:S(2)}, u32[]{:S(2)}) collective-permute-start(bf16[32,128]{1,0:T(8,128)(2,1)S(1)} %constant_dynamic-update-slice_fusion.packs_ref), channel_id=1, source_target_pairs={{0,7},{1,6},{2,5},{3,4},{4,3},{5,2},{6,1},{7,0},{8,15},{9,14},{10,... | collective-permute-start | bytes 24584 | tf_op jit(solution)/shard_map/ppermute | solution.py:39
  7.4 0.5 %collective-permute-start.3 = (bf16[32,128]{1,0:T(8,128)(2,1)S(1)}, bf16[32,128]{1,0:T(8,128)(2,1)S(1)}, u32[]{:S(2)}, u32[]{:S(2)}) collective-permute-start(bf16[32,128]{1,0:T(8,128)(2,1)S(1)} %constant_dynamic-update-slice_fusion.packs_ref), channel_id=1, source_target_pairs={{0,5},{1,4},{2,7},{3,6},{4,1},{5,0},{6,3},{7,2},{8,13},{9,12},{10,... | collective-permute-start | bytes 24584 | tf_op jit(solution)/shard_map/ppermute | solution.py:39
  7.9 0.1 collective-permute-start.2
  8.0 0.0 collective-permute-done.far_ref
  8.0 0.0 copy-done
  8.0 0.0 copy-done.1
  8.0 1.3 %pair_scores.1 = (f32[256,2048]{1,0:T(8,128)S(1)}, f32[256,2048]{1,0:T(8,128)S(1)}, f32[8,2048]{1,0:T(8,128)S(1)}, bf16[32,128]{1,0:T(8,128)(2,1)S(1)}) custom-call(bf16[1,128,2048]{2,1,0:T(8,128)(2,1)S(1)} %copy-done, bf16[1,128,2048]{2,1,0:T(8,128)(2,1)S(1)} %copy-done.1, bf16[128,1024]{1,0:T(8,128)(2,1)S(1)} %get-tuple-element.24.kv_ref, ...), custom_call_target="tpu_custom_call" | custom-call | flops 268435456 | bytes 5242880 | tf_op jit(solution)/shard_map/pair_scores/pallas_call | solution.py:281
  9.3 0.0 collective-permute-done.4
  9.3 1.2 %collective-permute-done.3 = bf16[32,128]{1,0:T(8,128)(2,1)S(1)} collective-permute-done((bf16[32,128]{1,0:T(8,128)(2,1)S(1)}, bf16[32,128]{1,0:T(8,128)(2,1)S(1)}, u32[]{:S(2)}, u32[]{:S(2)}) %collective-permute-start.3) | collective-permute-done | bytes 8224 | tf_op jit(solution)/shard_map/ppermute | solution.py:39
  10.5 0.5 %collective-permute-done.2 = bf16[32,128]{1,0:T(8,128)(2,1)S(1)} collective-permute-done((bf16[32,128]{1,0:T(8,128)(2,1)S(1)}, bf16[32,128]{1,0:T(8,128)(2,1)S(1)}, u32[]{:S(2)}, u32[]{:S(2)}) %collective-permute-start.2) | collective-permute-done | bytes 8224 | tf_op jit(solution)/shard_map/ppermute | solution.py:39
  11.0 1.9 %gradients.1 = (bf16[1,128,2048]{2,1,0:T(8,128)(2,1)}, f32[128,1024]{1,0:T(8,128)S(1)}, bf16[128,1024]{1,0:T(8,128)(2,1)S(1)}, bf16[32,2,640]{2,1,0:T(2,128)(2,1)S(1)}) custom-call(bf16[1,128,2048]{2,1,0:T(8,128)(2,1)S(1)} %copy-done, bf16[1,128,2048]{2,1,0:T(8,128)(2,1)S(1)} %copy-done.1, f32[256,2048]{1,0:T(8,128)S(1)} %get-tuple-element.27.weight_ref, ...), custom_call_target="tpu_custom_call" | custom-call | tf_op jit(solution)/shard_map/gradients/pallas_call | solution.py:302
  12.9 0.2 collective-permute-start.5
  13.1 12.3 %all_to_all.5.terms_ref = bf16[32,2,640]{2,1,0:T(2,128)(2,1)S(1)} all-to-all(bf16[32,2,640]{2,1,0:T(2,128)(2,1)S(1)} %get-tuple-element.34), channel_id=1, replica_groups=mesh['dp'=4,'ctx'=8] {'dp','ctx'}, dimensions={0} | all-to-all | bytes 163840 | tf_op jit(solution)/shard_map/all_to_all | solution.py:321
  25.5 0.0 collective-permute-done.5.recv_ref
  25.5 0.8 %add_up.1 = (bf16[1,128,512]{2,1,0:T(8,128)(2,1)}, bf16[1,128,512]{2,1,0:T(8,128)(2,1)}, f32[1,16]{1,0:T(1,128)}) custom-call(f32[8,128]{1,0:T(8,128)S(1)} %get-tuple-element.26.meta_ref, f32[128,1024]{1,0:T(8,128)S(1)} %get-tuple-element.32.own_ref, bf16[128,1024]{1,0:T(8,128)(2,1)S(1)} %collective-permute-done.5.recv_ref, ...), custom_call_target="tpu_custom_call" | custom-call | tf_op jit(solution)/shard_map/add_up/pallas_call | solution.py:322
  (4 shorter events, 0.0 us)
Async XLA Ops:
  0.6 1.4 %copy-start.5 = (f32[16]{0:T(128)S(1)}, f32[16]{0:T(128)}, u32[]{:S(2)}) copy-start(f32[16]{0:T(128)} %param.15) | copy-start | bytes 196
  0.6 1.4 %copy-start.4 = (s32[1,128]{1,0:T(1,128)S(1)}, s32[1,128]{1,0:T(1,128)}, u32[]{:S(2)}) copy-start(s32[1,128]{1,0:T(1,128)} %rank_ref.1) | copy-start | bytes 1540
  0.7 1.4 %copy-start.3 = (bf16[1,128,512]{2,1,0:T(8,128)(2,1)S(1)}, bf16[1,128,512]{2,1,0:T(8,128)(2,1)}, u32[]{:S(2)}) copy-start(bf16[1,128,512]{2,1,0:T(8,128)(2,1)} %values_ref.1) | copy-start | bytes 393220
  0.7 1.4 %copy-start.2 = (bf16[1,128,512]{2,1,0:T(8,128)(2,1)S(1)}, bf16[1,128,512]{2,1,0:T(8,128)(2,1)}, u32[]{:S(2)}) copy-start(bf16[1,128,512]{2,1,0:T(8,128)(2,1)} %keys_ref.1) | copy-start | bytes 393220
  2.1 5.9 %copy-start = (bf16[1,128,2048]{2,1,0:T(8,128)(2,1)S(1)}, bf16[1,128,2048]{2,1,0:T(8,128)(2,1)}, u32[]{:S(2)}) copy-start(bf16[1,128,2048]{2,1,0:T(8,128)(2,1)} %query_ref.3) | copy-start | bytes 1572868
  2.1 5.9 %copy-start.1 = (bf16[1,128,2048]{2,1,0:T(8,128)(2,1)S(1)}, bf16[1,128,2048]{2,1,0:T(8,128)(2,1)}, u32[]{:S(2)}) copy-start(bf16[1,128,2048]{2,1,0:T(8,128)(2,1)} %grad_ref.3) | copy-start | bytes 1572868
  2.2 5.7 %collective-permute-start = (bf16[128,1024]{1,0:T(8,128)(2,1)S(1)}, bf16[128,1024]{1,0:T(8,128)(2,1)S(1)}, u32[]{:S(2)}, u32[]{:S(2)}) collective-permute-start(bf16[128,1024]{1,0:T(8,128)(2,1)S(1)} %get-tuple-element.24.kv_ref), channel_id=1, source_target_pairs={{0,1},{1,0},{2,3},{3,2},{4,5},{5,4},{6,7},{7,6},{8,9},{9,8},{10,11... | collective-permute-start | bytes 786440 | tf_op jit(solution)/shard_map/ppermute | solution.py:39
  2.7 1.2 %collective-permute-start.1 = (bf16[16,128]{1,0:T(8,128)(2,1)S(1)}, bf16[16,128]{1,0:T(8,128)(2,1)S(1)}, u32[]{:S(2)}, u32[]{:S(2)}) collective-permute-start(bf16[16,128]{1,0:T(8,128)(2,1)S(1)} %get-tuple-element.25), channel_id=1, source_target_pairs={{0,1},{1,0},{2,3},{3,2},{4,5},{5,4},{6,7},{7,6},{8,9},{9,8},{10,11... | collective-permute-start | bytes 12296 | tf_op jit(solution)/shard_map/ppermute | solution.py:39
  3.9 5.4 %collective-permute-start.4 = (bf16[32,128]{1,0:T(8,128)(2,1)S(1)}, bf16[32,128]{1,0:T(8,128)(2,1)S(1)}, u32[]{:S(2)}, u32[]{:S(2)}) collective-permute-start(bf16[32,128]{1,0:T(8,128)(2,1)S(1)} %constant_dynamic-update-slice_fusion.packs_ref), channel_id=1, source_target_pairs={{0,7},{1,6},{2,5},{3,4},{4,3},{5,2},{6,1},{7,0},{8,15},{9,14},{10,... | collective-permute-start | bytes 24584 | tf_op jit(solution)/shard_map/ppermute | solution.py:39
  7.4 3.1 %collective-permute-start.3 = (bf16[32,128]{1,0:T(8,128)(2,1)S(1)}, bf16[32,128]{1,0:T(8,128)(2,1)S(1)}, u32[]{:S(2)}, u32[]{:S(2)}) collective-permute-start(bf16[32,128]{1,0:T(8,128)(2,1)S(1)} %constant_dynamic-update-slice_fusion.packs_ref), channel_id=1, source_target_pairs={{0,5},{1,4},{2,7},{3,6},{4,1},{5,0},{6,3},{7,2},{8,13},{9,12},{10,... | collective-permute-start | bytes 24584 | tf_op jit(solution)/shard_map/ppermute | solution.py:39
  7.9 3.1 %collective-permute-start.2 = (bf16[32,128]{1,0:T(8,128)(2,1)S(1)}, bf16[32,128]{1,0:T(8,128)(2,1)S(1)}, u32[]{:S(2)}, u32[]{:S(2)}) collective-permute-start(bf16[32,128]{1,0:T(8,128)(2,1)S(1)} %constant_dynamic-update-slice_fusion.packs_ref), channel_id=1, source_target_pairs={{0,3},{1,2},{2,1},{3,0},{4,7},{5,6},{6,5},{7,4},{8,11},{9,10},{10,... | collective-permute-start | bytes 24584 | tf_op jit(solution)/shard_map/ppermute | solution.py:39
  12.9 12.6 %collective-permute-start.5 = (bf16[128,1024]{1,0:T(8,128)(2,1)S(1)}, bf16[128,1024]{1,0:T(8,128)(2,1)S(1)}, u32[]{:S(2)}, u32[]{:S(2)}) collective-permute-start(bf16[128,1024]{1,0:T(8,128)(2,1)S(1)} %get-tuple-element.33), channel_id=1, source_target_pairs={{0,1},{1,0},{2,3},{3,2},{4,5},{5,4},{6,7},{7,6},{8,9},{9,8},{10,11... | collective-permute-start | bytes 786440 | tf_op jit(solution)/shard_map/ppermute | solution.py:39

commit v6 on v5

v6 whole, which is shorter than its diff:
```python
import functools

import jax
import jax.numpy as jnp
from jax import lax
from jax.experimental import pallas as pl
from jax.experimental.pallas import tpu as pltpu
from jax.sharding import PartitionSpec as P

HEADS = 16
KV_HEADS = 4
HDIM = 128
BUCKET = 128
GROUP = HEADS // KV_HEADS
NEG = -1e30
PACK = 16
COUNT_ROW = 8
MARK_ROW = 9
RANK_ROW = 10

f32 = jnp.float32
bf16 = jnp.bfloat16
NN = (((1,), (0,)), ((), ()))
NT = (((1,), (1,)), ((), ()))
TN = (((0,), (0,)), ((), ()))
VMEM = pl.BlockSpec(memory_space=pltpu.VMEM)
SMEM = pl.BlockSpec(memory_space=pltpu.SMEM)
HBM = pl.BlockSpec(memory_space=pltpu.HBM)
LARGE = pltpu.CompilerParams(vmem_limit_bytes=24 * 1024 * 1024)
LOADS = pl.CostEstimate(flops=10**10, transcendentals=0, bytes_accessed=10**7)
SMALL = pltpu.CompilerParams(vmem_limit_bytes=6 * 1024 * 1024)


def in_hbm(*arrays):
    return [pltpu.with_memory_space_constraint(array, pltpu.HBM) for array in arrays]


def moved(array, axis, apart):
    return lax.ppermute(array, axis, [(i, i ^ apart) for i in range(lax.axis_size(axis))])


def rounds(size):
    found, base = [], 2
    while base < size:
        found.append([base + 1] if base * 2 >= size else [base + 1, 2 * base + 1, 3 * base + 1])
        base *= 2 if base * 2 >= size else 4
    return found


def slot_order(size):
    order = [0, 1]
    for offsets in rounds(size):
        order = order + [d ^ near for d in offsets for near in order]
    return order


def iota(shape, dim):
    return lax.broadcasted_iota(jnp.int32, shape, dim)


def token_kernel(out_ref):
    out_ref[...] = iota(out_ref.shape, 1)


def pack_kernel(
    row_ref, count_ref, token_ref, rank_ref, keys_ref, values_ref, kv_ref, out_ref, meta_ref
):
    wide = keys_ref.shape[2]
    kv_ref[:, :wide] = keys_ref[0]
    kv_ref[:, wide:] = values_ref[0]
    length = kv_ref.shape[0]
    row = row_ref[0, 0]
    pick = (token_ref[...] == row).astype(bf16)
    picked = jnp.dot(pick, kv_ref[...], preferred_element_type=f32)
    ranks = rank_ref[...].astype(f32)
    mark = jnp.sum(jnp.where(token_ref[:1] == row, ranks, 0.0), axis=1, keepdims=True)
    mark = (mark >= BUCKET).astype(f32)
    at = iota((PACK, HDIM), 0)
    tile = jnp.zeros((PACK, HDIM), f32)
    for j in range(2 * KV_HEADS):
        tile = jnp.where(at == j, picked[:, j * HDIM : (j + 1) * HDIM], tile)
    tile = jnp.where(at == COUNT_ROW, count_ref[0, 0].astype(f32), tile)
    tile = jnp.where(at == MARK_ROW, mark, tile)
    tile = jnp.where(at == RANK_ROW, ranks, tile)
    out_ref[...] = tile.astype(bf16)
    at = iota((8, length), 0)
    meta = jnp.where(at == 0, row.astype(f32), 0.0)
    meta_ref[...] = meta


def columns(j):
    return slice(j * HDIM, (j + 1) * HDIM)


def stacked(ref, j):
    return jnp.concatenate([ref[0, :, columns(j * GROUP + g)] for g in range(GROUP)], 0)


def by_bucket(rows, first):
    low = jnp.concatenate([first] * GROUP, 0).astype(bf16)
    high = jnp.concatenate([1.0 - first] * GROUP, 0).astype(bf16)
    return jnp.concatenate([rows * low, rows * high], 1)


def score_kernel(
    query_ref, grad_ref, kv_ref, far_ref, packs_ref, sink_ref,
    weight_ref, up_ref, stats_ref, keys2_ref, home_ref, first_ref, same_ref,
):
    same_ref[...] = packs_ref[...]
    length = kv_ref.shape[0]
    span = 2 * length
    group = GROUP * length
    scale = HDIM**-0.5
    tiles = packs_ref[...].astype(f32)
    own_ranks = tiles[RANK_ROW : RANK_ROW + 1]
    far_ranks = tiles[PACK + RANK_ROW : PACK + RANK_ROW + 1]
    ranks = jnp.concatenate([own_ranks, far_ranks], 1)
    move = (iota((span, span), 0).astype(f32) == ranks).astype(f32)
    home_ref[...] = jnp.transpose(move).astype(bf16)
    in_order = jnp.dot(
        move.astype(bf16), jnp.concatenate([kv_ref[...], far_ref[...]], 0), preferred_element_type=f32
    ).astype(bf16)
    column = jnp.transpose(jnp.broadcast_to(own_ranks, (length, length)))
    first = (column < BUCKET).astype(f32)
    first_ref[...] = first
    for j in range(KV_HEADS):
        at = slice(j * group, (j + 1) * group)
        keys = jnp.concatenate([in_order[:BUCKET, columns(j)], in_order[BUCKET:, columns(j)]], 1)
        keys2_ref[:, 2 * j * HDIM : 2 * (j + 1) * HDIM] = keys
        to = columns(KV_HEADS + j)
        values = jnp.concatenate([in_order[:BUCKET, to], in_order[BUCKET:, to]], 1)
        query = by_bucket(stacked(query_ref, j), first)
        grad = by_bucket(stacked(grad_ref, j), first)
        score = lax.dot_general(keys, query, NT, preferred_element_type=f32) * scale
        heads = range(j * GROUP, (j + 1) * GROUP)
        sink = jnp.concatenate([jnp.broadcast_to(sink_ref[:, h : h + 1], (1, length)) for h in heads], 1)
        top = jnp.maximum(jnp.max(score, axis=0, keepdims=True), sink)
        weight = jnp.exp(score - top)
        sink_weight = jnp.exp(sink - top)
        weight_ref[:, at] = weight
        up = lax.dot_general(values, grad, NT, preferred_element_type=f32)
        up_ref[:, at] = up
        stats_ref[0:1, at] = top
        stats_ref[1:2, at] = jnp.sum(weight, axis=0, keepdims=True) + sink_weight
        stats_ref[2:3, at] = jnp.sum(weight * up, axis=0, keepdims=True)
        stats_ref[3:4, at] = sink_weight


def terms_kernel(
    slots, query_ref, grad_ref, weight_ref, up_ref, stats_ref, packs_ref,
    out_hbm, ds_ref, half_ref, slot_keys_ref, out_ref, rows_ref, sinks_ref, tiles_ref, sem,
):
    length = query_ref.shape[1]
    group = GROUP * length
    padded = -(-slots // 16) * 16
    order = slot_order(slots)
    scale = HDIM**-0.5
    tiles_ref[...] = packs_ref[...].astype(f32)

    def chosen(row):
        part = tiles_ref[pl.ds(row, slots, stride=PACK), :]
        if padded > slots:
            part = jnp.concatenate([part, jnp.zeros((padded - slots, HDIM), f32)], 0)
        return part

    slot_keys = [chosen(j).astype(bf16) for j in range(KV_HEADS)]
    slot_values = [chosen(KV_HEADS + j).astype(bf16) for j in range(KV_HEADS)]
    slot_keys_ref[...] = jnp.concatenate(slot_keys, 1)
    own_marks = (tiles_ref[RANK_ROW : RANK_ROW + 1] >= BUCKET).astype(f32)
    slot_at = iota((padded, length), 0)
    bias = jnp.log(jnp.maximum(chosen(COUNT_ROW), 1.0))
    same = (slot_at < 2) & (chosen(MARK_ROW) == own_marks)
    bias = jnp.where(same | (slot_at >= slots), NEG, bias)
    query = [stacked(query_ref, j) for j in range(KV_HEADS)]
    grad = [stacked(grad_ref, j) for j in range(KV_HEADS)]

    def against(parts, rows):
        return jnp.concatenate(
            [lax.dot_general(part, row, NT, preferred_element_type=f32) for part, row in zip(parts, rows)], 1
        )

    score = against(slot_keys, query) * scale + jnp.concatenate([bias] * HEADS, 1)
    up = against(slot_values, grad)
    pair_top = stats_ref[0:1]
    top = jnp.maximum(pair_top, jnp.max(score, axis=0, keepdims=True))
    weight = jnp.exp(score - top)
    pair_scale = jnp.exp(pair_top - top)
    inverse = 1.0 / (pair_scale * stats_ref[1:2] + jnp.sum(weight, axis=0, keepdims=True))
    pair_scale = pair_scale * inverse
    prob = weight * inverse
    delta = pair_scale * stats_ref[2:3] + jnp.sum(prob * up, axis=0, keepdims=True)
    ds = (prob * (up - delta)).astype(bf16)
    half = prob.astype(bf16)
    ds_ref[length:] = ds
    rows_ref[0:1] = pair_scale
    rows_ref[1:2] = delta
    sink_rows = pair_scale * stats_ref[3:4] * delta
    for h in range(HEADS):
        sinks_ref[h : h + 1] = sink_rows[:, h * length : (h + 1) * length]
    sinks = jnp.sum(sinks_ref[...], axis=1, keepdims=True)
    sinks = jnp.where(iota((HEADS, HDIM), 0) == iota((HEADS, HDIM), 1), -sinks, 0.0)
    sinks = jnp.sum(sinks, axis=0, keepdims=True)
    high = sinks.astype(bf16).astype(f32)
    ends = (high, sinks - high)

    def piece(first, second):
        shape = out_ref.shape[1:]
        upper = jnp.broadcast_to(jnp.concatenate([first, ends[0]], 1), shape)
        lower = jnp.broadcast_to(jnp.concatenate([second, ends[1]], 1), shape)
        return jnp.where(iota(shape, 0) == 0, upper, lower).astype(bf16)

    nothing = jnp.zeros((1, KV_HEADS * HDIM), f32)
    out_ref[...] = jnp.broadcast_to(piece(nothing, nothing)[None], out_ref.shape)
    key_rows, value_rows = (
        jnp.concatenate(
            [
                lax.dot_general(left[:, j * group : (j + 1) * group], right[j], NN, preferred_element_type=f32)
                for j in range(KV_HEADS)
            ],
            1,
        )
        for left, right in ((ds, query), (half, grad))
    )
    key_rows = key_rows * scale
    first = lax.axis_index("dp") * slots
    for slot in range(slots):
        out_ref[first + (lax.axis_index("ctx") ^ order[slot])] = piece(
            key_rows[slot : slot + 1], value_rows[slot : slot + 1]
        )
    copy = pltpu.make_async_copy(out_ref, out_hbm, sem)
    copy.start()

    @pl.loop(0, KV_HEADS)
    def _(j):
        at = pl.ds(pl.multiple_of(j * group, group), group)
        pair_prob = weight_ref[:, at] * rows_ref[0:1, at]
        ds_ref[pl.ds(0, length), at] = (pair_prob * (up_ref[:, at] - rows_ref[1:2, at])).astype(bf16)
        half_ref[:, at] = pair_prob.astype(bf16)

    copy.wait()


def gradient_kernel(
    query_ref, grad_ref, ds_ref, half_ref, slot_keys_ref, keys2_ref, home_ref, first_ref,
    dq_hbm, own_grad_ref, *refs,
):
    far_grad_refs, (dq_ref, sems) = refs[:-2], refs[-2:]
    length = first_ref.shape[0]
    group = GROUP * length
    wide = KV_HEADS * HDIM
    scale = HDIM**-0.5
    mine = jnp.concatenate([first_ref[...]] * GROUP, 0) > 0.5
    sent = []
    grads = [[], []]
    for j in range(KV_HEADS):
        at = slice(j * group, (j + 1) * group)
        slot_keys = slot_keys_ref[:, columns(j)]
        keys = jnp.concatenate(
            [keys2_ref[:, 2 * j * HDIM : 2 * (j + 1) * HDIM], jnp.concatenate([slot_keys, slot_keys], 1)], 0
        )
        dq = lax.dot_general(ds_ref[:, at], keys, TN, preferred_element_type=f32)
        dq = (jnp.where(mine, dq[:, :HDIM], dq[:, HDIM:]) * scale).astype(bf16)
        for g in range(GROUP):
            dq_ref[:, columns(j * GROUP + g)] = dq[g * length : (g + 1) * length]
        to = pl.ds(j * GROUP * HDIM, GROUP * HDIM)
        copy = pltpu.make_async_copy(dq_ref.at[:, to], dq_hbm.at[0, :, to], sems.at[j])
        copy.start()
        sent.append(copy)
        query = by_bucket(stacked(query_ref, j), first_ref[...])
        grad = by_bucket(stacked(grad_ref, j), first_ref[...])
        dk = lax.dot_general(ds_ref[:length, at], query, NN, preferred_element_type=f32) * scale
        dv = lax.dot_general(half_ref[:, at], grad, NN, preferred_element_type=f32)
        for i, part in enumerate((dk, dv)):
            grads[i].append(jnp.concatenate([part[:, :HDIM], part[:, HDIM:]], 0).astype(bf16))
    for i in range(2):
        at = slice(i * wide, (i + 1) * wide)
        back = jnp.dot(home_ref[...], jnp.concatenate(grads[i], 1), preferred_element_type=f32)
        own_grad_ref[:, at] = back[:length]
        for part in range(1):
            far_grad_refs[i * 1 + part][...] = back[length:, part * 512 : (part + 1) * 512].astype(bf16)
    for copy in sent:
        copy.wait()


def last_kernel(slots, meta_ref, own_ref, terms_ref, *refs):
    recv_refs, (dk_ref, dv_ref, sink_ref) = refs[:-3], refs[-3:]
    length = own_ref.shape[0]
    wide = KV_HEADS * HDIM
    ends = jnp.sum(terms_ref[:, :, wide:].astype(f32), axis=0)
    sink_ref[...] = (ends[0:1] + ends[1:2])[:, :HEADS]
    first = lax.axis_index("dp") * slots
    slot = jnp.sum(terms_ref[pl.ds(first, slots), :, :wide].astype(f32), axis=0)
    mine = iota((length, HDIM), 0).astype(f32) == meta_ref[0:1]
    for i, out_ref in enumerate((dk_ref, dv_ref)):
        for j in range(KV_HEADS):
            at = columns(i * KV_HEADS + j)
            total = own_ref[:, at] + recv_refs[(i * KV_HEADS + j) * HDIM // 512][:, columns((i * KV_HEADS + j) % 4)].astype(f32)
            total = total + jnp.where(mine, slot[i : i + 1, columns(j)], 0.0)
            out_ref[0, :, columns(j)] = total.astype(bf16)


def on_device(
    query_rows, key_rows, value_rows, grad_rows, bucket_rank, sample_rows, sample_count, sink_logit
):
    length = query_rows.shape[1]
    wide = KV_HEADS * HDIM
    slots = lax.axis_size("ctx")
    rows = HEADS * HDIM
    token = pl.pallas_call(
        token_kernel,
        out_shape=jax.ShapeDtypeStruct((PACK, length), jnp.int32),
        out_specs=VMEM,
        compiler_params=SMALL,
        cost_estimate=LOADS,
        name="token_lanes",
    )()
    sample_rows, sample_count, token = lax.optimization_barrier((sample_rows, sample_count, token))
    kv, tile, meta = pl.pallas_call(
        pack_kernel,
        out_shape=[
            jax.ShapeDtypeStruct((length, 2 * wide), bf16),
            jax.ShapeDtypeStruct((PACK, HDIM), bf16),
            jax.ShapeDtypeStruct((8, length), f32),
        ],
        in_specs=[SMEM] * 2 + [VMEM] * 4,
        out_specs=[VMEM] * 3,
        compiler_params=SMALL,
        cost_estimate=LOADS,
        name="pack_sample",
    )(sample_rows, sample_count, token, bucket_rank, key_rows, value_rows)

    far_tile = moved(tile, "ctx", 1)
    far_kv = moved(kv, "ctx", 1)
    packs = jnp.concatenate([tile, far_tile], 0)
    by_token = jax.ShapeDtypeStruct((length, rows), f32)
    weight, up, stats, keys2, home, first, same = pl.pallas_call(
        score_kernel,
        out_shape=[
            by_token,
            by_token,
            jax.ShapeDtypeStruct((8, rows), f32),
            jax.ShapeDtypeStruct((length, 2 * wide), bf16),
            jax.ShapeDtypeStruct((2 * length, 2 * length), bf16),
            jax.ShapeDtypeStruct((length, length), f32),
            jax.ShapeDtypeStruct(packs.shape, bf16),
        ],
        in_specs=[VMEM] * 6,
        out_specs=[VMEM] * 7,
        compiler_params=LARGE,
        cost_estimate=pl.CostEstimate(
            flops=8 * length * length * rows, transcendentals=2 * length * rows, bytes_accessed=20 * length * rows
        ),
        name="pair_scores",
    )(query_rows, grad_rows, kv, far_kv, packs, sink_logit[None])
    for offsets in rounds(slots):
        arrived = [moved(packs, "ctx", d) for d in offsets]
        packs = jnp.concatenate([same] + arrived, 0)
        same = packs
    devices = slots * lax.axis_size("dp")
    padded = -(-slots // 16) * 16
    terms, ds, half, slot_keys = pl.pallas_call(
        functools.partial(terms_kernel, slots),
        out_shape=[
            jax.ShapeDtypeStruct((devices, 2, wide + HDIM), bf16),
            jax.ShapeDtypeStruct((length + padded, rows), bf16),
            jax.ShapeDtypeStruct((length, rows), bf16),
            jax.ShapeDtypeStruct((padded, wide), bf16),
        ],
        in_specs=[VMEM] * 6,
        out_specs=[HBM] + [VMEM] * 3,
        scratch_shapes=[
            pltpu.VMEM((devices, 2, wide + HDIM), bf16),
            pltpu.VMEM((8, rows), f32),
            pltpu.VMEM((HEADS, length), f32),
            pltpu.VMEM((slots * PACK, HDIM), f32),
            pltpu.SemaphoreType.DMA,
        ],
        compiler_params=LARGE,
        name="slot_terms",
    )(query_rows, grad_rows, weight, up, stats, packs)
    terms = lax.all_to_all(terms, ("dp", "ctx"), 0, 0, tiled=True)
    dq, own, *far = pl.pallas_call(
        gradient_kernel,
        out_shape=[
            jax.ShapeDtypeStruct((1, length, rows), bf16),
            jax.ShapeDtypeStruct((length, 2 * wide), f32),
        ]
        + [jax.ShapeDtypeStruct((length, 2 * wide // 2), bf16)] * 2,
        in_specs=[VMEM] * 8,
        out_specs=[HBM] + [VMEM] * 3,
        scratch_shapes=[pltpu.VMEM((length, rows), bf16), pltpu.SemaphoreType.DMA((KV_HEADS,))],
        compiler_params=LARGE,
        cost_estimate=pl.CostEstimate(
            flops=12 * length * length * rows, transcendentals=0, bytes_accessed=20 * length * rows
        ),
        name="gradients",
    )(query_rows, grad_rows, ds, half, slot_keys, keys2, home, first)
    recv = [moved(part, "ctx", 1) for part in far]
    dk, dv, sink_grad = pl.pallas_call(
        functools.partial(last_kernel, slots),
        out_shape=[jax.ShapeDtypeStruct((1, length, wide), bf16)] * 2
        + [jax.ShapeDtypeStruct((1, HEADS), f32)],
        in_specs=[VMEM] * 5,
        out_specs=[VMEM] * 3,
        compiler_params=SMALL,
        name="add_up",
    )(meta, own, terms, *recv)
    return dq, dk, dv, sink_grad[0]


def solution(mesh):
    return jax.shard_map(
        on_device,
        mesh=mesh,
        in_specs=(
            P("dp", "ctx", None),
            P("dp", "ctx", None),
            P("dp", "ctx", None),
            P("dp", "ctx", None),
            P("dp", "ctx"),
            P("dp", "ctx"),
            P("dp", "ctx"),
            P(),
        ),
        out_specs=(P("dp", "ctx", None), P("dp", "ctx", None), P("dp", "ctx", None), P()),
        check_vma=False,
    )
```

time: 26.5 us -> 25.8 us (0.974)
  blocking collectives: 12.3 us -> 0 us
  waiting for transfers between devices: 2.83 us -> 8.5 us
  starting transfers between devices: 4.83 us -> 10.2 us
  Pallas kernels: 4.16 us -> 4.75 us
    all_to_all x1 -> x0, blocking collectives: 12.3 us -> none  [on_device(): terms = lax.all_to_all(terms, ('dp', 'ctx'), 0, 0, tiled=True)]
    all_to_all x0 -> x1, starting transfers between devices: none -> 4.93 us  [on_device(): terms = lax.all_to_all(terms, ('dp', 'ctx'), 0, 0, tiled=True)]
    all_to_all x0 -> x1, waiting for transfers between devices: none -> 4.47 us  [on_device(): terms = lax.all_to_all(terms, ('dp', 'ctx'), 0, 0, tiled=True)]
    ppermute x6 -> x7, waiting for transfers between devices: 2.83 us -> 4.03 us  [moved(): lax.ppermute(array, axis, [(i, i ^ apart) for i in range(lax.axis_size(ax...]
    pallas_call x2 -> x3, Pallas kernels: 3.2 us -> 3.8 us  [the longest x1 1.45 us: on_device(): pl.pallas_call(gradient_kernel, out_shape=[jax.ShapeDtypeStruct((1, lengt...]
    ppermute x6 -> x7, starting transfers between devices: 4.83 us -> 5.28 us  [moved(): lax.ppermute(array, axis, [(i, i ^ apart) for i in range(lax.axis_size(ax...]
  transfers between devices with their start and end apart: 6 -> 8, of which waited for: 3 -> 6; matrix products, arithmetic and copies ran while one was open for 0% -> 0% of each run, Pallas kernels for 5% -> 10%
where the time goes in v6:
time: 25.8 us; the launch traced here: 25.6 us
  starting transfers between devices  10.2 us (40%)
  waiting for transfers between devices  8.5 us (33%)
  Pallas kernels  4.75 us (18%)
  between operations  2.11 us (8%)
    ppermute x7, starting transfers between devices, moved(): lax.ppermute(array, axis, [(i, i ^ apart) for i in range(lax.axis_size(ax...  5.28 us
    all_to_all x1, starting transfers between devices, on_device(): terms = lax.all_to_all(terms, ('dp', 'ctx'), 0, 0, tiled=True)  4.93 us
    all_to_all x1, waiting for transfers between devices, on_device(): terms = lax.all_to_all(terms, ('dp', 'ctx'), 0, 0, tiled=True)  4.47 us
    ppermute x7, waiting for transfers between devices, moved(): lax.ppermute(array, axis, [(i, i ^ apart) for i in range(lax.axis_size(ax...  4.03 us
    pallas_call x1, Pallas kernels, on_device(): pl.pallas_call(gradient_kernel, out_shape=[jax.ShapeDtypeStruct((1, lengt...  1.45 us
    pallas_call x1, Pallas kernels, on_device(): pl.pallas_call(functools.partial(terms_kernel, slots), out_shape=[jax.Sha...  1.27 us
    pallas_call x1, Pallas kernels, on_device(): pl.pallas_call(score_kernel, out_shape=[by_token, by_token, jax.ShapeDtyp...  1.07 us
    pallas_call x1, Pallas kernels, on_device(): pl.pallas_call(functools.partial(last_kernel, slots), out_shape=[jax.Shap...  0.8 us
  transfers between devices with their start and end apart: 8, of which 6 were waited for; matrix products, arithmetic and copies ran while one was open for 0% of the time, Pallas kernels for 10%

profile of v6, /device:TPU:0, one launch (start us, length us, event | category | flops | bytes accessed | tf_op | source)
XLA Modules:
  0.0 25.6 jit_solution(5833561496216194896)
XLA Ops:
  0.6 0.0 copy-start.4
  0.6 0.0 copy-start.3
  1.3 0.0 copy-start.5
  2.0 0.0 copy-done.4
  2.0 0.0 copy-done.3
  2.0 0.0 copy-done.5
  2.0 0.0 copy-start
  2.1 0.0 copy-start.1
  2.1 0.2 pack_sample.1
  2.2 0.5 %collective-permute-start = (bf16[128,1024]{1,0:T(8,128)(2,1)S(1)}, bf16[128,1024]{1,0:T(8,128)(2,1)S(1)}, u32[]{:S(2)}, u32[]{:S(2)}) collective-permute-start(bf16[128,1024]{1,0:T(8,128)(2,1)S(1)} %get-tuple-element.31.kv_ref), channel_id=1, source_target_pairs={{0,1},{1,0},{2,3},{3,2},{4,5},{5,4},{6,7},{7,6},{8,9},{9,8},{10,11... | collective-permute-start | bytes 786440 | tf_op jit(solution)/shard_map/ppermute | solution.py:39
  2.7 0.1 collective-permute-start.1
  2.8 1.1 %collective-permute-done.1 = bf16[16,128]{1,0:T(8,128)(2,1)S(1)} collective-permute-done((bf16[16,128]{1,0:T(8,128)(2,1)S(1)}, bf16[16,128]{1,0:T(8,128)(2,1)S(1)}, u32[]{:S(2)}, u32[]{:S(2)}) %collective-permute-start.1) | collective-permute-done | bytes 4128 | tf_op jit(solution)/shard_map/ppermute | solution.py:39
  3.9 0.0 copy-start.2
  3.9 3.6 %collective-permute-start.4 = (bf16[32,128]{1,0:T(8,128)(2,1)S(1)}, bf16[32,128]{1,0:T(8,128)(2,1)S(1)}, u32[]{:S(2)}, u32[]{:S(2)}) collective-permute-start(bf16[32,128]{1,0:T(8,128)(2,1)S(1)} %constant_dynamic-update-slice_fusion.packs_ref), channel_id=1, source_target_pairs={{0,7},{1,6},{2,5},{3,4},{4,3},{5,2},{6,1},{7,0},{8,15},{9,14},{10,... | collective-permute-start | bytes 24584 | tf_op jit(solution)/shard_map/ppermute | solution.py:39
  7.4 0.5 %collective-permute-start.3 = (bf16[32,128]{1,0:T(8,128)(2,1)S(1)}, bf16[32,128]{1,0:T(8,128)(2,1)S(1)}, u32[]{:S(2)}, u32[]{:S(2)}) collective-permute-start(bf16[32,128]{1,0:T(8,128)(2,1)S(1)} %constant_dynamic-update-slice_fusion.packs_ref), channel_id=1, source_target_pairs={{0,5},{1,4},{2,7},{3,6},{4,1},{5,0},{6,3},{7,2},{8,13},{9,12},{10,... | collective-permute-start | bytes 24584 | tf_op jit(solution)/shard_map/ppermute | solution.py:39
  7.9 0.1 collective-permute-start.2
  8.0 0.0 collective-permute-done.far_ref
  8.0 0.0 copy-done
  8.0 0.0 copy-done.1
  8.1 0.0 copy-done.2
  8.1 1.1 %pair_scores.1 = (f32[128,2048]{1,0:T(8,128)S(1)}, f32[128,2048]{1,0:T(8,128)S(1)}, f32[8,2048]{1,0:T(8,128)S(1)}, bf16[128,1024]{1,0:T(8,128)(2,1)S(1)}, bf16[2...) custom-call(bf16[1,128,2048]{2,1,0:T(8,128)(2,1)S(1)} %copy-done, ...), custom_call_target="tpu_custom_call" | custom-call | flops 268435456 | bytes 5242880 | tf_op jit(solution)/shard_map/pair_scores/pallas_call | solution.py:336
  9.1 0.0 collective-permute-done.4
  9.1 1.4 %collective-permute-done.3 = bf16[32,128]{1,0:T(8,128)(2,1)S(1)} collective-permute-done((bf16[32,128]{1,0:T(8,128)(2,1)S(1)}, bf16[32,128]{1,0:T(8,128)(2,1)S(1)}, u32[]{:S(2)}, u32[]{:S(2)}) %collective-permute-start.3) | collective-permute-done | bytes 8224 | tf_op jit(solution)/shard_map/ppermute | solution.py:39
  10.5 0.5 %collective-permute-done.2 = bf16[32,128]{1,0:T(8,128)(2,1)S(1)} collective-permute-done((bf16[32,128]{1,0:T(8,128)(2,1)S(1)}, bf16[32,128]{1,0:T(8,128)(2,1)S(1)}, u32[]{:S(2)}, u32[]{:S(2)}) %collective-permute-start.2) | collective-permute-done | bytes 8224 | tf_op jit(solution)/shard_map/ppermute | solution.py:39
  11.0 1.3 %slot_terms.1 = (bf16[32,2,640]{2,1,0:T(2,128)(2,1)}, bf16[144,2048]{1,0:T(8,128)(2,1)S(1)}, bf16[128,2048]{1,0:T(8,128)(2,1)S(1)}, bf16[16,512]{1,0:T(8,128)(2,1)S(1)}) custom-call(bf16[1,128,2048]{2,1,0:T(8,128)(2,1)S(1)} %copy-done, bf16[1,128,2048]{2,1,0:T(8,128)(2,1)S(1)} %copy-done.1, f32[128,2048]{1,0:T(8,128)S(1)} %get-tuple-element.33.weight_ref, ...), custom_call_target="tpu_custom_call" | custom-call | tf_op jit(solution)/shard_map/slot_terms/pallas_call | solution.py:361
  12.3 4.9 %all-to-all-start = ((bf16[32,2,640]{2,1,0:T(2,128)(2,1)}), bf16[32,2,640]{2,1,0:T(2,128)(2,1)S(1)}, u32[]{:S(2)}, u32[]{:S(2)}) async-start(bf16[32,2,640]{2,1,0:T(2,128)(2,1)} %get-tuple-element.46), calls=%async_computation | async-start | bytes 163840 | tf_op jit(solution)/shard_map/all_to_all | solution.py:381
  17.2 1.5 %gradients.1 = (bf16[1,128,2048]{2,1,0:T(8,128)(2,1)}, f32[128,1024]{1,0:T(8,128)S(1)}, bf16[128,512]{1,0:T(8,128)(2,1)S(1)}, bf16[128,512]{1,0:T(8,128)(2,1)S(1)}) custom-call(bf16[1,128,2048]{2,1,0:T(8,128)(2,1)S(1)} %copy-done, bf16[1,128,2048]{2,1,0:T(8,128)(2,1)S(1)} %copy-done.1, bf16[144,2048]{1,0:T(8,128)(2,1)S(1)} %get-tuple-element.37.ds_ref, ...), custom_call_target="tpu_custom_call" | custom-call | flops 402653184 | bytes 5242880 | tf_op jit(solution)/shard_map/gradients/pallas_call | solution.py:382
  18.7 0.3 %collective-permute-start.5 = (bf16[128,512]{1,0:T(8,128)(2,1)S(1)}, bf16[128,512]{1,0:T(8,128)(2,1)S(1)}, u32[]{:S(2)}, u32[]{:S(2)}) collective-permute-start(bf16[128,512]{1,0:T(8,128)(2,1)S(1)} %get-tuple-element.47), channel_id=1, source_target_pairs={{0,1},{1,0},{2,3},{3,2},{4,5},{5,4},{6,7},{7,6},{8,9},{9,8},{10,11... | collective-permute-start | bytes 393224 | tf_op jit(solution)/shard_map/ppermute | solution.py:39
  19.0 0.3 %collective-permute-start.6 = (bf16[128,512]{1,0:T(8,128)(2,1)S(1)}, bf16[128,512]{1,0:T(8,128)(2,1)S(1)}, u32[]{:S(2)}, u32[]{:S(2)}) collective-permute-start(bf16[128,512]{1,0:T(8,128)(2,1)S(1)} %get-tuple-element.48), channel_id=1, source_target_pairs={{0,1},{1,0},{2,3},{3,2},{4,5},{5,4},{6,7},{7,6},{8,9},{9,8},{10,11... | collective-permute-start | bytes 393224 | tf_op jit(solution)/shard_map/ppermute | solution.py:39
  19.2 0.8 %collective-permute-done.5.refs_0_ = bf16[128,512]{1,0:T(8,128)(2,1)S(1)} collective-permute-done((bf16[128,512]{1,0:T(8,128)(2,1)S(1)}, bf16[128,512]{1,0:T(8,128)(2,1)S(1)}, u32[]{:S(2)}, u32[]{:S(2)}) %collective-permute-start.5) | collective-permute-done | bytes 131104 | tf_op jit(solution)/shard_map/ppermute | solution.py:39
  20.1 0.3 collective-permute-done.6.refs_1_
  20.3 4.5 %all-to-all-done.terms_ref = bf16[32,2,640]{2,1,0:T(2,128)(2,1)S(1)} async-done(((bf16[32,2,640]{2,1,0:T(2,128)(2,1)}), bf16[32,2,640]{2,1,0:T(2,128)(2,1)S(1)}, u32[]{:S(2)}, u32[]{:S(2)}) %all-to-all-start) | async-done | bytes 81952 | tf_op jit(solution)/shard_map/all_to_all | solution.py:381
  24.8 0.8 %add_up.1 = (bf16[1,128,512]{2,1,0:T(8,128)(2,1)}, bf16[1,128,512]{2,1,0:T(8,128)(2,1)}, f32[1,16]{1,0:T(1,128)}) custom-call(f32[8,128]{1,0:T(8,128)S(1)} %get-tuple-element.44.meta_ref, f32[128,1024]{1,0:T(8,128)S(1)} %get-tuple-element.45.own_ref, bf16[32,2,640]{2,1,0:T(2,128)(2,1)S(1)} %all-to-all-done.terms_ref, ...), custom_call_target="tpu_custom_call" | custom-call | tf_op jit(solution)/shard_map/add_up/pallas_call | solution.py:399
  (4 shorter events, 0.0 us)
Async XLA Ops:
  0.6 1.4 %copy-start.4 = (bf16[1,128,512]{2,1,0:T(8,128)(2,1)S(1)}, bf16[1,128,512]{2,1,0:T(8,128)(2,1)}, u32[]{:S(2)}) copy-start(bf16[1,128,512]{2,1,0:T(8,128)(2,1)} %values_ref.1) | copy-start | bytes 393220
  0.6 1.4 %copy-start.3 = (bf16[1,128,512]{2,1,0:T(8,128)(2,1)S(1)}, bf16[1,128,512]{2,1,0:T(8,128)(2,1)}, u32[]{:S(2)}) copy-start(bf16[1,128,512]{2,1,0:T(8,128)(2,1)} %keys_ref.1) | copy-start | bytes 393220
  1.3 0.7 %copy-start.5 = (s32[1,128]{1,0:T(1,128)S(1)}, s32[1,128]{1,0:T(1,128)}, u32[]{:S(2)}) copy-start(s32[1,128]{1,0:T(1,128)} %rank_ref.1) | copy-start | bytes 1540
  2.0 6.0 %copy-start = (bf16[1,128,2048]{2,1,0:T(8,128)(2,1)S(1)}, bf16[1,128,2048]{2,1,0:T(8,128)(2,1)}, u32[]{:S(2)}) copy-start(bf16[1,128,2048]{2,1,0:T(8,128)(2,1)} %query_ref.5) | copy-start | bytes 1572868
  2.1 6.0 %copy-start.1 = (bf16[1,128,2048]{2,1,0:T(8,128)(2,1)S(1)}, bf16[1,128,2048]{2,1,0:T(8,128)(2,1)}, u32[]{:S(2)}) copy-start(bf16[1,128,2048]{2,1,0:T(8,128)(2,1)} %grad_ref.5) | copy-start | bytes 1572868
  2.2 5.8 %collective-permute-start = (bf16[128,1024]{1,0:T(8,128)(2,1)S(1)}, bf16[128,1024]{1,0:T(8,128)(2,1)S(1)}, u32[]{:S(2)}, u32[]{:S(2)}) collective-permute-start(bf16[128,1024]{1,0:T(8,128)(2,1)S(1)} %get-tuple-element.31.kv_ref), channel_id=1, source_target_pairs={{0,1},{1,0},{2,3},{3,2},{4,5},{5,4},{6,7},{7,6},{8,9},{9,8},{10,11... | collective-permute-start | bytes 786440 | tf_op jit(solution)/shard_map/ppermute | solution.py:39
  2.7 1.2 %collective-permute-start.1 = (bf16[16,128]{1,0:T(8,128)(2,1)S(1)}, bf16[16,128]{1,0:T(8,128)(2,1)S(1)}, u32[]{:S(2)}, u32[]{:S(2)}) collective-permute-start(bf16[16,128]{1,0:T(8,128)(2,1)S(1)} %get-tuple-element.32), channel_id=1, source_target_pairs={{0,1},{1,0},{2,3},{3,2},{4,5},{5,4},{6,7},{7,6},{8,9},{9,8},{10,11... | collective-permute-start | bytes 12296 | tf_op jit(solution)/shard_map/ppermute | solution.py:39
  3.9 4.2 %copy-start.2 = (f32[16]{0:T(128)S(1)}, f32[16]{0:T(128)}, u32[]{:S(2)}) copy-start(f32[16]{0:T(128)} %param.15) | copy-start | bytes 196
  3.9 5.3 %collective-permute-start.4 = (bf16[32,128]{1,0:T(8,128)(2,1)S(1)}, bf16[32,128]{1,0:T(8,128)(2,1)S(1)}, u32[]{:S(2)}, u32[]{:S(2)}) collective-permute-start(bf16[32,128]{1,0:T(8,128)(2,1)S(1)} %constant_dynamic-update-slice_fusion.packs_ref), channel_id=1, source_target_pairs={{0,7},{1,6},{2,5},{3,4},{4,3},{5,2},{6,1},{7,0},{8,15},{9,14},{10,... | collective-permute-start | bytes 24584 | tf_op jit(solution)/shard_map/ppermute | solution.py:39
  7.4 3.1 %collective-permute-start.3 = (bf16[32,128]{1,0:T(8,128)(2,1)S(1)}, bf16[32,128]{1,0:T(8,128)(2,1)S(1)}, u32[]{:S(2)}, u32[]{:S(2)}) collective-permute-start(bf16[32,128]{1,0:T(8,128)(2,1)S(1)} %constant_dynamic-update-slice_fusion.packs_ref), channel_id=1, source_target_pairs={{0,5},{1,4},{2,7},{3,6},{4,1},{5,0},{6,3},{7,2},{8,13},{9,12},{10,... | collective-permute-start | bytes 24584 | tf_op jit(solution)/shard_map/ppermute | solution.py:39
  7.9 3.1 %collective-permute-start.2 = (bf16[32,128]{1,0:T(8,128)(2,1)S(1)}, bf16[32,128]{1,0:T(8,128)(2,1)S(1)}, u32[]{:S(2)}, u32[]{:S(2)}) collective-permute-start(bf16[32,128]{1,0:T(8,128)(2,1)S(1)} %constant_dynamic-update-slice_fusion.packs_ref), channel_id=1, source_target_pairs={{0,3},{1,2},{2,1},{3,0},{4,7},{5,6},{6,5},{7,4},{8,11},{9,10},{10,... | collective-permute-start | bytes 24584 | tf_op jit(solution)/shard_map/ppermute | solution.py:39
  12.3 12.5 %all-to-all-start = ((bf16[32,2,640]{2,1,0:T(2,128)(2,1)}), bf16[32,2,640]{2,1,0:T(2,128)(2,1)S(1)}, u32[]{:S(2)}, u32[]{:S(2)}) async-start(bf16[32,2,640]{2,1,0:T(2,128)(2,1)} %get-tuple-element.46), calls=%async_computation | async-start | bytes 163840 | tf_op jit(solution)/shard_map/all_to_all | solution.py:381
  18.7 1.4 %collective-permute-start.5 = (bf16[128,512]{1,0:T(8,128)(2,1)S(1)}, bf16[128,512]{1,0:T(8,128)(2,1)S(1)}, u32[]{:S(2)}, u32[]{:S(2)}) collective-permute-start(bf16[128,512]{1,0:T(8,128)(2,1)S(1)} %get-tuple-element.47), channel_id=1, source_target_pairs={{0,1},{1,0},{2,3},{3,2},{4,5},{5,4},{6,7},{7,6},{8,9},{9,8},{10,11... | collective-permute-start | bytes 393224 | tf_op jit(solution)/shard_map/ppermute | solution.py:39
  19.0 1.3 %collective-permute-start.6 = (bf16[128,512]{1,0:T(8,128)(2,1)S(1)}, bf16[128,512]{1,0:T(8,128)(2,1)S(1)}, u32[]{:S(2)}, u32[]{:S(2)}) collective-permute-start(bf16[128,512]{1,0:T(8,128)(2,1)S(1)} %get-tuple-element.48), channel_id=1, source_target_pairs={{0,1},{1,0},{2,3},{3,2},{4,5},{5,4},{6,7},{7,6},{8,9},{9,8},{10,11... | collective-permute-start | bytes 393224 | tf_op jit(solution)/shard_map/ppermute | solution.py:39

commit v7 on v6

--- a/solution.py
+++ b/solution.py
@@ -271,32 +271,43 @@
         dk = lax.dot_general(ds_ref[:length, at], query, NN, preferred_element_type=f32) * scale
         dv = lax.dot_general(half_ref[:, at], grad, NN, preferred_element_type=f32)
         for i, part in enumerate((dk, dv)):
-            grads[i].append(jnp.concatenate([part[:, :HDIM], part[:, HDIM:]], 0).astype(bf16))
+            grads[i].append(jnp.concatenate([part[:, :HDIM], part[:, HDIM:]], 0))
     for i in range(2):
-        at = slice(i * wide, (i + 1) * wide)
-        back = jnp.dot(home_ref[...], jnp.concatenate(grads[i], 1), preferred_element_type=f32)
-        own_grad_ref[:, at] = back[:length]
-        for part in range(1):
-            far_grad_refs[i * 1 + part][...] = back[length:, part * 512 : (part + 1) * 512].astype(bf16)
+        in_order = jnp.concatenate(grads[i], 1)
+        high = in_order.astype(bf16)
+        low = (in_order - high.astype(f32)).astype(bf16)
+        back = jnp.dot(home_ref[...], high, preferred_element_type=f32)
+        rest = jnp.dot(home_ref[:length], low, preferred_element_type=f32)
+        own_grad_ref[:, i * wide : (i + 1) * wide] = back[:length] + rest
+        far_grad_refs[i][...] = back[length:].astype(bf16)
     for copy in sent:
         copy.wait()
 
 
-def last_kernel(slots, meta_ref, own_ref, terms_ref, *refs):
-    recv_refs, (dk_ref, dv_ref, sink_ref) = refs[:-3], refs[-3:]
+def total_kernel(meta_ref, own_ref, key_recv_ref, value_recv_ref, total_ref, row_ref):
     length = own_ref.shape[0]
+    mine = iota((length, HDIM), 0).astype(f32) == meta_ref[0:1]
+    for i, recv_ref in enumerate((key_recv_ref, value_recv_ref)):
+        for j in range(KV_HEADS):
+            at = columns(i * KV_HEADS + j)
+            total = own_ref[:, at] + recv_ref[:, columns(j)].astype(f32)
+            total_ref[:, at] = total.astype(bf16)
+            row = jnp.sum(jnp.where(mine, total, 0.0), axis=0, keepdims=True)
+            row_ref[i : i + 1, columns(j)] = row
+
+
+def last_kernel(slots, meta_ref, total_ref, row_ref, terms_ref, dk_ref, dv_ref, sink_ref):
+    length = total_ref.shape[0]
     wide = KV_HEADS * HDIM
     ends = jnp.sum(terms_ref[:, :, wide:].astype(f32), axis=0)
     sink_ref[...] = (ends[0:1] + ends[1:2])[:, :HEADS]
     first = lax.axis_index("dp") * slots
-    slot = jnp.sum(terms_ref[pl.ds(first, slots), :, :wide].astype(f32), axis=0)
+    row = row_ref[0:2] + jnp.sum(terms_ref[pl.ds(first, slots), :, :wide].astype(f32), axis=0)
     mine = iota((length, HDIM), 0).astype(f32) == meta_ref[0:1]
     for i, out_ref in enumerate((dk_ref, dv_ref)):
         for j in range(KV_HEADS):
-            at = columns(i * KV_HEADS + j)
-            total = own_ref[:, at] + recv_refs[(i * KV_HEADS + j) * HDIM // 512][:, columns((i * KV_HEADS + j) % 4)].astype(f32)
-            total = total + jnp.where(mine, slot[i : i + 1, columns(j)], 0.0)
-            out_ref[0, :, columns(j)] = total.astype(bf16)
+            total = total_ref[:, columns(i * KV_HEADS + j)].astype(f32)
+            out_ref[0, :, columns(j)] = jnp.where(mine, row[i : i + 1, columns(j)], total).astype(bf16)
 
 
 def on_device(
@@ -396,15 +407,26 @@
         name="gradients",
     )(query_rows, grad_rows, ds, half, slot_keys, keys2, home, first)
     recv = [moved(part, "ctx", 1) for part in far]
+    total, sampled = pl.pallas_call(
+        total_kernel,
+        out_shape=[
+            jax.ShapeDtypeStruct((length, 2 * wide), bf16),
+            jax.ShapeDtypeStruct((8, wide), f32),
+        ],
+        in_specs=[VMEM] * 4,
+        out_specs=[VMEM] * 2,
+        compiler_params=SMALL,
+        name="pair_total",
+    )(meta, own, *recv)
     dk, dv, sink_grad = pl.pallas_call(
         functools.partial(last_kernel, slots),
         out_shape=[jax.ShapeDtypeStruct((1, length, wide), bf16)] * 2
         + [jax.ShapeDtypeStruct((1, HEADS), f32)],
-        in_specs=[VMEM] * 5,
+        in_specs=[VMEM] * 4,
         out_specs=[VMEM] * 3,
         compiler_params=SMALL,
         name="add_up",
-    )(meta, own, terms, *recv)
+    )(meta, total, sampled, terms)
     return dq, dk, dv, sink_grad[0]
 
 

time: 25.8 us -> 25.8 us (level)
  no operation moved by 1% of the time
where the time goes in v7:
time: 25.8 us; the launch traced here: 25.6 us
  starting transfers between devices  10.2 us (40%)
  waiting for transfers between devices  8.38 us (32%)
  Pallas kernels  4.84 us (19%)
  between operations  2.11 us (8%)
    ppermute x7, starting transfers between devices, moved(): lax.ppermute(array, axis, [(i, i ^ apart) for i in range(lax.axis_size(ax...  5.28 us
    all_to_all x1, starting transfers between devices, on_device(): terms = lax.all_to_all(terms, ('dp', 'ctx'), 0, 0, tiled=True)  4.93 us
    all_to_all x1, waiting for transfers between devices, on_device(): terms = lax.all_to_all(terms, ('dp', 'ctx'), 0, 0, tiled=True)  4.35 us
    ppermute x7, waiting for transfers between devices, moved(): lax.ppermute(array, axis, [(i, i ^ apart) for i in range(lax.axis_size(ax...  4.02 us
    pallas_call x1, Pallas kernels, on_device(): pl.pallas_call(gradient_kernel, out_shape=[jax.ShapeDtypeStruct((1, lengt...  1.46 us
    pallas_call x1, Pallas kernels, on_device(): pl.pallas_call(functools.partial(terms_kernel, slots), out_shape=[jax.Sha...  1.27 us
    pallas_call x1, Pallas kernels, on_device(): pl.pallas_call(score_kernel, out_shape=[by_token, by_token, jax.ShapeDtyp...  1.07 us
    pallas_call x1, Pallas kernels, on_device(): pl.pallas_call(functools.partial(last_kernel, slots), out_shape=[jax.Shap...  0.77 us
  transfers between devices with their start and end apart: 8, of which 6 were waited for; matrix products, arithmetic and copies ran while one was open for 0% of the time, Pallas kernels for 10%

profile of v7, /device:TPU:0, one launch (start us, length us, event | category | flops | bytes accessed | tf_op | source)
XLA Modules:
  0.0 25.6 jit_solution(14582569059606017828)
XLA Ops:
  0.6 0.0 copy-start.4
  0.6 0.0 copy-start.3
  1.3 0.0 copy-start.5
  2.0 0.0 copy-done.4
  2.0 0.0 copy-done.3
  2.0 0.0 copy-done.5
  2.0 0.0 copy-start
  2.1 0.0 copy-start.1
  2.1 0.2 pack_sample.1
  2.2 0.5 %collective-permute-start = (bf16[128,1024]{1,0:T(8,128)(2,1)S(1)}, bf16[128,1024]{1,0:T(8,128)(2,1)S(1)}, u32[]{:S(2)}, u32[]{:S(2)}) collective-permute-start(bf16[128,1024]{1,0:T(8,128)(2,1)S(1)} %get-tuple-element.33.kv_ref), channel_id=1, source_target_pairs={{0,1},{1,0},{2,3},{3,2},{4,5},{5,4},{6,7},{7,6},{8,9},{9,8},{10,11... | collective-permute-start | bytes 786440 | tf_op jit(solution)/shard_map/ppermute | solution.py:39
  2.7 0.1 collective-permute-start.1
  2.8 1.1 %collective-permute-done.1 = bf16[16,128]{1,0:T(8,128)(2,1)S(1)} collective-permute-done((bf16[16,128]{1,0:T(8,128)(2,1)S(1)}, bf16[16,128]{1,0:T(8,128)(2,1)S(1)}, u32[]{:S(2)}, u32[]{:S(2)}) %collective-permute-start.1) | collective-permute-done | bytes 4128 | tf_op jit(solution)/shard_map/ppermute | solution.py:39
  3.9 0.0 copy-start.2
  3.9 3.6 %collective-permute-start.4 = (bf16[32,128]{1,0:T(8,128)(2,1)S(1)}, bf16[32,128]{1,0:T(8,128)(2,1)S(1)}, u32[]{:S(2)}, u32[]{:S(2)}) collective-permute-start(bf16[32,128]{1,0:T(8,128)(2,1)S(1)} %constant_dynamic-update-slice_fusion.packs_ref), channel_id=1, source_target_pairs={{0,7},{1,6},{2,5},{3,4},{4,3},{5,2},{6,1},{7,0},{8,15},{9,14},{10,... | collective-permute-start | bytes 24584 | tf_op jit(solution)/shard_map/ppermute | solution.py:39
  7.4 0.5 %collective-permute-start.3 = (bf16[32,128]{1,0:T(8,128)(2,1)S(1)}, bf16[32,128]{1,0:T(8,128)(2,1)S(1)}, u32[]{:S(2)}, u32[]{:S(2)}) collective-permute-start(bf16[32,128]{1,0:T(8,128)(2,1)S(1)} %constant_dynamic-update-slice_fusion.packs_ref), channel_id=1, source_target_pairs={{0,5},{1,4},{2,7},{3,6},{4,1},{5,0},{6,3},{7,2},{8,13},{9,12},{10,... | collective-permute-start | bytes 24584 | tf_op jit(solution)/shard_map/ppermute | solution.py:39
  7.9 0.1 collective-permute-start.2
  8.0 0.0 collective-permute-done.far_ref
  8.0 0.0 copy-done
  8.0 0.0 copy-done.1
  8.1 0.0 copy-done.2
  8.1 1.1 %pair_scores.1 = (f32[128,2048]{1,0:T(8,128)S(1)}, f32[128,2048]{1,0:T(8,128)S(1)}, f32[8,2048]{1,0:T(8,128)S(1)}, bf16[128,1024]{1,0:T(8,128)(2,1)S(1)}, bf16[2...) custom-call(bf16[1,128,2048]{2,1,0:T(8,128)(2,1)S(1)} %copy-done, ...), custom_call_target="tpu_custom_call" | custom-call | flops 268435456 | bytes 5242880 | tf_op jit(solution)/shard_map/pair_scores/pallas_call | solution.py:347
  9.1 0.0 collective-permute-done.4
  9.1 1.4 %collective-permute-done.3 = bf16[32,128]{1,0:T(8,128)(2,1)S(1)} collective-permute-done((bf16[32,128]{1,0:T(8,128)(2,1)S(1)}, bf16[32,128]{1,0:T(8,128)(2,1)S(1)}, u32[]{:S(2)}, u32[]{:S(2)}) %collective-permute-start.3) | collective-permute-done | bytes 8224 | tf_op jit(solution)/shard_map/ppermute | solution.py:39
  10.5 0.5 %collective-permute-done.2 = bf16[32,128]{1,0:T(8,128)(2,1)S(1)} collective-permute-done((bf16[32,128]{1,0:T(8,128)(2,1)S(1)}, bf16[32,128]{1,0:T(8,128)(2,1)S(1)}, u32[]{:S(2)}, u32[]{:S(2)}) %collective-permute-start.2) | collective-permute-done | bytes 8224 | tf_op jit(solution)/shard_map/ppermute | solution.py:39
  11.0 1.3 %slot_terms.1 = (bf16[32,2,640]{2,1,0:T(2,128)(2,1)}, bf16[144,2048]{1,0:T(8,128)(2,1)S(1)}, bf16[128,2048]{1,0:T(8,128)(2,1)S(1)}, bf16[16,512]{1,0:T(8,128)(2,1)S(1)}) custom-call(bf16[1,128,2048]{2,1,0:T(8,128)(2,1)S(1)} %copy-done, bf16[1,128,2048]{2,1,0:T(8,128)(2,1)S(1)} %copy-done.1, f32[128,2048]{1,0:T(8,128)S(1)} %get-tuple-element.35.weight_ref, ...), custom_call_target="tpu_custom_call" | custom-call | tf_op jit(solution)/shard_map/slot_terms/pallas_call | solution.py:372
  12.3 4.9 %all-to-all-start = ((bf16[32,2,640]{2,1,0:T(2,128)(2,1)}), bf16[32,2,640]{2,1,0:T(2,128)(2,1)S(1)}, u32[]{:S(2)}, u32[]{:S(2)}) async-start(bf16[32,2,640]{2,1,0:T(2,128)(2,1)} %get-tuple-element.52), calls=%async_computation | async-start | bytes 163840 | tf_op jit(solution)/shard_map/all_to_all | solution.py:392
  17.2 1.5 %gradients.1 = (bf16[1,128,2048]{2,1,0:T(8,128)(2,1)}, f32[128,1024]{1,0:T(8,128)S(1)}, bf16[128,512]{1,0:T(8,128)(2,1)S(1)}, bf16[128,512]{1,0:T(8,128)(2,1)S(1)}) custom-call(bf16[1,128,2048]{2,1,0:T(8,128)(2,1)S(1)} %copy-done, bf16[1,128,2048]{2,1,0:T(8,128)(2,1)S(1)} %copy-done.1, bf16[144,2048]{1,0:T(8,128)(2,1)S(1)} %get-tuple-element.39.ds_ref, ...), custom_call_target="tpu_custom_call" | custom-call | flops 402653184 | bytes 5242880 | tf_op jit(solution)/shard_map/gradients/pallas_call | solution.py:393
  18.7 0.3 %collective-permute-start.5 = (bf16[128,512]{1,0:T(8,128)(2,1)S(1)}, bf16[128,512]{1,0:T(8,128)(2,1)S(1)}, u32[]{:S(2)}, u32[]{:S(2)}) collective-permute-start(bf16[128,512]{1,0:T(8,128)(2,1)S(1)} %get-tuple-element.48), channel_id=1, source_target_pairs={{0,1},{1,0},{2,3},{3,2},{4,5},{5,4},{6,7},{7,6},{8,9},{9,8},{10,11... | collective-permute-start | bytes 393224 | tf_op jit(solution)/shard_map/ppermute | solution.py:39
  19.0 0.3 %collective-permute-start.6 = (bf16[128,512]{1,0:T(8,128)(2,1)S(1)}, bf16[128,512]{1,0:T(8,128)(2,1)S(1)}, u32[]{:S(2)}, u32[]{:S(2)}) collective-permute-start(bf16[128,512]{1,0:T(8,128)(2,1)S(1)} %get-tuple-element.49), channel_id=1, source_target_pairs={{0,1},{1,0},{2,3},{3,2},{4,5},{5,4},{6,7},{7,6},{8,9},{9,8},{10,11... | collective-permute-start | bytes 393224 | tf_op jit(solution)/shard_map/ppermute | solution.py:39
  19.3 0.8 %collective-permute-done.5.key_recv_ref = bf16[128,512]{1,0:T(8,128)(2,1)S(1)} collective-permute-done((bf16[128,512]{1,0:T(8,128)(2,1)S(1)}, bf16[128,512]{1,0:T(8,128)(2,1)S(1)}, u32[]{:S(2)}, u32[]{:S(2)}) %collective-permute-start.5) | collective-permute-done | bytes 131104 | tf_op jit(solution)/shard_map/ppermute | solution.py:39
  20.1 0.3 collective-permute-done.6.value_recv_ref
  20.3 0.1 pair_total.1
  20.5 4.4 %all-to-all-done.terms_ref = bf16[32,2,640]{2,1,0:T(2,128)(2,1)S(1)} async-done(((bf16[32,2,640]{2,1,0:T(2,128)(2,1)}), bf16[32,2,640]{2,1,0:T(2,128)(2,1)S(1)}, u32[]{:S(2)}, u32[]{:S(2)}) %all-to-all-start) | async-done | bytes 81952 | tf_op jit(solution)/shard_map/all_to_all | solution.py:392
  24.8 0.8 %add_up.1 = (bf16[1,128,512]{2,1,0:T(8,128)(2,1)}, bf16[1,128,512]{2,1,0:T(8,128)(2,1)}, f32[1,16]{1,0:T(1,128)}) custom-call(f32[8,128]{1,0:T(8,128)S(1)} %get-tuple-element.46.meta_ref, bf16[128,1024]{1,0:T(8,128)(2,1)S(1)} %get-tuple-element.50.total_ref, f32[8,512]{1,0:T(8,128)S(1)} %get-tuple-element.51.row_ref, ...), custom_call_target="tpu_custom_call" | custom-call | tf_op jit(solution)/shard_map/add_up/pallas_call | solution.py:421
  (4 shorter events, 0.0 us)
Async XLA Ops:
  0.6 1.4 %copy-start.4 = (bf16[1,128,512]{2,1,0:T(8,128)(2,1)S(1)}, bf16[1,128,512]{2,1,0:T(8,128)(2,1)}, u32[]{:S(2)}) copy-start(bf16[1,128,512]{2,1,0:T(8,128)(2,1)} %values_ref.1) | copy-start | bytes 393220
  0.6 1.4 %copy-start.3 = (bf16[1,128,512]{2,1,0:T(8,128)(2,1)S(1)}, bf16[1,128,512]{2,1,0:T(8,128)(2,1)}, u32[]{:S(2)}) copy-start(bf16[1,128,512]{2,1,0:T(8,128)(2,1)} %keys_ref.1) | copy-start | bytes 393220
  1.3 0.7 %copy-start.5 = (s32[1,128]{1,0:T(1,128)S(1)}, s32[1,128]{1,0:T(1,128)}, u32[]{:S(2)}) copy-start(s32[1,128]{1,0:T(1,128)} %rank_ref.1) | copy-start | bytes 1540
  2.0 6.0 %copy-start = (bf16[1,128,2048]{2,1,0:T(8,128)(2,1)S(1)}, bf16[1,128,2048]{2,1,0:T(8,128)(2,1)}, u32[]{:S(2)}) copy-start(bf16[1,128,2048]{2,1,0:T(8,128)(2,1)} %query_ref.5) | copy-start | bytes 1572868
  2.1 6.0 %copy-start.1 = (bf16[1,128,2048]{2,1,0:T(8,128)(2,1)S(1)}, bf16[1,128,2048]{2,1,0:T(8,128)(2,1)}, u32[]{:S(2)}) copy-start(bf16[1,128,2048]{2,1,0:T(8,128)(2,1)} %grad_ref.5) | copy-start | bytes 1572868
  2.2 5.8 %collective-permute-start = (bf16[128,1024]{1,0:T(8,128)(2,1)S(1)}, bf16[128,1024]{1,0:T(8,128)(2,1)S(1)}, u32[]{:S(2)}, u32[]{:S(2)}) collective-permute-start(bf16[128,1024]{1,0:T(8,128)(2,1)S(1)} %get-tuple-element.33.kv_ref), channel_id=1, source_target_pairs={{0,1},{1,0},{2,3},{3,2},{4,5},{5,4},{6,7},{7,6},{8,9},{9,8},{10,11... | collective-permute-start | bytes 786440 | tf_op jit(solution)/shard_map/ppermute | solution.py:39
  2.7 1.2 %collective-permute-start.1 = (bf16[16,128]{1,0:T(8,128)(2,1)S(1)}, bf16[16,128]{1,0:T(8,128)(2,1)S(1)}, u32[]{:S(2)}, u32[]{:S(2)}) collective-permute-start(bf16[16,128]{1,0:T(8,128)(2,1)S(1)} %get-tuple-element.34), channel_id=1, source_target_pairs={{0,1},{1,0},{2,3},{3,2},{4,5},{5,4},{6,7},{7,6},{8,9},{9,8},{10,11... | collective-permute-start | bytes 12296 | tf_op jit(solution)/shard_map/ppermute | solution.py:39
  3.9 4.2 %copy-start.2 = (f32[16]{0:T(128)S(1)}, f32[16]{0:T(128)}, u32[]{:S(2)}) copy-start(f32[16]{0:T(128)} %param.15) | copy-start | bytes 196
  3.9 5.3 %collective-permute-start.4 = (bf16[32,128]{1,0:T(8,128)(2,1)S(1)}, bf16[32,128]{1,0:T(8,128)(2,1)S(1)}, u32[]{:S(2)}, u32[]{:S(2)}) collective-permute-start(bf16[32,128]{1,0:T(8,128)(2,1)S(1)} %constant_dynamic-update-slice_fusion.packs_ref), channel_id=1, source_target_pairs={{0,7},{1,6},{2,5},{3,4},{4,3},{5,2},{6,1},{7,0},{8,15},{9,14},{10,... | collective-permute-start | bytes 24584 | tf_op jit(solution)/shard_map/ppermute | solution.py:39
  7.4 3.1 %collective-permute-start.3 = (bf16[32,128]{1,0:T(8,128)(2,1)S(1)}, bf16[32,128]{1,0:T(8,128)(2,1)S(1)}, u32[]{:S(2)}, u32[]{:S(2)}) collective-permute-start(bf16[32,128]{1,0:T(8,128)(2,1)S(1)} %constant_dynamic-update-slice_fusion.packs_ref), channel_id=1, source_target_pairs={{0,5},{1,4},{2,7},{3,6},{4,1},{5,0},{6,3},{7,2},{8,13},{9,12},{10,... | collective-permute-start | bytes 24584 | tf_op jit(solution)/shard_map/ppermute | solution.py:39
  7.9 3.1 %collective-permute-start.2 = (bf16[32,128]{1,0:T(8,128)(2,1)S(1)}, bf16[32,128]{1,0:T(8,128)(2,1)S(1)}, u32[]{:S(2)}, u32[]{:S(2)}) collective-permute-start(bf16[32,128]{1,0:T(8,128)(2,1)S(1)} %constant_dynamic-update-slice_fusion.packs_ref), channel_id=1, source_target_pairs={{0,3},{1,2},{2,1},{3,0},{4,7},{5,6},{6,5},{7,4},{8,11},{9,10},{10,... | collective-permute-start | bytes 24584 | tf_op jit(solution)/shard_map/ppermute | solution.py:39
  12.3 12.5 %all-to-all-start = ((bf16[32,2,640]{2,1,0:T(2,128)(2,1)}), bf16[32,2,640]{2,1,0:T(2,128)(2,1)S(1)}, u32[]{:S(2)}, u32[]{:S(2)}) async-start(bf16[32,2,640]{2,1,0:T(2,128)(2,1)} %get-tuple-element.52), calls=%async_computation | async-start | bytes 163840 | tf_op jit(solution)/shard_map/all_to_all | solution.py:392
  18.7 1.4 %collective-permute-start.5 = (bf16[128,512]{1,0:T(8,128)(2,1)S(1)}, bf16[128,512]{1,0:T(8,128)(2,1)S(1)}, u32[]{:S(2)}, u32[]{:S(2)}) collective-permute-start(bf16[128,512]{1,0:T(8,128)(2,1)S(1)} %get-tuple-element.48), channel_id=1, source_target_pairs={{0,1},{1,0},{2,3},{3,2},{4,5},{5,4},{6,7},{7,6},{8,9},{9,8},{10,11... | collective-permute-start | bytes 393224 | tf_op jit(solution)/shard_map/ppermute | solution.py:39
  19.0 1.3 %collective-permute-start.6 = (bf16[128,512]{1,0:T(8,128)(2,1)S(1)}, bf16[128,512]{1,0:T(8,128)(2,1)S(1)}, u32[]{:S(2)}, u32[]{:S(2)}) collective-permute-start(bf16[128,512]{1,0:T(8,128)(2,1)S(1)} %get-tuple-element.49), channel_id=1, source_target_pairs={{0,1},{1,0},{2,3},{3,2},{4,5},{5,4},{6,7},{7,6},{8,9},{9,8},{10,11... | collective-permute-start | bytes 393224 | tf_op jit(solution)/shard_map/ppermute | solution.py:39

commit v8 on v7

--- a/solution.py
+++ b/solution.py
@@ -284,30 +284,41 @@
         copy.wait()
 
 
-def total_kernel(meta_ref, own_ref, key_recv_ref, value_recv_ref, total_ref, row_ref):
-    length = own_ref.shape[0]
-    mine = iota((length, HDIM), 0).astype(f32) == meta_ref[0:1]
-    for i, recv_ref in enumerate((key_recv_ref, value_recv_ref)):
+def total_kernel(meta_ref, own_ref, key_recv_ref, value_recv_ref, dk_ref, dv_ref, block_ref):
+    wide = KV_HEADS * HDIM
+    row = jnp.max(meta_ref[0:1]).astype(jnp.int32)
+    start = pl.multiple_of(row // PACK * PACK, PACK)
+    for i, (recv_ref, out_ref) in enumerate(((key_recv_ref, dk_ref), (value_recv_ref, dv_ref))):
         for j in range(KV_HEADS):
-            at = columns(i * KV_HEADS + j)
-            total = own_ref[:, at] + recv_ref[:, columns(j)].astype(f32)
-            total_ref[:, at] = total.astype(bf16)
-            row = jnp.sum(jnp.where(mine, total, 0.0), axis=0, keepdims=True)
-            row_ref[i : i + 1, columns(j)] = row
-
-
-def last_kernel(slots, meta_ref, total_ref, row_ref, terms_ref, dk_ref, dv_ref, sink_ref):
-    length = total_ref.shape[0]
+            total = own_ref[:, columns(i * KV_HEADS + j)] + recv_ref[:, columns(j)].astype(f32)
+            out_ref[0, :, columns(j)] = total.astype(bf16)
+        at = slice(i * wide, (i + 1) * wide)
+        block_ref[:, at] = own_ref[pl.ds(start, PACK), at] + recv_ref[pl.ds(start, PACK), :].astype(f32)
+
+
+def last_kernel(
+    slots, meta_ref, block_ref, terms_ref, dk_in, dv_in, dk_hbm, dv_hbm, sink_hbm, dk_ref, dv_ref, sink_ref, sems
+):
     wide = KV_HEADS * HDIM
+    row = jnp.max(meta_ref[0:1]).astype(jnp.int32)
+    start = pl.multiple_of(row // PACK * PACK, PACK)
+    first = lax.axis_index("dp") * slots
+    terms = jnp.sum(terms_ref[pl.ds(first, slots), :, :wide].astype(f32), axis=0)
+    mine = iota((PACK, wide), 0) == row - start
+    sent = []
+    for i, (out_ref, out_hbm) in enumerate(((dk_ref, dk_hbm), (dv_ref, dv_hbm))):
+        block = block_ref[:, i * wide : (i + 1) * wide]
+        out_ref[...] = (block + jnp.where(mine, terms[i : i + 1], 0.0)).astype(bf16)
+        copy = pltpu.make_async_copy(out_ref, out_hbm.at[0, pl.ds(start, PACK), :], sems.at[i])
+        copy.start()
+        sent.append(copy)
     ends = jnp.sum(terms_ref[:, :, wide:].astype(f32), axis=0)
     sink_ref[...] = (ends[0:1] + ends[1:2])[:, :HEADS]
-    first = lax.axis_index("dp") * slots
-    row = row_ref[0:2] + jnp.sum(terms_ref[pl.ds(first, slots), :, :wide].astype(f32), axis=0)
-    mine = iota((length, HDIM), 0).astype(f32) == meta_ref[0:1]
-    for i, out_ref in enumerate((dk_ref, dv_ref)):
-        for j in range(KV_HEADS):
-            total = total_ref[:, columns(i * KV_HEADS + j)].astype(f32)
-            out_ref[0, :, columns(j)] = jnp.where(mine, row[i : i + 1, columns(j)], total).astype(bf16)
+    copy = pltpu.make_async_copy(sink_ref, sink_hbm, sems.at[2])
+    copy.start()
+    sent.append(copy)
+    for copy in sent:
+        copy.wait()
 
 
 def on_device(
@@ -407,26 +418,26 @@
         name="gradients",
     )(query_rows, grad_rows, ds, half, slot_keys, keys2, home, first)
     recv = [moved(part, "ctx", 1) for part in far]
-    total, sampled = pl.pallas_call(
+    grad_shape = jax.ShapeDtypeStruct((1, length, wide), bf16)
+    dk, dv, block = pl.pallas_call(
         total_kernel,
-        out_shape=[
-            jax.ShapeDtypeStruct((length, 2 * wide), bf16),
-            jax.ShapeDtypeStruct((8, wide), f32),
-        ],
+        out_shape=[grad_shape, grad_shape, jax.ShapeDtypeStruct((PACK, 2 * wide), f32)],
         in_specs=[VMEM] * 4,
-        out_specs=[VMEM] * 2,
+        out_specs=[VMEM] * 3,
         compiler_params=SMALL,
         name="pair_total",
     )(meta, own, *recv)
     dk, dv, sink_grad = pl.pallas_call(
         functools.partial(last_kernel, slots),
-        out_shape=[jax.ShapeDtypeStruct((1, length, wide), bf16)] * 2
-        + [jax.ShapeDtypeStruct((1, HEADS), f32)],
-        in_specs=[VMEM] * 4,
-        out_specs=[VMEM] * 3,
+        out_shape=[grad_shape, grad_shape, jax.ShapeDtypeStruct((1, HEADS), f32)],
+        in_specs=[VMEM] * 3 + [HBM] * 2,
+        out_specs=[HBM] * 3,
+        scratch_shapes=[pltpu.VMEM((PACK, wide), bf16)] * 2
+        + [pltpu.VMEM((1, HEADS), f32), pltpu.SemaphoreType.DMA((3,))],
+        input_output_aliases={3: 0, 4: 1},
         compiler_params=SMALL,
         name="add_up",
-    )(meta, total, sampled, terms)
+    )(meta, block, terms, dk, dv)
     return dq, dk, dv, sink_grad[0]
 
 

time: 25.8 us -> 25.8 us (level)
  waiting for transfers between devices: 8.38 us -> 7.73 us
  Pallas kernels: 4.84 us -> 5.48 us
    pallas_call x2, Pallas kernels: 0.88 us -> 1.53 us  [the longest x1 0.77 us: on_device(): pl.pallas_call(functools.partial(last_kernel, slots), out_shape=[grad_sha...]
    all_to_all x1, waiting for transfers between devices: 4.35 us -> 3.7 us  [on_device(): terms = lax.all_to_all(terms, ('dp', 'ctx'), 0, 0, tiled=True)]
  transfers between devices with their start and end apart: 8 -> 8, of which waited for: 6 -> 6; matrix products, arithmetic and copies ran while one was open for 0% -> 0% of each run, Pallas kernels for 10% -> 13%
where the time goes in v8:
time: 25.8 us; the launch traced here: 25.6 us
  starting transfers between devices  10.2 us (40%)
  waiting for transfers between devices  7.73 us (30%)
  Pallas kernels  5.48 us (21%)
  between operations  2.11 us (8%)
    ppermute x7, starting transfers between devices, moved(): lax.ppermute(array, axis, [(i, i ^ apart) for i in range(lax.axis_size(ax...  5.28 us
    all_to_all x1, starting transfers between devices, on_device(): terms = lax.all_to_all(terms, ('dp', 'ctx'), 0, 0, tiled=True)  4.93 us
    ppermute x7, waiting for transfers between devices, moved(): lax.ppermute(array, axis, [(i, i ^ apart) for i in range(lax.axis_size(ax...  4.02 us
    all_to_all x1, waiting for transfers between devices, on_device(): terms = lax.all_to_all(terms, ('dp', 'ctx'), 0, 0, tiled=True)  3.7 us
    pallas_call x1, Pallas kernels, on_device(): pl.pallas_call(gradient_kernel, out_shape=[jax.ShapeDtypeStruct((1, lengt...  1.46 us
    pallas_call x1, Pallas kernels, on_device(): pl.pallas_call(functools.partial(terms_kernel, slots), out_shape=[jax.Sha...  1.26 us
    pallas_call x1, Pallas kernels, on_device(): pl.pallas_call(score_kernel, out_shape=[by_token, by_token, jax.ShapeDtyp...  1.07 us
    pallas_call x1, Pallas kernels, on_device(): pl.pallas_call(functools.partial(last_kernel, slots), out_shape=[grad_sha...  0.77 us
  transfers between devices with their start and end apart: 8, of which 6 were waited for; matrix products, arithmetic and copies ran while one was open for 0% of the time, Pallas kernels for 13%

profile of v8, /device:TPU:0, one launch (start us, length us, event | category | flops | bytes accessed | tf_op | source)
XLA Modules:
  0.0 25.6 jit_solution(7331019568276168538)
XLA Ops:
  0.6 0.0 copy-start.4
  0.6 0.0 copy-start.3
  1.3 0.0 copy-start.5
  2.0 0.0 copy-done.4
  2.0 0.0 copy-done.3
  2.0 0.0 copy-done.5
  2.0 0.0 copy-start
  2.1 0.0 copy-start.1
  2.1 0.2 pack_sample.1
  2.2 0.5 %collective-permute-start = (bf16[128,1024]{1,0:T(8,128)(2,1)S(1)}, bf16[128,1024]{1,0:T(8,128)(2,1)S(1)}, u32[]{:S(2)}, u32[]{:S(2)}) collective-permute-start(bf16[128,1024]{1,0:T(8,128)(2,1)S(1)} %get-tuple-element.34.kv_ref), channel_id=1, source_target_pairs={{0,1},{1,0},{2,3},{3,2},{4,5},{5,4},{6,7},{7,6},{8,9},{9,8},{10,11... | collective-permute-start | bytes 786440 | tf_op jit(solution)/shard_map/ppermute | solution.py:39
  2.7 0.1 collective-permute-start.1
  2.8 1.1 %collective-permute-done.1 = bf16[16,128]{1,0:T(8,128)(2,1)S(1)} collective-permute-done((bf16[16,128]{1,0:T(8,128)(2,1)S(1)}, bf16[16,128]{1,0:T(8,128)(2,1)S(1)}, u32[]{:S(2)}, u32[]{:S(2)}) %collective-permute-start.1) | collective-permute-done | bytes 4128 | tf_op jit(solution)/shard_map/ppermute | solution.py:39
  3.9 0.0 copy-start.2
  3.9 3.6 %collective-permute-start.4 = (bf16[32,128]{1,0:T(8,128)(2,1)S(1)}, bf16[32,128]{1,0:T(8,128)(2,1)S(1)}, u32[]{:S(2)}, u32[]{:S(2)}) collective-permute-start(bf16[32,128]{1,0:T(8,128)(2,1)S(1)} %constant_dynamic-update-slice_fusion.packs_ref), channel_id=1, source_target_pairs={{0,7},{1,6},{2,5},{3,4},{4,3},{5,2},{6,1},{7,0},{8,15},{9,14},{10,... | collective-permute-start | bytes 24584 | tf_op jit(solution)/shard_map/ppermute | solution.py:39
  7.4 0.5 %collective-permute-start.3 = (bf16[32,128]{1,0:T(8,128)(2,1)S(1)}, bf16[32,128]{1,0:T(8,128)(2,1)S(1)}, u32[]{:S(2)}, u32[]{:S(2)}) collective-permute-start(bf16[32,128]{1,0:T(8,128)(2,1)S(1)} %constant_dynamic-update-slice_fusion.packs_ref), channel_id=1, source_target_pairs={{0,5},{1,4},{2,7},{3,6},{4,1},{5,0},{6,3},{7,2},{8,13},{9,12},{10,... | collective-permute-start | bytes 24584 | tf_op jit(solution)/shard_map/ppermute | solution.py:39
  7.9 0.1 collective-permute-start.2
  8.0 0.0 collective-permute-done.far_ref
  8.0 0.0 copy-done
  8.0 0.0 copy-done.1
  8.1 0.0 copy-done.2
  8.1 1.1 %pair_scores.1 = (f32[128,2048]{1,0:T(8,128)S(1)}, f32[128,2048]{1,0:T(8,128)S(1)}, f32[8,2048]{1,0:T(8,128)S(1)}, bf16[128,1024]{1,0:T(8,128)(2,1)S(1)}, bf16[2...) custom-call(bf16[1,128,2048]{2,1,0:T(8,128)(2,1)S(1)} %copy-done, ...), custom_call_target="tpu_custom_call" | custom-call | flops 268435456 | bytes 5242880 | tf_op jit(solution)/shard_map/pair_scores/pallas_call | solution.py:358
  9.1 0.0 collective-permute-done.4
  9.1 1.4 %collective-permute-done.3 = bf16[32,128]{1,0:T(8,128)(2,1)S(1)} collective-permute-done((bf16[32,128]{1,0:T(8,128)(2,1)S(1)}, bf16[32,128]{1,0:T(8,128)(2,1)S(1)}, u32[]{:S(2)}, u32[]{:S(2)}) %collective-permute-start.3) | collective-permute-done | bytes 8224 | tf_op jit(solution)/shard_map/ppermute | solution.py:39
  10.5 0.5 %collective-permute-done.2 = bf16[32,128]{1,0:T(8,128)(2,1)S(1)} collective-permute-done((bf16[32,128]{1,0:T(8,128)(2,1)S(1)}, bf16[32,128]{1,0:T(8,128)(2,1)S(1)}, u32[]{:S(2)}, u32[]{:S(2)}) %collective-permute-start.2) | collective-permute-done | bytes 8224 | tf_op jit(solution)/shard_map/ppermute | solution.py:39
  11.0 1.3 %slot_terms.1 = (bf16[32,2,640]{2,1,0:T(2,128)(2,1)}, bf16[144,2048]{1,0:T(8,128)(2,1)S(1)}, bf16[128,2048]{1,0:T(8,128)(2,1)S(1)}, bf16[16,512]{1,0:T(8,128)(2,1)S(1)}) custom-call(bf16[1,128,2048]{2,1,0:T(8,128)(2,1)S(1)} %copy-done, bf16[1,128,2048]{2,1,0:T(8,128)(2,1)S(1)} %copy-done.1, f32[128,2048]{1,0:T(8,128)S(1)} %get-tuple-element.36.weight_ref, ...), custom_call_target="tpu_custom_call" | custom-call | tf_op jit(solution)/shard_map/slot_terms/pallas_call | solution.py:383
  12.3 4.9 %all-to-all-start = ((bf16[32,2,640]{2,1,0:T(2,128)(2,1)}), bf16[32,2,640]{2,1,0:T(2,128)(2,1)S(1)}, u32[]{:S(2)}, u32[]{:S(2)}) async-start(bf16[32,2,640]{2,1,0:T(2,128)(2,1)} %get-tuple-element.52), calls=%async_computation | async-start | bytes 163840 | tf_op jit(solution)/shard_map/all_to_all | solution.py:403
  17.2 1.5 %gradients.1 = (bf16[1,128,2048]{2,1,0:T(8,128)(2,1)}, f32[128,1024]{1,0:T(8,128)S(1)}, bf16[128,512]{1,0:T(8,128)(2,1)S(1)}, bf16[128,512]{1,0:T(8,128)(2,1)S(1)}) custom-call(bf16[1,128,2048]{2,1,0:T(8,128)(2,1)S(1)} %copy-done, bf16[1,128,2048]{2,1,0:T(8,128)(2,1)S(1)} %copy-done.1, bf16[144,2048]{1,0:T(8,128)(2,1)S(1)} %get-tuple-element.40.ds_ref, ...), custom_call_target="tpu_custom_call" | custom-call | flops 402653184 | bytes 5242880 | tf_op jit(solution)/shard_map/gradients/pallas_call | solution.py:404
  18.7 0.3 %collective-permute-start.5 = (bf16[128,512]{1,0:T(8,128)(2,1)S(1)}, bf16[128,512]{1,0:T(8,128)(2,1)S(1)}, u32[]{:S(2)}, u32[]{:S(2)}) collective-permute-start(bf16[128,512]{1,0:T(8,128)(2,1)S(1)} %get-tuple-element.49), channel_id=1, source_target_pairs={{0,1},{1,0},{2,3},{3,2},{4,5},{5,4},{6,7},{7,6},{8,9},{9,8},{10,11... | collective-permute-start | bytes 393224 | tf_op jit(solution)/shard_map/ppermute | solution.py:39
  19.0 0.3 %collective-permute-start.6 = (bf16[128,512]{1,0:T(8,128)(2,1)S(1)}, bf16[128,512]{1,0:T(8,128)(2,1)S(1)}, u32[]{:S(2)}, u32[]{:S(2)}) collective-permute-start(bf16[128,512]{1,0:T(8,128)(2,1)S(1)} %get-tuple-element.50), channel_id=1, source_target_pairs={{0,1},{1,0},{2,3},{3,2},{4,5},{5,4},{6,7},{7,6},{8,9},{9,8},{10,11... | collective-permute-start | bytes 393224 | tf_op jit(solution)/shard_map/ppermute | solution.py:39
  19.2 0.8 %collective-permute-done.5.key_recv_ref = bf16[128,512]{1,0:T(8,128)(2,1)S(1)} collective-permute-done((bf16[128,512]{1,0:T(8,128)(2,1)S(1)}, bf16[128,512]{1,0:T(8,128)(2,1)S(1)}, u32[]{:S(2)}, u32[]{:S(2)}) %collective-permute-start.5) | collective-permute-done | bytes 131104 | tf_op jit(solution)/shard_map/ppermute | solution.py:39
  20.1 0.3 collective-permute-done.6.value_recv_ref
  20.3 0.8 %pair_total.1 = (bf16[1,128,512]{2,1,0:T(8,128)(2,1)}, bf16[1,128,512]{2,1,0:T(8,128)(2,1)}, f32[16,1024]{1,0:T(8,128)S(1)}) custom-call(f32[8,128]{1,0:T(8,128)S(1)} %get-tuple-element.47.meta_ref, f32[128,1024]{1,0:T(8,128)S(1)} %get-tuple-element.48.own_ref, bf16[128,512]{1,0:T(8,128)(2,1)S(1)} %collective-permute-done.5.key_recv_ref, ...), custom_call_target="tpu_custom_call" | custom-call | tf_op jit(solution)/shard_map/pair_total/pallas_call | solution.py:422
  21.1 3.7 %all-to-all-done.terms_ref = bf16[32,2,640]{2,1,0:T(2,128)(2,1)S(1)} async-done(((bf16[32,2,640]{2,1,0:T(2,128)(2,1)}), bf16[32,2,640]{2,1,0:T(2,128)(2,1)S(1)}, u32[]{:S(2)}, u32[]{:S(2)}) %all-to-all-start) | async-done | bytes 81952 | tf_op jit(solution)/shard_map/all_to_all | solution.py:403
  24.8 0.8 %add_up.1 = (bf16[1,128,512]{2,1,0:T(8,128)(2,1)}, bf16[1,128,512]{2,1,0:T(8,128)(2,1)}, f32[1,16]{1,0:T(1,128)}) custom-call(f32[8,128]{1,0:T(8,128)S(1)} %get-tuple-element.47.meta_ref, f32[16,1024]{1,0:T(8,128)S(1)} %get-tuple-element.51.block_ref, bf16[32,2,640]{2,1,0:T(2,128)(2,1)S(1)} %all-to-all-done.terms_ref, ...), custom_call_target="tpu_custom_call", output_to_operand_aliasing={{0}: (3, {}), {1}: (4, {})} | custom-call | tf_op jit(solution)/shard_map/add_up/pallas_call | solution.py:430
  (4 shorter events, 0.0 us)
Async XLA Ops:
  0.6 1.4 %copy-start.4 = (bf16[1,128,512]{2,1,0:T(8,128)(2,1)S(1)}, bf16[1,128,512]{2,1,0:T(8,128)(2,1)}, u32[]{:S(2)}) copy-start(bf16[1,128,512]{2,1,0:T(8,128)(2,1)} %values_ref.1) | copy-start | bytes 393220
  0.6 1.4 %copy-start.3 = (bf16[1,128,512]{2,1,0:T(8,128)(2,1)S(1)}, bf16[1,128,512]{2,1,0:T(8,128)(2,1)}, u32[]{:S(2)}) copy-start(bf16[1,128,512]{2,1,0:T(8,128)(2,1)} %keys_ref.1) | copy-start | bytes 393220
  1.3 0.7 %copy-start.5 = (s32[1,128]{1,0:T(1,128)S(1)}, s32[1,128]{1,0:T(1,128)}, u32[]{:S(2)}) copy-start(s32[1,128]{1,0:T(1,128)} %rank_ref.1) | copy-start | bytes 1540
  2.0 6.0 %copy-start = (bf16[1,128,2048]{2,1,0:T(8,128)(2,1)S(1)}, bf16[1,128,2048]{2,1,0:T(8,128)(2,1)}, u32[]{:S(2)}) copy-start(bf16[1,128,2048]{2,1,0:T(8,128)(2,1)} %query_ref.5) | copy-start | bytes 1572868
  2.1 6.0 %copy-start.1 = (bf16[1,128,2048]{2,1,0:T(8,128)(2,1)S(1)}, bf16[1,128,2048]{2,1,0:T(8,128)(2,1)}, u32[]{:S(2)}) copy-start(bf16[1,128,2048]{2,1,0:T(8,128)(2,1)} %grad_ref.5) | copy-start | bytes 1572868
  2.2 5.8 %collective-permute-start = (bf16[128,1024]{1,0:T(8,128)(2,1)S(1)}, bf16[128,1024]{1,0:T(8,128)(2,1)S(1)}, u32[]{:S(2)}, u32[]{:S(2)}) collective-permute-start(bf16[128,1024]{1,0:T(8,128)(2,1)S(1)} %get-tuple-element.34.kv_ref), channel_id=1, source_target_pairs={{0,1},{1,0},{2,3},{3,2},{4,5},{5,4},{6,7},{7,6},{8,9},{9,8},{10,11... | collective-permute-start | bytes 786440 | tf_op jit(solution)/shard_map/ppermute | solution.py:39
  2.7 1.2 %collective-permute-start.1 = (bf16[16,128]{1,0:T(8,128)(2,1)S(1)}, bf16[16,128]{1,0:T(8,128)(2,1)S(1)}, u32[]{:S(2)}, u32[]{:S(2)}) collective-permute-start(bf16[16,128]{1,0:T(8,128)(2,1)S(1)} %get-tuple-element.35), channel_id=1, source_target_pairs={{0,1},{1,0},{2,3},{3,2},{4,5},{5,4},{6,7},{7,6},{8,9},{9,8},{10,11... | collective-permute-start | bytes 12296 | tf_op jit(solution)/shard_map/ppermute | solution.py:39
  3.9 4.2 %copy-start.2 = (f32[16]{0:T(128)S(1)}, f32[16]{0:T(128)}, u32[]{:S(2)}) copy-start(f32[16]{0:T(128)} %param.15) | copy-start | bytes 196
  3.9 5.3 %collective-permute-start.4 = (bf16[32,128]{1,0:T(8,128)(2,1)S(1)}, bf16[32,128]{1,0:T(8,128)(2,1)S(1)}, u32[]{:S(2)}, u32[]{:S(2)}) collective-permute-start(bf16[32,128]{1,0:T(8,128)(2,1)S(1)} %constant_dynamic-update-slice_fusion.packs_ref), channel_id=1, source_target_pairs={{0,7},{1,6},{2,5},{3,4},{4,3},{5,2},{6,1},{7,0},{8,15},{9,14},{10,... | collective-permute-start | bytes 24584 | tf_op jit(solution)/shard_map/ppermute | solution.py:39
  7.4 3.1 %collective-permute-start.3 = (bf16[32,128]{1,0:T(8,128)(2,1)S(1)}, bf16[32,128]{1,0:T(8,128)(2,1)S(1)}, u32[]{:S(2)}, u32[]{:S(2)}) collective-permute-start(bf16[32,128]{1,0:T(8,128)(2,1)S(1)} %constant_dynamic-update-slice_fusion.packs_ref), channel_id=1, source_target_pairs={{0,5},{1,4},{2,7},{3,6},{4,1},{5,0},{6,3},{7,2},{8,13},{9,12},{10,... | collective-permute-start | bytes 24584 | tf_op jit(solution)/shard_map/ppermute | solution.py:39
  7.9 3.1 %collective-permute-start.2 = (bf16[32,128]{1,0:T(8,128)(2,1)S(1)}, bf16[32,128]{1,0:T(8,128)(2,1)S(1)}, u32[]{:S(2)}, u32[]{:S(2)}) collective-permute-start(bf16[32,128]{1,0:T(8,128)(2,1)S(1)} %constant_dynamic-update-slice_fusion.packs_ref), channel_id=1, source_target_pairs={{0,3},{1,2},{2,1},{3,0},{4,7},{5,6},{6,5},{7,4},{8,11},{9,10},{10,... | collective-permute-start | bytes 24584 | tf_op jit(solution)/shard_map/ppermute | solution.py:39
  12.3 12.5 %all-to-all-start = ((bf16[32,2,640]{2,1,0:T(2,128)(2,1)}), bf16[32,2,640]{2,1,0:T(2,128)(2,1)S(1)}, u32[]{:S(2)}, u32[]{:S(2)}) async-start(bf16[32,2,640]{2,1,0:T(2,128)(2,1)} %get-tuple-element.52), calls=%async_computation | async-start | bytes 163840 | tf_op jit(solution)/shard_map/all_to_all | solution.py:403
  18.7 1.4 %collective-permute-start.5 = (bf16[128,512]{1,0:T(8,128)(2,1)S(1)}, bf16[128,512]{1,0:T(8,128)(2,1)S(1)}, u32[]{:S(2)}, u32[]{:S(2)}) collective-permute-start(bf16[128,512]{1,0:T(8,128)(2,1)S(1)} %get-tuple-element.49), channel_id=1, source_target_pairs={{0,1},{1,0},{2,3},{3,2},{4,5},{5,4},{6,7},{7,6},{8,9},{9,8},{10,11... | collective-permute-start | bytes 393224 | tf_op jit(solution)/shard_map/ppermute | solution.py:39
  19.0 1.3 %collective-permute-start.6 = (bf16[128,512]{1,0:T(8,128)(2,1)S(1)}, bf16[128,512]{1,0:T(8,128)(2,1)S(1)}, u32[]{:S(2)}, u32[]{:S(2)}) collective-permute-start(bf16[128,512]{1,0:T(8,128)(2,1)S(1)} %get-tuple-element.50), channel_id=1, source_target_pairs={{0,1},{1,0},{2,3},{3,2},{4,5},{5,4},{6,7},{7,6},{8,9},{9,8},{10,11... | collective-permute-start | bytes 393224 | tf_op jit(solution)/shard_map/ppermute | solution.py:39

commit v9 on v7

--- a/solution.py
+++ b/solution.py
@@ -341,6 +341,7 @@
     )(sample_rows, sample_count, token, bucket_rank, key_rows, value_rows)
 
     far_tile = moved(tile, "ctx", 1)
+    kv, far_tile = lax.optimization_barrier((kv, far_tile))
     far_kv = moved(kv, "ctx", 1)
     packs = jnp.concatenate([tile, far_tile], 0)
     by_token = jax.ShapeDtypeStruct((length, rows), f32)

time: 25.8 us -> 25.6 us (level)
  waiting for transfers between devices: 8.38 us -> 8.1 us
    ppermute x7, waiting for transfers between devices: 4.02 us -> 3.74 us  [moved(): lax.ppermute(array, axis, [(i, i ^ apart) for i in range(lax.axis_size(ax...]
where the time goes in v9:
time: 25.6 us; the launch traced here: 25.4 us
  starting transfers between devices  10.3 us (40%)
  waiting for transfers between devices  8.1 us (32%)
  Pallas kernels  4.84 us (19%)
  between operations  2.11 us (8%)
    ppermute x7, starting transfers between devices, moved(): lax.ppermute(array, axis, [(i, i ^ apart) for i in range(lax.axis_size(ax...  5.37 us
    all_to_all x1, starting transfers between devices, on_device(): terms = lax.all_to_all(terms, ('dp', 'ctx'), 0, 0, tiled=True)  4.93 us
    all_to_all x1, waiting for transfers between devices, on_device(): terms = lax.all_to_all(terms, ('dp', 'ctx'), 0, 0, tiled=True)  4.35 us
    ppermute x7, waiting for transfers between devices, moved(): lax.ppermute(array, axis, [(i, i ^ apart) for i in range(lax.axis_size(ax...  3.74 us
    pallas_call x1, Pallas kernels, on_device(): pl.pallas_call(gradient_kernel, out_shape=[jax.ShapeDtypeStruct((1, lengt...  1.46 us
    pallas_call x1, Pallas kernels, on_device(): pl.pallas_call(functools.partial(terms_kernel, slots), out_shape=[jax.Sha...  1.27 us
    pallas_call x1, Pallas kernels, on_device(): pl.pallas_call(score_kernel, out_shape=[by_token, by_token, jax.ShapeDtyp...  1.08 us
    pallas_call x1, Pallas kernels, on_device(): pl.pallas_call(functools.partial(last_kernel, slots), out_shape=[jax.Shap...  0.77 us
  transfers between devices with their start and end apart: 8, of which 6 were waited for; matrix products, arithmetic and copies ran while one was open for 0% of the time, Pallas kernels for 10%

profile of v9, /device:TPU:0, one launch (start us, length us, event | category | flops | bytes accessed | tf_op | source)
XLA Modules:
  0.0 25.4 jit_solution(12884911971675084807)
XLA Ops:
  0.6 0.0 copy-start.4
  0.6 0.0 copy-start.3
  1.3 0.0 copy-start.5
  2.0 0.0 copy-done.4
  2.0 0.0 copy-done.3
  2.0 0.0 copy-done.5
  2.0 0.0 copy-start
  2.1 0.0 copy-start.1
  2.1 0.2 pack_sample.1
  2.2 0.5 %collective-permute-start = (bf16[16,128]{1,0:T(8,128)(2,1)S(1)}, bf16[16,128]{1,0:T(8,128)(2,1)S(1)}, u32[]{:S(2)}, u32[]{:S(2)}) collective-permute-start(bf16[16,128]{1,0:T(8,128)(2,1)S(1)} %get-tuple-element.36), channel_id=1, source_target_pairs={{0,1},{1,0},{2,3},{3,2},{4,5},{5,4},{6,7},{7,6},{8,9},{9,8},{10,11... | collective-permute-start | bytes 12296 | tf_op jit(solution)/shard_map/ppermute | solution.py:39
  2.7 0.8 %collective-permute-done = bf16[16,128]{1,0:T(8,128)(2,1)S(1)} collective-permute-done((bf16[16,128]{1,0:T(8,128)(2,1)S(1)}, bf16[16,128]{1,0:T(8,128)(2,1)S(1)}, u32[]{:S(2)}, u32[]{:S(2)}) %collective-permute-start) | collective-permute-done | bytes 4128 | tf_op jit(solution)/shard_map/ppermute | solution.py:39
  3.5 0.3 %collective-permute-start.1 = (bf16[128,1024]{1,0:T(8,128)(2,1)S(1)}, bf16[128,1024]{1,0:T(8,128)(2,1)S(1)}, u32[]{:S(2)}, u32[]{:S(2)}) collective-permute-start(bf16[128,1024]{1,0:T(8,128)(2,1)S(1)} %get-tuple-element.37.kv_ref), channel_id=1, source_target_pairs={{0,1},{1,0},{2,3},{3,2},{4,5},{5,4},{6,7},{7,6},{8,9},{9,8},{10,11... | collective-permute-start | bytes 786440 | tf_op jit(solution)/shard_map/ppermute | solution.py:39
  3.9 0.0 copy-start.2
  3.9 3.6 %collective-permute-start.4 = (bf16[32,128]{1,0:T(8,128)(2,1)S(1)}, bf16[32,128]{1,0:T(8,128)(2,1)S(1)}, u32[]{:S(2)}, u32[]{:S(2)}) collective-permute-start(bf16[32,128]{1,0:T(8,128)(2,1)S(1)} %constant_dynamic-update-slice_fusion.packs_ref), channel_id=1, source_target_pairs={{0,7},{1,6},{2,5},{3,4},{4,3},{5,2},{6,1},{7,0},{8,15},{9,14},{10,... | collective-permute-start | bytes 24584 | tf_op jit(solution)/shard_map/ppermute | solution.py:39
  7.4 0.3 %collective-permute-start.3 = (bf16[32,128]{1,0:T(8,128)(2,1)S(1)}, bf16[32,128]{1,0:T(8,128)(2,1)S(1)}, u32[]{:S(2)}, u32[]{:S(2)}) collective-permute-start(bf16[32,128]{1,0:T(8,128)(2,1)S(1)} %constant_dynamic-update-slice_fusion.packs_ref), channel_id=1, source_target_pairs={{0,5},{1,4},{2,7},{3,6},{4,1},{5,0},{6,3},{7,2},{8,13},{9,12},{10,... | collective-permute-start | bytes 24584 | tf_op jit(solution)/shard_map/ppermute | solution.py:39
  7.7 0.1 collective-permute-start.2
  7.9 0.0 collective-permute-done.1.far_ref
  7.9 0.0 copy-done
  7.9 0.0 copy-done.1
  7.9 0.0 copy-done.2
  7.9 1.1 %pair_scores.1 = (f32[128,2048]{1,0:T(8,128)S(1)}, f32[128,2048]{1,0:T(8,128)S(1)}, f32[8,2048]{1,0:T(8,128)S(1)}, bf16[128,1024]{1,0:T(8,128)(2,1)S(1)}, bf16[2...) custom-call(bf16[1,128,2048]{2,1,0:T(8,128)(2,1)S(1)} %copy-done, ...), custom_call_target="tpu_custom_call" | custom-call | flops 268435456 | bytes 5242880 | tf_op jit(solution)/shard_map/pair_scores/pallas_call | solution.py:348
  9.0 0.0 collective-permute-done.4
  9.0 1.5 %collective-permute-done.3 = bf16[32,128]{1,0:T(8,128)(2,1)S(1)} collective-permute-done((bf16[32,128]{1,0:T(8,128)(2,1)S(1)}, bf16[32,128]{1,0:T(8,128)(2,1)S(1)}, u32[]{:S(2)}, u32[]{:S(2)}) %collective-permute-start.3) | collective-permute-done | bytes 8224 | tf_op jit(solution)/shard_map/ppermute | solution.py:39
  10.5 0.3 %collective-permute-done.2 = bf16[32,128]{1,0:T(8,128)(2,1)S(1)} collective-permute-done((bf16[32,128]{1,0:T(8,128)(2,1)S(1)}, bf16[32,128]{1,0:T(8,128)(2,1)S(1)}, u32[]{:S(2)}, u32[]{:S(2)}) %collective-permute-start.2) | collective-permute-done | bytes 8224 | tf_op jit(solution)/shard_map/ppermute | solution.py:39
  10.8 1.3 %slot_terms.1 = (bf16[32,2,640]{2,1,0:T(2,128)(2,1)}, bf16[144,2048]{1,0:T(8,128)(2,1)S(1)}, bf16[128,2048]{1,0:T(8,128)(2,1)S(1)}, bf16[16,512]{1,0:T(8,128)(2,1)S(1)}) custom-call(bf16[1,128,2048]{2,1,0:T(8,128)(2,1)S(1)} %copy-done, bf16[1,128,2048]{2,1,0:T(8,128)(2,1)S(1)} %copy-done.1, f32[128,2048]{1,0:T(8,128)S(1)} %get-tuple-element.39.weight_ref, ...), custom_call_target="tpu_custom_call" | custom-call | tf_op jit(solution)/shard_map/slot_terms/pallas_call | solution.py:373
  12.1 4.9 %all-to-all-start = ((bf16[32,2,640]{2,1,0:T(2,128)(2,1)}), bf16[32,2,640]{2,1,0:T(2,128)(2,1)S(1)}, u32[]{:S(2)}, u32[]{:S(2)}) async-start(bf16[32,2,640]{2,1,0:T(2,128)(2,1)} %get-tuple-element.56), calls=%async_computation | async-start | bytes 163840 | tf_op jit(solution)/shard_map/all_to_all | solution.py:393
  17.0 1.5 %gradients.1 = (bf16[1,128,2048]{2,1,0:T(8,128)(2,1)}, f32[128,1024]{1,0:T(8,128)S(1)}, bf16[128,512]{1,0:T(8,128)(2,1)S(1)}, bf16[128,512]{1,0:T(8,128)(2,1)S(1)}) custom-call(bf16[1,128,2048]{2,1,0:T(8,128)(2,1)S(1)} %copy-done, bf16[1,128,2048]{2,1,0:T(8,128)(2,1)S(1)} %copy-done.1, bf16[144,2048]{1,0:T(8,128)(2,1)S(1)} %get-tuple-element.43.ds_ref, ...), custom_call_target="tpu_custom_call" | custom-call | flops 402653184 | bytes 5242880 | tf_op jit(solution)/shard_map/gradients/pallas_call | solution.py:394
  18.5 0.3 %collective-permute-start.5 = (bf16[128,512]{1,0:T(8,128)(2,1)S(1)}, bf16[128,512]{1,0:T(8,128)(2,1)S(1)}, u32[]{:S(2)}, u32[]{:S(2)}) collective-permute-start(bf16[128,512]{1,0:T(8,128)(2,1)S(1)} %get-tuple-element.52), channel_id=1, source_target_pairs={{0,1},{1,0},{2,3},{3,2},{4,5},{5,4},{6,7},{7,6},{8,9},{9,8},{10,11... | collective-permute-start | bytes 393224 | tf_op jit(solution)/shard_map/ppermute | solution.py:39
  18.8 0.3 %collective-permute-start.6 = (bf16[128,512]{1,0:T(8,128)(2,1)S(1)}, bf16[128,512]{1,0:T(8,128)(2,1)S(1)}, u32[]{:S(2)}, u32[]{:S(2)}) collective-permute-start(bf16[128,512]{1,0:T(8,128)(2,1)S(1)} %get-tuple-element.53), channel_id=1, source_target_pairs={{0,1},{1,0},{2,3},{3,2},{4,5},{5,4},{6,7},{7,6},{8,9},{9,8},{10,11... | collective-permute-start | bytes 393224 | tf_op jit(solution)/shard_map/ppermute | solution.py:39
  19.1 0.8 %collective-permute-done.5.key_recv_ref = bf16[128,512]{1,0:T(8,128)(2,1)S(1)} collective-permute-done((bf16[128,512]{1,0:T(8,128)(2,1)S(1)}, bf16[128,512]{1,0:T(8,128)(2,1)S(1)}, u32[]{:S(2)}, u32[]{:S(2)}) %collective-permute-start.5) | collective-permute-done | bytes 131104 | tf_op jit(solution)/shard_map/ppermute | solution.py:39
  19.9 0.3 collective-permute-done.6.value_recv_ref
  20.2 0.1 pair_total.1
  20.3 4.4 %all-to-all-done.terms_ref = bf16[32,2,640]{2,1,0:T(2,128)(2,1)S(1)} async-done(((bf16[32,2,640]{2,1,0:T(2,128)(2,1)}), bf16[32,2,640]{2,1,0:T(2,128)(2,1)S(1)}, u32[]{:S(2)}, u32[]{:S(2)}) %all-to-all-start) | async-done | bytes 81952 | tf_op jit(solution)/shard_map/all_to_all | solution.py:393
  24.6 0.8 %add_up.1 = (bf16[1,128,512]{2,1,0:T(8,128)(2,1)}, bf16[1,128,512]{2,1,0:T(8,128)(2,1)}, f32[1,16]{1,0:T(1,128)}) custom-call(f32[8,128]{1,0:T(8,128)S(1)} %get-tuple-element.50.meta_ref, bf16[128,1024]{1,0:T(8,128)(2,1)S(1)} %get-tuple-element.54.total_ref, f32[8,512]{1,0:T(8,128)S(1)} %get-tuple-element.55.row_ref, ...), custom_call_target="tpu_custom_call" | custom-call | tf_op jit(solution)/shard_map/add_up/pallas_call | solution.py:422
  (4 shorter events, 0.0 us)
Async XLA Ops:
  0.6 1.4 %copy-start.4 = (bf16[1,128,512]{2,1,0:T(8,128)(2,1)S(1)}, bf16[1,128,512]{2,1,0:T(8,128)(2,1)}, u32[]{:S(2)}) copy-start(bf16[1,128,512]{2,1,0:T(8,128)(2,1)} %values_ref.1) | copy-start | bytes 393220
  0.6 1.4 %copy-start.3 = (bf16[1,128,512]{2,1,0:T(8,128)(2,1)S(1)}, bf16[1,128,512]{2,1,0:T(8,128)(2,1)}, u32[]{:S(2)}) copy-start(bf16[1,128,512]{2,1,0:T(8,128)(2,1)} %keys_ref.1) | copy-start | bytes 393220
  1.3 0.7 %copy-start.5 = (s32[1,128]{1,0:T(1,128)S(1)}, s32[1,128]{1,0:T(1,128)}, u32[]{:S(2)}) copy-start(s32[1,128]{1,0:T(1,128)} %rank_ref.1) | copy-start | bytes 1540
  2.0 5.8 %copy-start = (bf16[1,128,2048]{2,1,0:T(8,128)(2,1)S(1)}, bf16[1,128,2048]{2,1,0:T(8,128)(2,1)}, u32[]{:S(2)}) copy-start(bf16[1,128,2048]{2,1,0:T(8,128)(2,1)} %query_ref.5) | copy-start | bytes 1572868
  2.1 5.8 %copy-start.1 = (bf16[1,128,2048]{2,1,0:T(8,128)(2,1)S(1)}, bf16[1,128,2048]{2,1,0:T(8,128)(2,1)}, u32[]{:S(2)}) copy-start(bf16[1,128,2048]{2,1,0:T(8,128)(2,1)} %grad_ref.5) | copy-start | bytes 1572868
  2.2 1.3 %collective-permute-start = (bf16[16,128]{1,0:T(8,128)(2,1)S(1)}, bf16[16,128]{1,0:T(8,128)(2,1)S(1)}, u32[]{:S(2)}, u32[]{:S(2)}) collective-permute-start(bf16[16,128]{1,0:T(8,128)(2,1)S(1)} %get-tuple-element.36), channel_id=1, source_target_pairs={{0,1},{1,0},{2,3},{3,2},{4,5},{5,4},{6,7},{7,6},{8,9},{9,8},{10,11... | collective-permute-start | bytes 12296 | tf_op jit(solution)/shard_map/ppermute | solution.py:39
  3.5 4.3 %collective-permute-start.1 = (bf16[128,1024]{1,0:T(8,128)(2,1)S(1)}, bf16[128,1024]{1,0:T(8,128)(2,1)S(1)}, u32[]{:S(2)}, u32[]{:S(2)}) collective-permute-start(bf16[128,1024]{1,0:T(8,128)(2,1)S(1)} %get-tuple-element.37.kv_ref), channel_id=1, source_target_pairs={{0,1},{1,0},{2,3},{3,2},{4,5},{5,4},{6,7},{7,6},{8,9},{9,8},{10,11... | collective-permute-start | bytes 786440 | tf_op jit(solution)/shard_map/ppermute | solution.py:39
  3.9 4.0 %copy-start.2 = (f32[16]{0:T(128)S(1)}, f32[16]{0:T(128)}, u32[]{:S(2)}) copy-start(f32[16]{0:T(128)} %param.15) | copy-start | bytes 196
  3.9 5.1 %collective-permute-start.4 = (bf16[32,128]{1,0:T(8,128)(2,1)S(1)}, bf16[32,128]{1,0:T(8,128)(2,1)S(1)}, u32[]{:S(2)}, u32[]{:S(2)}) collective-permute-start(bf16[32,128]{1,0:T(8,128)(2,1)S(1)} %constant_dynamic-update-slice_fusion.packs_ref), channel_id=1, source_target_pairs={{0,7},{1,6},{2,5},{3,4},{4,3},{5,2},{6,1},{7,0},{8,15},{9,14},{10,... | collective-permute-start | bytes 24584 | tf_op jit(solution)/shard_map/ppermute | solution.py:39
  7.4 3.1 %collective-permute-start.3 = (bf16[32,128]{1,0:T(8,128)(2,1)S(1)}, bf16[32,128]{1,0:T(8,128)(2,1)S(1)}, u32[]{:S(2)}, u32[]{:S(2)}) collective-permute-start(bf16[32,128]{1,0:T(8,128)(2,1)S(1)} %constant_dynamic-update-slice_fusion.packs_ref), channel_id=1, source_target_pairs={{0,5},{1,4},{2,7},{3,6},{4,1},{5,0},{6,3},{7,2},{8,13},{9,12},{10,... | collective-permute-start | bytes 24584 | tf_op jit(solution)/shard_map/ppermute | solution.py:39
  7.7 3.1 %collective-permute-start.2 = (bf16[32,128]{1,0:T(8,128)(2,1)S(1)}, bf16[32,128]{1,0:T(8,128)(2,1)S(1)}, u32[]{:S(2)}, u32[]{:S(2)}) collective-permute-start(bf16[32,128]{1,0:T(8,128)(2,1)S(1)} %constant_dynamic-update-slice_fusion.packs_ref), channel_id=1, source_target_pairs={{0,3},{1,2},{2,1},{3,0},{4,7},{5,6},{6,5},{7,4},{8,11},{9,10},{10,... | collective-permute-start | bytes 24584 | tf_op jit(solution)/shard_map/ppermute | solution.py:39
  12.1 12.5 %all-to-all-start = ((bf16[32,2,640]{2,1,0:T(2,128)(2,1)}), bf16[32,2,640]{2,1,0:T(2,128)(2,1)S(1)}, u32[]{:S(2)}, u32[]{:S(2)}) async-start(bf16[32,2,640]{2,1,0:T(2,128)(2,1)} %get-tuple-element.56), calls=%async_computation | async-start | bytes 163840 | tf_op jit(solution)/shard_map/all_to_all | solution.py:393
  18.5 1.4 %collective-permute-start.5 = (bf16[128,512]{1,0:T(8,128)(2,1)S(1)}, bf16[128,512]{1,0:T(8,128)(2,1)S(1)}, u32[]{:S(2)}, u32[]{:S(2)}) collective-permute-start(bf16[128,512]{1,0:T(8,128)(2,1)S(1)} %get-tuple-element.52), channel_id=1, source_target_pairs={{0,1},{1,0},{2,3},{3,2},{4,5},{5,4},{6,7},{7,6},{8,9},{9,8},{10,11... | collective-permute-start | bytes 393224 | tf_op jit(solution)/shard_map/ppermute | solution.py:39
  18.8 1.3 %collective-permute-start.6 = (bf16[128,512]{1,0:T(8,128)(2,1)S(1)}, bf16[128,512]{1,0:T(8,128)(2,1)S(1)}, u32[]{:S(2)}, u32[]{:S(2)}) collective-permute-start(bf16[128,512]{1,0:T(8,128)(2,1)S(1)} %get-tuple-element.53), channel_id=1, source_target_pairs={{0,1},{1,0},{2,3},{3,2},{4,5},{5,4},{6,7},{7,6},{8,9},{9,8},{10,11... | collective-permute-start | bytes 393224 | tf_op jit(solution)/shard_map/ppermute | solution.py:39

commit v10 on v8

--- a/solution.py
+++ b/solution.py
@@ -352,6 +352,7 @@
     )(sample_rows, sample_count, token, bucket_rank, key_rows, value_rows)
 
     far_tile = moved(tile, "ctx", 1)
+    kv, far_tile = lax.optimization_barrier((kv, far_tile))
     far_kv = moved(kv, "ctx", 1)
     packs = jnp.concatenate([tile, far_tile], 0)
     by_token = jax.ShapeDtypeStruct((length, rows), f32)

time: 25.8 us -> 25.6 us (level)
  waiting for transfers between devices: 7.73 us -> 7.45 us
    ppermute x7, waiting for transfers between devices: 4.02 us -> 3.74 us  [moved(): lax.ppermute(array, axis, [(i, i ^ apart) for i in range(lax.axis_size(ax...]
where the time goes in v10:
time: 25.6 us; the launch traced here: 25.4 us
  starting transfers between devices  10.3 us (40%)
  waiting for transfers between devices  7.45 us (29%)
  Pallas kernels  5.48 us (21%)
  between operations  2.11 us (8%)
    ppermute x7, starting transfers between devices, moved(): lax.ppermute(array, axis, [(i, i ^ apart) for i in range(lax.axis_size(ax...  5.37 us
    all_to_all x1, starting transfers between devices, on_device(): terms = lax.all_to_all(terms, ('dp', 'ctx'), 0, 0, tiled=True)  4.93 us
    ppermute x7, waiting for transfers between devices, moved(): lax.ppermute(array, axis, [(i, i ^ apart) for i in range(lax.axis_size(ax...  3.74 us
    all_to_all x1, waiting for transfers between devices, on_device(): terms = lax.all_to_all(terms, ('dp', 'ctx'), 0, 0, tiled=True)  3.71 us
    pallas_call x1, Pallas kernels, on_device(): pl.pallas_call(gradient_kernel, out_shape=[jax.ShapeDtypeStruct((1, lengt...  1.46 us
    pallas_call x1, Pallas kernels, on_device(): pl.pallas_call(functools.partial(terms_kernel, slots), out_shape=[jax.Sha...  1.26 us
    pallas_call x1, Pallas kernels, on_device(): pl.pallas_call(score_kernel, out_shape=[by_token, by_token, jax.ShapeDtyp...  1.08 us
    pallas_call x1, Pallas kernels, on_device(): pl.pallas_call(functools.partial(last_kernel, slots), out_shape=[grad_sha...  0.77 us
  transfers between devices with their start and end apart: 8, of which 6 were waited for; matrix products, arithmetic and copies ran while one was open for 0% of the time, Pallas kernels for 13%

profile of v10, /device:TPU:0, one launch (start us, length us, event | category | flops | bytes accessed | tf_op | source)
XLA Modules:
  0.0 25.4 jit_solution(7029471543287589481)
XLA Ops:
  0.6 0.0 copy-start.4
  0.6 0.0 copy-start.3
  1.3 0.0 copy-start.5
  2.0 0.0 copy-done.4
  2.0 0.0 copy-done.3
  2.0 0.0 copy-done.5
  2.0 0.0 copy-start
  2.1 0.0 copy-start.1
  2.1 0.2 pack_sample.1
  2.2 0.5 %collective-permute-start = (bf16[16,128]{1,0:T(8,128)(2,1)S(1)}, bf16[16,128]{1,0:T(8,128)(2,1)S(1)}, u32[]{:S(2)}, u32[]{:S(2)}) collective-permute-start(bf16[16,128]{1,0:T(8,128)(2,1)S(1)} %get-tuple-element.37), channel_id=1, source_target_pairs={{0,1},{1,0},{2,3},{3,2},{4,5},{5,4},{6,7},{7,6},{8,9},{9,8},{10,11... | collective-permute-start | bytes 12296 | tf_op jit(solution)/shard_map/ppermute | solution.py:39
  2.7 0.8 %collective-permute-done = bf16[16,128]{1,0:T(8,128)(2,1)S(1)} collective-permute-done((bf16[16,128]{1,0:T(8,128)(2,1)S(1)}, bf16[16,128]{1,0:T(8,128)(2,1)S(1)}, u32[]{:S(2)}, u32[]{:S(2)}) %collective-permute-start) | collective-permute-done | bytes 4128 | tf_op jit(solution)/shard_map/ppermute | solution.py:39
  3.5 0.3 %collective-permute-start.1 = (bf16[128,1024]{1,0:T(8,128)(2,1)S(1)}, bf16[128,1024]{1,0:T(8,128)(2,1)S(1)}, u32[]{:S(2)}, u32[]{:S(2)}) collective-permute-start(bf16[128,1024]{1,0:T(8,128)(2,1)S(1)} %get-tuple-element.38.kv_ref), channel_id=1, source_target_pairs={{0,1},{1,0},{2,3},{3,2},{4,5},{5,4},{6,7},{7,6},{8,9},{9,8},{10,11... | collective-permute-start | bytes 786440 | tf_op jit(solution)/shard_map/ppermute | solution.py:39
  3.9 0.0 copy-start.2
  3.9 3.6 %collective-permute-start.4 = (bf16[32,128]{1,0:T(8,128)(2,1)S(1)}, bf16[32,128]{1,0:T(8,128)(2,1)S(1)}, u32[]{:S(2)}, u32[]{:S(2)}) collective-permute-start(bf16[32,128]{1,0:T(8,128)(2,1)S(1)} %constant_dynamic-update-slice_fusion.packs_ref), channel_id=1, source_target_pairs={{0,7},{1,6},{2,5},{3,4},{4,3},{5,2},{6,1},{7,0},{8,15},{9,14},{10,... | collective-permute-start | bytes 24584 | tf_op jit(solution)/shard_map/ppermute | solution.py:39
  7.4 0.3 %collective-permute-start.3 = (bf16[32,128]{1,0:T(8,128)(2,1)S(1)}, bf16[32,128]{1,0:T(8,128)(2,1)S(1)}, u32[]{:S(2)}, u32[]{:S(2)}) collective-permute-start(bf16[32,128]{1,0:T(8,128)(2,1)S(1)} %constant_dynamic-update-slice_fusion.packs_ref), channel_id=1, source_target_pairs={{0,5},{1,4},{2,7},{3,6},{4,1},{5,0},{6,3},{7,2},{8,13},{9,12},{10,... | collective-permute-start | bytes 24584 | tf_op jit(solution)/shard_map/ppermute | solution.py:39
  7.7 0.1 collective-permute-start.2
  7.9 0.0 collective-permute-done.1.far_ref
  7.9 0.0 copy-done
  7.9 0.0 copy-done.1
  7.9 0.0 copy-done.2
  7.9 1.1 %pair_scores.1 = (f32[128,2048]{1,0:T(8,128)S(1)}, f32[128,2048]{1,0:T(8,128)S(1)}, f32[8,2048]{1,0:T(8,128)S(1)}, bf16[128,1024]{1,0:T(8,128)(2,1)S(1)}, bf16[2...) custom-call(bf16[1,128,2048]{2,1,0:T(8,128)(2,1)S(1)} %copy-done, ...), custom_call_target="tpu_custom_call" | custom-call | flops 268435456 | bytes 5242880 | tf_op jit(solution)/shard_map/pair_scores/pallas_call | solution.py:359
  9.0 0.0 collective-permute-done.4
  9.0 1.5 %collective-permute-done.3 = bf16[32,128]{1,0:T(8,128)(2,1)S(1)} collective-permute-done((bf16[32,128]{1,0:T(8,128)(2,1)S(1)}, bf16[32,128]{1,0:T(8,128)(2,1)S(1)}, u32[]{:S(2)}, u32[]{:S(2)}) %collective-permute-start.3) | collective-permute-done | bytes 8224 | tf_op jit(solution)/shard_map/ppermute | solution.py:39
  10.5 0.3 %collective-permute-done.2 = bf16[32,128]{1,0:T(8,128)(2,1)S(1)} collective-permute-done((bf16[32,128]{1,0:T(8,128)(2,1)S(1)}, bf16[32,128]{1,0:T(8,128)(2,1)S(1)}, u32[]{:S(2)}, u32[]{:S(2)}) %collective-permute-start.2) | collective-permute-done | bytes 8224 | tf_op jit(solution)/shard_map/ppermute | solution.py:39
  10.8 1.3 %slot_terms.1 = (bf16[32,2,640]{2,1,0:T(2,128)(2,1)}, bf16[144,2048]{1,0:T(8,128)(2,1)S(1)}, bf16[128,2048]{1,0:T(8,128)(2,1)S(1)}, bf16[16,512]{1,0:T(8,128)(2,1)S(1)}) custom-call(bf16[1,128,2048]{2,1,0:T(8,128)(2,1)S(1)} %copy-done, bf16[1,128,2048]{2,1,0:T(8,128)(2,1)S(1)} %copy-done.1, f32[128,2048]{1,0:T(8,128)S(1)} %get-tuple-element.40.weight_ref, ...), custom_call_target="tpu_custom_call" | custom-call | tf_op jit(solution)/shard_map/slot_terms/pallas_call | solution.py:384
  12.1 4.9 %all-to-all-start = ((bf16[32,2,640]{2,1,0:T(2,128)(2,1)}), bf16[32,2,640]{2,1,0:T(2,128)(2,1)S(1)}, u32[]{:S(2)}, u32[]{:S(2)}) async-start(bf16[32,2,640]{2,1,0:T(2,128)(2,1)} %get-tuple-element.56), calls=%async_computation | async-start | bytes 163840 | tf_op jit(solution)/shard_map/all_to_all | solution.py:404
  17.0 1.5 %gradients.1 = (bf16[1,128,2048]{2,1,0:T(8,128)(2,1)}, f32[128,1024]{1,0:T(8,128)S(1)}, bf16[128,512]{1,0:T(8,128)(2,1)S(1)}, bf16[128,512]{1,0:T(8,128)(2,1)S(1)}) custom-call(bf16[1,128,2048]{2,1,0:T(8,128)(2,1)S(1)} %copy-done, bf16[1,128,2048]{2,1,0:T(8,128)(2,1)S(1)} %copy-done.1, bf16[144,2048]{1,0:T(8,128)(2,1)S(1)} %get-tuple-element.44.ds_ref, ...), custom_call_target="tpu_custom_call" | custom-call | flops 402653184 | bytes 5242880 | tf_op jit(solution)/shard_map/gradients/pallas_call | solution.py:405
  18.5 0.3 %collective-permute-start.5 = (bf16[128,512]{1,0:T(8,128)(2,1)S(1)}, bf16[128,512]{1,0:T(8,128)(2,1)S(1)}, u32[]{:S(2)}, u32[]{:S(2)}) collective-permute-start(bf16[128,512]{1,0:T(8,128)(2,1)S(1)} %get-tuple-element.53), channel_id=1, source_target_pairs={{0,1},{1,0},{2,3},{3,2},{4,5},{5,4},{6,7},{7,6},{8,9},{9,8},{10,11... | collective-permute-start | bytes 393224 | tf_op jit(solution)/shard_map/ppermute | solution.py:39
  18.8 0.3 %collective-permute-start.6 = (bf16[128,512]{1,0:T(8,128)(2,1)S(1)}, bf16[128,512]{1,0:T(8,128)(2,1)S(1)}, u32[]{:S(2)}, u32[]{:S(2)}) collective-permute-start(bf16[128,512]{1,0:T(8,128)(2,1)S(1)} %get-tuple-element.54), channel_id=1, source_target_pairs={{0,1},{1,0},{2,3},{3,2},{4,5},{5,4},{6,7},{7,6},{8,9},{9,8},{10,11... | collective-permute-start | bytes 393224 | tf_op jit(solution)/shard_map/ppermute | solution.py:39
  19.1 0.8 %collective-permute-done.5.key_recv_ref = bf16[128,512]{1,0:T(8,128)(2,1)S(1)} collective-permute-done((bf16[128,512]{1,0:T(8,128)(2,1)S(1)}, bf16[128,512]{1,0:T(8,128)(2,1)S(1)}, u32[]{:S(2)}, u32[]{:S(2)}) %collective-permute-start.5) | collective-permute-done | bytes 131104 | tf_op jit(solution)/shard_map/ppermute | solution.py:39
  19.9 0.2 collective-permute-done.6.value_recv_ref
  20.1 0.8 %pair_total.1 = (bf16[1,128,512]{2,1,0:T(8,128)(2,1)}, bf16[1,128,512]{2,1,0:T(8,128)(2,1)}, f32[16,1024]{1,0:T(8,128)S(1)}) custom-call(f32[8,128]{1,0:T(8,128)S(1)} %get-tuple-element.51.meta_ref, f32[128,1024]{1,0:T(8,128)S(1)} %get-tuple-element.52.own_ref, bf16[128,512]{1,0:T(8,128)(2,1)S(1)} %collective-permute-done.5.key_recv_ref, ...), custom_call_target="tpu_custom_call" | custom-call | tf_op jit(solution)/shard_map/pair_total/pallas_call | solution.py:423
  20.9 3.7 %all-to-all-done.terms_ref = bf16[32,2,640]{2,1,0:T(2,128)(2,1)S(1)} async-done(((bf16[32,2,640]{2,1,0:T(2,128)(2,1)}), bf16[32,2,640]{2,1,0:T(2,128)(2,1)S(1)}, u32[]{:S(2)}, u32[]{:S(2)}) %all-to-all-start) | async-done | bytes 81952 | tf_op jit(solution)/shard_map/all_to_all | solution.py:404
  24.6 0.8 %add_up.1 = (bf16[1,128,512]{2,1,0:T(8,128)(2,1)}, bf16[1,128,512]{2,1,0:T(8,128)(2,1)}, f32[1,16]{1,0:T(1,128)}) custom-call(f32[8,128]{1,0:T(8,128)S(1)} %get-tuple-element.51.meta_ref, f32[16,1024]{1,0:T(8,128)S(1)} %get-tuple-element.55.block_ref, bf16[32,2,640]{2,1,0:T(2,128)(2,1)S(1)} %all-to-all-done.terms_ref, ...), custom_call_target="tpu_custom_call", output_to_operand_aliasing={{0}: (3, {}), {1}: (4, {})} | custom-call | tf_op jit(solution)/shard_map/add_up/pallas_call | solution.py:431
  (4 shorter events, 0.0 us)
Async XLA Ops:
  0.6 1.4 %copy-start.4 = (bf16[1,128,512]{2,1,0:T(8,128)(2,1)S(1)}, bf16[1,128,512]{2,1,0:T(8,128)(2,1)}, u32[]{:S(2)}) copy-start(bf16[1,128,512]{2,1,0:T(8,128)(2,1)} %values_ref.1) | copy-start | bytes 393220
  0.6 1.4 %copy-start.3 = (bf16[1,128,512]{2,1,0:T(8,128)(2,1)S(1)}, bf16[1,128,512]{2,1,0:T(8,128)(2,1)}, u32[]{:S(2)}) copy-start(bf16[1,128,512]{2,1,0:T(8,128)(2,1)} %keys_ref.1) | copy-start | bytes 393220
  1.3 0.7 %copy-start.5 = (s32[1,128]{1,0:T(1,128)S(1)}, s32[1,128]{1,0:T(1,128)}, u32[]{:S(2)}) copy-start(s32[1,128]{1,0:T(1,128)} %rank_ref.1) | copy-start | bytes 1540
  2.0 5.8 %copy-start = (bf16[1,128,2048]{2,1,0:T(8,128)(2,1)S(1)}, bf16[1,128,2048]{2,1,0:T(8,128)(2,1)}, u32[]{:S(2)}) copy-start(bf16[1,128,2048]{2,1,0:T(8,128)(2,1)} %query_ref.5) | copy-start | bytes 1572868
  2.1 5.8 %copy-start.1 = (bf16[1,128,2048]{2,1,0:T(8,128)(2,1)S(1)}, bf16[1,128,2048]{2,1,0:T(8,128)(2,1)}, u32[]{:S(2)}) copy-start(bf16[1,128,2048]{2,1,0:T(8,128)(2,1)} %grad_ref.5) | copy-start | bytes 1572868
  2.2 1.3 %collective-permute-start = (bf16[16,128]{1,0:T(8,128)(2,1)S(1)}, bf16[16,128]{1,0:T(8,128)(2,1)S(1)}, u32[]{:S(2)}, u32[]{:S(2)}) collective-permute-start(bf16[16,128]{1,0:T(8,128)(2,1)S(1)} %get-tuple-element.37), channel_id=1, source_target_pairs={{0,1},{1,0},{2,3},{3,2},{4,5},{5,4},{6,7},{7,6},{8,9},{9,8},{10,11... | collective-permute-start | bytes 12296 | tf_op jit(solution)/shard_map/ppermute | solution.py:39
  3.5 4.3 %collective-permute-start.1 = (bf16[128,1024]{1,0:T(8,128)(2,1)S(1)}, bf16[128,1024]{1,0:T(8,128)(2,1)S(1)}, u32[]{:S(2)}, u32[]{:S(2)}) collective-permute-start(bf16[128,1024]{1,0:T(8,128)(2,1)S(1)} %get-tuple-element.38.kv_ref), channel_id=1, source_target_pairs={{0,1},{1,0},{2,3},{3,2},{4,5},{5,4},{6,7},{7,6},{8,9},{9,8},{10,11... | collective-permute-start | bytes 786440 | tf_op jit(solution)/shard_map/ppermute | solution.py:39
  3.9 4.0 %copy-start.2 = (f32[16]{0:T(128)S(1)}, f32[16]{0:T(128)}, u32[]{:S(2)}) copy-start(f32[16]{0:T(128)} %param.15) | copy-start | bytes 196
  3.9 5.1 %collective-permute-start.4 = (bf16[32,128]{1,0:T(8,128)(2,1)S(1)}, bf16[32,128]{1,0:T(8,128)(2,1)S(1)}, u32[]{:S(2)}, u32[]{:S(2)}) collective-permute-start(bf16[32,128]{1,0:T(8,128)(2,1)S(1)} %constant_dynamic-update-slice_fusion.packs_ref), channel_id=1, source_target_pairs={{0,7},{1,6},{2,5},{3,4},{4,3},{5,2},{6,1},{7,0},{8,15},{9,14},{10,... | collective-permute-start | bytes 24584 | tf_op jit(solution)/shard_map/ppermute | solution.py:39
  7.4 3.1 %collective-permute-start.3 = (bf16[32,128]{1,0:T(8,128)(2,1)S(1)}, bf16[32,128]{1,0:T(8,128)(2,1)S(1)}, u32[]{:S(2)}, u32[]{:S(2)}) collective-permute-start(bf16[32,128]{1,0:T(8,128)(2,1)S(1)} %constant_dynamic-update-slice_fusion.packs_ref), channel_id=1, source_target_pairs={{0,5},{1,4},{2,7},{3,6},{4,1},{5,0},{6,3},{7,2},{8,13},{9,12},{10,... | collective-permute-start | bytes 24584 | tf_op jit(solution)/shard_map/ppermute | solution.py:39
  7.7 3.1 %collective-permute-start.2 = (bf16[32,128]{1,0:T(8,128)(2,1)S(1)}, bf16[32,128]{1,0:T(8,128)(2,1)S(1)}, u32[]{:S(2)}, u32[]{:S(2)}) collective-permute-start(bf16[32,128]{1,0:T(8,128)(2,1)S(1)} %constant_dynamic-update-slice_fusion.packs_ref), channel_id=1, source_target_pairs={{0,3},{1,2},{2,1},{3,0},{4,7},{5,6},{6,5},{7,4},{8,11},{9,10},{10,... | collective-permute-start | bytes 24584 | tf_op jit(solution)/shard_map/ppermute | solution.py:39
  12.1 12.5 %all-to-all-start = ((bf16[32,2,640]{2,1,0:T(2,128)(2,1)}), bf16[32,2,640]{2,1,0:T(2,128)(2,1)S(1)}, u32[]{:S(2)}, u32[]{:S(2)}) async-start(bf16[32,2,640]{2,1,0:T(2,128)(2,1)} %get-tuple-element.56), calls=%async_computation | async-start | bytes 163840 | tf_op jit(solution)/shard_map/all_to_all | solution.py:404
  18.5 1.4 %collective-permute-start.5 = (bf16[128,512]{1,0:T(8,128)(2,1)S(1)}, bf16[128,512]{1,0:T(8,128)(2,1)S(1)}, u32[]{:S(2)}, u32[]{:S(2)}) collective-permute-start(bf16[128,512]{1,0:T(8,128)(2,1)S(1)} %get-tuple-element.53), channel_id=1, source_target_pairs={{0,1},{1,0},{2,3},{3,2},{4,5},{5,4},{6,7},{7,6},{8,9},{9,8},{10,11... | collective-permute-start | bytes 393224 | tf_op jit(solution)/shard_map/ppermute | solution.py:39
  18.8 1.3 %collective-permute-start.6 = (bf16[128,512]{1,0:T(8,128)(2,1)S(1)}, bf16[128,512]{1,0:T(8,128)(2,1)S(1)}, u32[]{:S(2)}, u32[]{:S(2)}) collective-permute-start(bf16[128,512]{1,0:T(8,128)(2,1)S(1)} %get-tuple-element.54), channel_id=1, source_target_pairs={{0,1},{1,0},{2,3},{3,2},{4,5},{5,4},{6,7},{7,6},{8,9},{9,8},{10,11... | collective-permute-start | bytes 393224 | tf_op jit(solution)/shard_map/ppermute | solution.py:39
